TPU v7x, 32 devices: a whole 2x2x4 slice. The times are simulated.
32 devices in a mesh: dp: 16 (over z, x, core), tensor: 2 (over y).
Axes of the slice: x: 2, y: 2, z: 4, core: 2. Of those that a mesh axis runs over, the one named last changes fastest.
Arguments:
- block_input: bfloat16 [2, 16, 1024, 768], P(None, 'dp', 'tensor'), may hold values from -6 to 6
- cotangent: bfloat16 [2, 16, 1024, 768], P(None, 'dp', 'tensor'), may hold values from -6 to 6
- lengths: int32 [2, 16], P(None, 'dp'), may hold values from 128 to 1024, as said below
- ln1_gain: float32 [768], replicated, may hold values from 0.5 to 1.5
- ln1_bias: float32 [768], replicated, may hold values from -1.5 to 1.5
- ln2_gain: float32 [768], replicated, may hold values from 0.5 to 1.5
- ln2_bias: float32 [768], replicated, may hold values from -1.5 to 1.5
- w_query: bfloat16 [768, 768], P('dp', 'tensor'), may hold values from -0.21875 to 0.21875
- b_query: float32 [768], P('tensor'), may hold values from -3 to 3
- w_shared: bfloat16 [768, 128], P('dp'), may hold values from -0.21875 to 0.21875
- b_shared: float32 [128], replicated, may hold values from -3 to 3
- w_out: bfloat16 [768, 768], P('tensor', 'dp'), may hold values from -1.75 to 1.75
- b_out: float32 [768], replicated, may hold values from -3 to 3
- w_up: bfloat16 [768, 3072], P('dp', 'tensor'), may hold values from -0.21875 to 0.21875
- b_up: float32 [3072], P('tensor'), may hold values from -3 to 3
- w_down: bfloat16 [3072, 768], P('tensor', 'dp'), may hold values from -0.109375 to 0.109375
- b_down: float32 [768], replicated, may hold values from -3 to 3
Outputs:
- output: bfloat16 [2, 16, 1024, 768], P(None, 'dp', 'tensor')
- grad_input: bfloat16 [2, 16, 1024, 768], P(None, 'dp', 'tensor')
- grad_ln1_gain: float32 [768], replicated
- grad_ln1_bias: float32 [768], replicated
- grad_ln2_gain: float32 [768], replicated
- grad_ln2_bias: float32 [768], replicated
- grad_w_query: float32 [768, 768], P('dp', 'tensor')
- grad_b_query: float32 [768], P('tensor')
- grad_w_shared: float32 [768, 128], P('dp')
- grad_b_shared: float32 [128], replicated
- grad_w_out: float32 [768, 768], P('tensor', 'dp')
- grad_b_out: float32 [768], replicated
- grad_w_up: float32 [768, 3072], P('dp', 'tensor')
- grad_b_up: float32 [3072], P('tensor')
- grad_w_down: float32 [3072, 768], P('tensor', 'dp')
- grad_b_down: float32 [768], replicated
Inputs may be any that keep to these rules, and one draw needn't show every extreme that they name: `lengths`: each entry is the number of real tokens at the start of its padded sequence, the rest padding. For every sequence index s one of its 2 micro-batches has a length over 512, and one sequence of the whole batch has length exactly 1024.
All inputs are finite; a program needn't handle non-finite values.
Results may differ from a plain program's by a relative error of at most 0.011.
Values may be sent and summed in bfloat16 or wider, within the bound.
A program may use at most 192 MiB of HBM per device.

v0:
```python
from functools import partial

import jax
import jax.numpy as jnp
from jax import lax
from jax.sharding import PartitionSpec as P

HEAD_DIM = 64
ROT = 16
MB = 2
QBLK = 512


EPS = 1e-05


def tables(count):
    places = jnp.arange(count).astype(jnp.float32)
    freqs = jnp.power(10000.0, -jnp.arange(ROT // 2).astype(jnp.float32) * 2.0 / ROT)
    angles = places[:, None] * freqs[None, :]
    return (jnp.cos(angles)[:, None, :], jnp.sin(angles)[:, None, :])


def rotate(vector, cosine, sine):
    first = vector[..., : ROT // 2]
    second = vector[..., ROT // 2 : ROT]
    return jnp.concatenate(
        [first * cosine - second * sine, second * cosine + first * sine, vector[..., ROT:]], axis=-1
    )


def unrotate(grad, cosine, sine):
    first = grad[..., : ROT // 2]
    second = grad[..., ROT // 2 : ROT]
    return jnp.concatenate(
        [first * cosine + second * sine, second * cosine - first * sine, grad[..., ROT:]], axis=-1
    )


def normalize(vector):
    centre = vector - jnp.mean(vector, axis=-1, keepdims=True)
    spread = jnp.mean(centre * centre, axis=-1, keepdims=True)
    scale = lax.rsqrt(spread + EPS)
    return (centre * scale, scale)


def norm_back(grad, normed, scale, gain):
    weighted = grad * gain
    return scale * (
        weighted
        - jnp.mean(weighted, axis=-1, keepdims=True)
        - normed * jnp.mean(weighted * normed, axis=-1, keepdims=True)
    )


def block_scores(rows, keys, start, limit, count):
    scores = jnp.einsum("qhd,kd->hqk", rows, keys, preferred_element_type=jnp.float32)
    row_pos = start + jnp.arange(QBLK)
    key_pos = jnp.arange(count)
    allowed = (key_pos[None, :] <= row_pos[:, None]) & (key_pos[None, :] < limit)
    return (scores, allowed[None])


def attend(queries, keys, values, limit):
    count = queries.shape[0]

    def block(start):
        rows = lax.dynamic_slice_in_dim(queries, start, QBLK, 0)
        scores, allowed = block_scores(rows, keys, start, limit, count)
        scores = jnp.where(allowed, scores, jnp.float32(-1e30))
        top = jnp.max(scores, axis=-1, keepdims=True)
        expo = jnp.exp(scores - top)
        total = jnp.sum(expo, axis=-1, keepdims=True)
        weights = (expo / total).astype(jnp.bfloat16)
        result = jnp.einsum("hqk,kd->qhd", weights, values, preferred_element_type=jnp.float32)
        return (result, (top + jnp.log(total))[..., 0])

    starts = jnp.arange(count // QBLK) * QBLK
    results, logsum = lax.map(block, starts)
    return (results.reshape(count, -1, HEAD_DIM), logsum)


def attend_back(queries, keys, values, limit, logsum, grad_out):
    count = queries.shape[0]

    def block(carry, item):
        start, block_logsum = item
        rows = lax.dynamic_slice_in_dim(queries, start, QBLK, 0)
        grads = lax.dynamic_slice_in_dim(grad_out, start, QBLK, 0)
        scores, allowed = block_scores(rows, keys, start, limit, count)
        probs = jnp.where(allowed, jnp.exp(scores - block_logsum[:, :, None]), 0.0)
        weights = probs.astype(jnp.bfloat16)
        dprobs = jnp.einsum("qhd,kd->hqk", grads, values, preferred_element_type=jnp.float32)
        delta = jnp.sum(probs * dprobs, axis=-1, keepdims=True)
        dscores = (probs * (dprobs - delta)).astype(jnp.bfloat16)
        drows = jnp.einsum("hqk,kd->qhd", dscores, keys, preferred_element_type=jnp.float32)
        dkeys = carry[0] + jnp.einsum(
            "hqk,qhd->kd", dscores, rows, preferred_element_type=jnp.float32
        )
        dvalues = carry[1] + jnp.einsum(
            "hqk,qhd->kd", weights, grads, preferred_element_type=jnp.float32
        )
        return ((dkeys, dvalues), drows)

    starts = jnp.arange(count // QBLK) * QBLK
    empty = jnp.zeros((count, HEAD_DIM), jnp.float32)
    (dkeys, dvalues), drows = lax.scan(block, (empty, empty), (starts, logsum))
    return (drows.reshape(count, -1, HEAD_DIM), dkeys, dvalues)


def fetch_each(w_query, w_shared, w_out, w_up, w_down):
    return (
        lax.all_gather(w_query, "dp", axis=0, tiled=True),
        lax.all_gather(w_shared, "dp", axis=0, tiled=True),
        lax.all_gather(w_out, "dp", axis=1, tiled=True),
        lax.all_gather(w_up, "dp", axis=0, tiled=True),
        lax.all_gather(w_down, "dp", axis=1, tiled=True),
    )


def reduce_each(step_grads):
    return (
        lax.psum_scatter(step_grads[0], "dp", scatter_dimension=0, tiled=True),
        lax.psum_scatter(step_grads[1], "dp", scatter_dimension=0, tiled=True),
        lax.psum_scatter(step_grads[2], "dp", scatter_dimension=1, tiled=True),
        lax.psum_scatter(step_grads[3], "dp", scatter_dimension=0, tiled=True),
        lax.psum_scatter(step_grads[4], "dp", scatter_dimension=1, tiled=True),
    )


def per_device(
    block_input,
    cotangent,
    lengths,
    ln1_gain,
    ln1_bias,
    ln2_gain,
    ln2_bias,
    w_query,
    b_query,
    w_shared,
    b_shared,
    w_out,
    b_out,
    w_up,
    b_up,
    w_down,
    b_down,
):
    shard_rows = block_input.shape[2]
    groups = lax.axis_size("tensor")
    rank = lax.axis_index("tensor")
    seq_len = shard_rows * groups
    tail_bias = b_out + b_down
    weight_sums = None
    cos_all, sin_all = tables(seq_len)
    own_pos = rank * shard_rows + jnp.arange(shard_rows)
    outputs = []
    input_grads = []
    sum_bq = jnp.zeros(b_query.shape, jnp.float32)
    sum_bkv = jnp.zeros(b_shared.shape, jnp.float32)
    sum_bup = jnp.zeros(b_up.shape, jnp.float32)
    sum_gain1 = jnp.zeros(ln1_gain.shape, jnp.float32)
    sum_shift1 = jnp.zeros(ln1_gain.shape, jnp.float32)
    sum_gain2 = jnp.zeros(ln1_gain.shape, jnp.float32)
    sum_shift2 = jnp.zeros(ln1_gain.shape, jnp.float32)
    sum_out = jnp.zeros(ln1_gain.shape, jnp.float32)
    for micro in range(MB):
        fetched = fetch_each(w_query, w_shared, w_out, w_up, w_down)
        wq_all, wkv_all, wo_all, wup_all, wdown_all = fetched
        limit = lengths[micro, 0]
        inputs = block_input[micro, 0].astype(jnp.float32)
        normed_one, scale_one = normalize(inputs)
        normed_two, scale_two = normalize(inputs)
        low_one = (normed_one * ln1_gain + ln1_bias).astype(jnp.bfloat16)
        low_two = (normed_two * ln2_gain + ln2_bias).astype(jnp.bfloat16)
        whole_one, whole_two = (
            lax.all_gather(low_one, "tensor", axis=0, tiled=True),
            lax.all_gather(low_two, "tensor", axis=0, tiled=True),
        )
        query_lin = jnp.dot(whole_one, wq_all, preferred_element_type=jnp.float32) + b_query
        query_lin = query_lin.reshape(seq_len, -1, HEAD_DIM)
        queries = (rotate(query_lin, cos_all, sin_all) * 0.125).astype(jnp.bfloat16)
        shared = jnp.dot(whole_one, wkv_all, preferred_element_type=jnp.float32) + b_shared
        keys = rotate(shared[:, None, :HEAD_DIM], cos_all, sin_all)[:, 0].astype(jnp.bfloat16)
        values = shared[:, HEAD_DIM:].astype(jnp.bfloat16)
        attended, logsum = attend(queries, keys, values, limit)
        attended_low = attended.reshape(seq_len, -1).astype(jnp.bfloat16)
        hidden = jnp.dot(whole_two, wup_all, preferred_element_type=jnp.float32) + b_up
        active = jax.nn.gelu(hidden, approximate=False).astype(jnp.bfloat16)
        partial_out = jnp.dot(attended_low, wo_all, preferred_element_type=jnp.float32) + jnp.dot(
            active, wdown_all, preferred_element_type=jnp.float32
        )
        branch = lax.psum_scatter(partial_out, "tensor", scatter_dimension=0, tiled=True)
        outputs.append((inputs + branch + tail_bias).astype(jnp.bfloat16))
        valid = (own_pos < limit).astype(jnp.float32)[:, None]
        upstream = cotangent[micro, 0].astype(jnp.float32) * valid
        whole_up = lax.all_gather(upstream.astype(jnp.bfloat16), "tensor", axis=0, tiled=True)
        sum_out = sum_out + jnp.sum(upstream, axis=0)
        grad_down = jnp.einsum("lf,ld->fd", active, whole_up, preferred_element_type=jnp.float32)
        dactive = jnp.einsum("ld,fd->lf", whole_up, wdown_all, preferred_element_type=jnp.float32)
        gelu_pull = jax.vjp(partial(jax.nn.gelu, approximate=False), hidden)[1]
        dhidden = gelu_pull(dactive)[0].astype(jnp.bfloat16)
        sum_bup = sum_bup + jnp.sum(dhidden.astype(jnp.float32), axis=0)
        grad_up = jnp.einsum("ld,lf->df", whole_two, dhidden, preferred_element_type=jnp.float32)
        dnormed_two = jnp.einsum("lf,df->ld", dhidden, wup_all, preferred_element_type=jnp.float32)
        dattended = jnp.einsum("ld,ed->le", whole_up, wo_all, preferred_element_type=jnp.float32)
        dattended = dattended.astype(jnp.bfloat16).reshape(seq_len, -1, HEAD_DIM)
        grad_out = jnp.einsum(
            "le,ld->ed", attended_low, whole_up, preferred_element_type=jnp.float32
        )
        dqueries, dkeys, dvalues = attend_back(queries, keys, values, limit, logsum, dattended)
        dquery_lin = (
            unrotate(dqueries * 0.125, cos_all, sin_all).reshape(seq_len, -1).astype(jnp.bfloat16)
        )
        dkey_lin = unrotate(dkeys[:, None, :], cos_all, sin_all)[:, 0]
        dshared = lax.psum(jnp.concatenate([dkey_lin, dvalues], axis=1), "tensor")
        dshared = dshared.astype(jnp.bfloat16)
        sum_bq = sum_bq + jnp.sum(dquery_lin.astype(jnp.float32), axis=0)
        sum_bkv = sum_bkv + jnp.sum(dshared.astype(jnp.float32), axis=0)
        grad_q = jnp.einsum("ld,le->de", whole_one, dquery_lin, preferred_element_type=jnp.float32)
        grad_kv = jnp.einsum("ld,lc->dc", whole_one, dshared, preferred_element_type=jnp.float32)
        dnormed_one = jnp.einsum(
            "le,de->ld", dquery_lin, wq_all, preferred_element_type=jnp.float32
        )
        dnormed_one, dnormed_two = (
            lax.psum_scatter(dnormed_one, "tensor", scatter_dimension=0, tiled=True),
            lax.psum_scatter(dnormed_two, "tensor", scatter_dimension=0, tiled=True),
        )
        own_shared = lax.dynamic_slice_in_dim(dshared, rank * shard_rows, shard_rows, 0)
        dnormed_one = dnormed_one + jnp.einsum(
            "lc,dc->ld", own_shared, wkv_all, preferred_element_type=jnp.float32
        )
        sum_gain1 = sum_gain1 + jnp.sum(dnormed_one * normed_one, axis=0)
        sum_shift1 = sum_shift1 + jnp.sum(dnormed_one, axis=0)
        sum_gain2 = sum_gain2 + jnp.sum(dnormed_two * normed_two, axis=0)
        sum_shift2 = sum_shift2 + jnp.sum(dnormed_two, axis=0)
        dinputs = (
            upstream
            + norm_back(dnormed_one, normed_one, scale_one, ln1_gain)
            + norm_back(dnormed_two, normed_two, scale_two, ln2_gain)
        )
        input_grads.append(dinputs.astype(jnp.bfloat16))
        step_grads = (grad_q, grad_kv, grad_out, grad_up, grad_down)
        step_grads = reduce_each(step_grads)
        if weight_sums is None:
            weight_sums = step_grads
        else:
            weight_sums = jax.tree.map(jnp.add, weight_sums, step_grads)
    output = jnp.stack(outputs, axis=0)[:, None]
    grad_input = jnp.stack(input_grads, axis=0)[:, None]
    sum_bq, sum_bkv, sum_bup = lax.psum((sum_bq, sum_bkv, sum_bup), "dp")
    sum_gain1, sum_shift1, sum_gain2, sum_shift2, sum_out = lax.psum(
        (sum_gain1, sum_shift1, sum_gain2, sum_shift2, sum_out), ("dp", "tensor")
    )
    grad_q, grad_kv, grad_o, grad_up, grad_down = weight_sums
    return (
        output,
        grad_input,
        sum_gain1,
        sum_shift1,
        sum_gain2,
        sum_shift2,
        grad_q,
        sum_bq,
        grad_kv,
        sum_bkv,
        grad_o,
        sum_out,
        grad_up,
        sum_bup,
        grad_down,
        sum_out,
    )


def solution(mesh):
    in_specs = (
        P(None, "dp", "tensor", None),
        P(None, "dp", "tensor", None),
        P(None, "dp"),
        P(),
        P(),
        P(),
        P(),
        P("dp", "tensor"),
        P("tensor"),
        P("dp", None),
        P(),
        P("tensor", "dp"),
        P(),
        P("dp", "tensor"),
        P("tensor"),
        P("tensor", "dp"),
        P(),
    )
    out_specs = (
        P(None, "dp", "tensor", None),
        P(None, "dp", "tensor", None),
        P(),
        P(),
        P(),
        P(),
        P("dp", "tensor"),
        P("tensor"),
        P("dp", None),
        P(),
        P("tensor", "dp"),
        P(),
        P("dp", "tensor"),
        P("tensor"),
        P("tensor", "dp"),
        P(),
    )
    return jax.shard_map(
        per_device, mesh=mesh, in_specs=in_specs, out_specs=out_specs, check_vma=False
    )
```

profile of v0, /device:TPU:0, one launch (start us, length us, event | category | flops | bytes accessed | tf_op | source)
XLA Modules:
  0.0 965.6 jit_solution(14386503645061550123)
XLA Ops:
  21.6 24.8 %all_gather.39 = bf16[768,384]{1,0:T(8,128)(2,1)S(1)} all-gather(bf16[48,384]{1,0:T(8,128)(2,1)S(1)} %copy-done.65), channel_id=1, replica_groups=mesh['dp'=16,'tensor'=2] {'dp'}, dimensions={0}, use_global_device_ids=true | all-gather | bytes 626688 | tf_op jit(solution)/shard_map/all_gather | solution.py:113
  46.4 18.0 %all_gather.40 = bf16[768,128]{1,0:T(8,128)(2,1)S(1)} all-gather(bf16[48,128]{1,0:T(8,128)(2,1)S(1)} %copy-done.81), channel_id=1, replica_groups=mesh['dp'=16,'tensor'=2] {'dp'}, dimensions={0}, use_global_device_ids=true | all-gather | bytes 208896 | tf_op jit(solution)/shard_map/all_gather | solution.py:114
  65.3 20.6 %all_gather.41 = bf16[384,768]{0,1:T(8,128)(2,1)S(1)} all-gather(bf16[384,48]{0,1:T(8,128)(2,1)S(1)} %copy-done.66), channel_id=1, replica_groups=mesh['dp'=16,'tensor'=2] {'dp'}, dimensions={1}, use_global_device_ids=true | all-gather | bytes 626688 | tf_op jit(solution)/shard_map/all_gather | solution.py:115
  97.1 30.9 %while.55 = (s32[]{:T(128)}, bf16[2,512,6,64]{1,3,2,0:T(8,128)(2,1)}, f32[2,6,512]{2,1,0:T(8,128)S(1)}, s32[2]{0:T(128)S(1)}, s32[]{:T(128)}, /*index=5*/bf16[10...) while((s32[]{:T(128)}, ...), condition=%wide.region_12.13_spmd, body=%wide.region_9.12_spmd.sunk | while | flops 834664960 | bytes 41405100 | solution.py:79
  107.0 5.6 fusion.331
  122.4 5.6 fusion.331
  132.5 75.6 %while.57 = (s32[]{:T(128)}, f32[1024,64]{0,1:T(8,128)S(1)}, f32[1024,64]{0,1:T(8,128)}, f32[2,512,6,64]{1,3,2,0:T(8,128)}, s32[2]{0:T(128)S(1)}, /*index=5*/s32...) while((s32[]{:T(128)}, f32[1024,64]{0,1:T(8,128)S(1)}, ...), condition=%wide.region_26.27_spmd.clone, body=%wide.region_24.26_spmd.clone.sunk | while | flops 2052323840 | bytes 179014464 | solution.py:107
  139.0 8.3 fusion.357
  147.3 6.7 fusion.358
  159.5 4.1 fusion.359
  163.6 6.6 fusion.360
  176.5 8.3 fusion.357
  184.8 6.9 fusion.358
  197.2 4.1 fusion.359
  201.4 6.7 fusion.360
  212.4 28.0 %while.54 = (s32[]{:T(128)}, bf16[2,512,6,64]{1,3,2,0:T(8,128)(2,1)S(1)}, f32[2,6,512]{2,1,0:T(8,128)S(1)}, s32[2]{0:T(128)S(1)}, s32[]{:T(128)}, /*index=5*/bf1...) while((s32[]{:T(128)}, ...), condition=%wide.region_5.6_spmd, body=%wide.region_2.5_spmd.sunk | while | flops 834664960 | bytes 41412780 | solution.py:79
  222.3 4.1 fusion.327
  236.3 4.1 fusion.327
  245.3 73.1 %while.56 = (s32[]{:T(128)}, f32[1024,64]{0,1:T(8,128)S(1)}, f32[1024,64]{0,1:T(8,128)}, f32[2,512,6,64]{1,3,2,0:T(8,128)}, s32[2]{0:T(128)S(1)}, /*index=5*/s32...) while((s32[]{:T(128)}, f32[1024,64]{0,1:T(8,128)S(1)}, ...), condition=%wide.region_16.17_spmd.clone, body=%wide.region_14.16_spmd.clone.sunk | while | flops 2052323840 | bytes 194742688 | solution.py:107
  252.0 7.2 fusion.342
  259.2 6.8 fusion.343
  270.7 4.7 fusion.344
  275.5 6.6 fusion.345
  288.4 7.3 fusion.342
  295.6 6.8 fusion.343
  307.1 4.7 fusion.344
  311.8 6.7 fusion.345
  330.1 8.1 fusion.210
  338.2 7.5 fusion.212
  345.8 4.4 fusion.217
  352.3 35.4 %convert_reduce_fusion.1 = (f32[1536]{0:T(1024)S(1)}, bf16[1024,1536]{1,0:T(8,128)(2,1)S(1)}, f32[1024,1536]{1,0:T(8,128)}, f32[1536]{0:T(1024)S(1)}, bf16[1024,1536]{1,0:T(8,128)(2,1)}, /*index=5*/f32[1024,1536]{1,0:T(8,128)}) fusion(f32[1024,1536]{1,0:T(8,128)S(1)} %copy-done.24, f32[1536]{0:T(1024)S(1)} %copy-done.82, f32[1024,1536]{1,0:T(8,128)S(1)} %fusion.217, ...), kind=kOutput, calls=%fused_computation.115 | convolution fusion | flops 2651845632 | bytes 41699328 | tf_op jit(solution)/shard_map/ld,fd->lf/dot_general | solution.py:201
  389.4 4.3 fusion.215
  393.8 6.9 fusion.218
  403.1 11.2 %multiply_convert_fusion.1 = (bf16[1024,1536]{1,0:T(8,128)(2,1)}, bf16[1024,1536]{1,0:T(8,128)(2,1)S(1)}) fusion(f32[1024,1536]{1,0:T(8,128)} %get-tuple-element.453, f32[1024,1536]{1,0:T(8,128)} %fusion.210, f32[1536]{0:T(1024)S(1)} %copy-done.82, f32[1024,1536]{1,0:T(8,128)} %get-tuple-element.504, f32[1024,1536]{1,0:T(8,128)} %fusion.212), kind=kLoop, calls=%fused_computation.131 | loop fusion | flops 12582912 | bytes 31463424 | tf_op jit(solution)/shard_map/convert_element_type | solution.py:190
  422.1 4.6 fusion.211
  434.4 46.7 %all-reduce.4 = (bf16[1024,128]{0,1:T(8,128)(2,1)}, bf16[1024,128]{0,1:T(8,128)(2,1)S(1)}) all-reduce(f32[1024,128]{0,1:T(8,128)} %pad_maximum_fusion, f32[1024,128]{0,1:T(8,128)} %pad_maximum_fusion.1), channel_id=1, replica_groups=mesh['dp'=16,'tensor'=2] {'tensor'}, use_global_device_ids=true, to_apply=%region_18.19 | all-reduce | flops 262144 | bytes 1572864 | tf_op jit(solution)/shard_map/psum | solution.py:217
  494.4 5.2 fusion.223
  499.6 4.3 convolution_add_fusion
  505.8 4.2 fusion.222
  510.1 4.6 convolution_add_fusion.1
  515.9 61.4 %all-reduce.1 = (f32[384]{0:T(512)}, f32[128]{0:T(128)}, f32[1536]{0:T(1024)}) all-reduce(f32[384]{0:T(512)S(1)} %add.426, f32[128]{0:T(128)S(1)} %add.428, f32[1536]{0:T(1024)S(1)} %add.432), channel_id=1, replica_groups=mesh['dp'=16,'tensor'=2] {'dp'}, use_global_device_ids=true, to_apply=%region_50.51 | all-reduce | flops 2048 | bytes 16384 | tf_op jit(solution)/shard_map/psum | solution.py:252
  580.4 5.5 fusion.153
  588.1 37.5 %all-reduce = (f32[768]{0:T(1024)}, f32[768]{0:T(1024)}, f32[768]{0:T(1024)}, f32[768]{0:T(1024)}, f32[768]{0:T(1024)S(1)}) all-reduce(f32[768]{0:T(1024)S(1)} %add.420, f32[768]{0:T(1024)S(1)} %add.421, f32[768]{0:T(1024)S(1)} %add.422, f32[768]{0:T(1024)S(1)} %add.423, ...), channel_id=1, replica_groups=mesh['dp'=16,'tensor'=2] {'dp','tensor'}, use_global_device_ids=true, to_apply=%region_36.37 | all-reduce | flops 3840 | bytes 30720 | tf_op jit(solution)/shard_map/psum | solution.py:253
  631.9 44.9 %reduce-scatter.26.cloned.1.call-done = f32[48,128]{1,0:T(8,128)} async-done(((f32[768,128]{1,0:T(8,128)}), f32[48,128]{1,0:T(8,128)}) %reduce-scatter.26.cloned.1.call-update) | async-done | bytes 24592 | tf_op jit(solution)/shard_map/reduce_scatter | solution.py:124
  676.8 61.6 %reduce-scatter.28.cloned.1.call-done = f32[384,48]{0,1:T(8,128)} async-done(((f32[384,768]{0,1:T(8,128)}), f32[384,48]{0,1:T(8,128)}) %reduce-scatter.28.cloned.1.call-update) | async-done | bytes 73744 | tf_op jit(solution)/shard_map/reduce_scatter | solution.py:125
  738.3 61.5 %reduce-scatter.24.cloned.1.call-done = f32[48,384]{1,0:T(8,128)} async-done(((f32[768,384]{1,0:T(8,128)}), f32[48,384]{1,0:T(8,128)}) %reduce-scatter.24.cloned.1.call-update) | async-done | bytes 73744 | tf_op jit(solution)/shard_map/reduce_scatter | solution.py:123
  799.9 79.4 %reduce-scatter.32.cloned.1.call-done = f32[1536,48]{0,1:T(8,128)} async-done(((f32[1536,768]{0,1:T(8,128)}), f32[1536,48]{0,1:T(8,128)}) %reduce-scatter.32.cloned.1.call-update) | async-done | bytes 294928 | tf_op jit(solution)/shard_map/reduce_scatter | solution.py:127
  879.2 79.0 %reduce-scatter.30.cloned.1.call-done = f32[48,1536]{1,0:T(8,128)} async-done(((f32[768,1536]{1,0:T(8,128)}), f32[48,1536]{1,0:T(8,128)}) %reduce-scatter.30.cloned.1.call-update) | async-done | bytes 294928 | tf_op jit(solution)/shard_map/reduce_scatter | solution.py:126
  (427 shorter events, 169.9 us)
Async XLA Ops:
  7.2 78.9 %all-gather.17.cloned.1.call-start = ((), (), s32[]{:S(2)}) async-start(), calls=%async_computation.16 | async-start | bytes 2359296 | tf_op jit(solution)/shard_map/all_gather | solution.py:178
  13.7 75.6 %all-gather.9.cloned.1.call-start = ((), (), s32[]{:S(2)}) async-start(), calls=%async_computation.11 | async-start | bytes 2359296 | tf_op jit(solution)/shard_map/all_gather | solution.py:178
  14.5 113.6 %all-gather.23.cloned.1.call-start = ((), (), s32[]{:S(2)}) async-start(), calls=%async_computation.22 | async-start | bytes 2359296 | tf_op jit(solution)/shard_map/all_gather | solution.py:198
  18.0 28.4 %copy-start.81 = (bf16[48,128]{1,0:T(8,128)(2,1)S(1)}, bf16[48,128]{1,0:T(8,128)(2,1)}, u32[]{:S(2)}) copy-start(bf16[48,128]{1,0:T(8,128)(2,1)} %param.34) | copy-start | bytes 36868
  18.0 47.2 %copy-start.66 = (bf16[384,48]{0,1:T(8,128)(2,1)S(1)}, bf16[384,48]{0,1:T(8,128)(2,1)}, u32[]{:S(2)}) copy-start(bf16[384,48]{0,1:T(8,128)(2,1)} %param.36) | copy-start | bytes 110596
  18.1 222.4 %all-gather.21.cloned.1.call-start = ((), (), s32[]{:S(2)}) async-start(), calls=%async_computation.19 | async-start | bytes 2359296 | tf_op jit(solution)/shard_map/all_gather | solution.py:198
  18.1 68.0 %copy-start.91 = (f32[128]{0:T(128)S(1)}, f32[128]{0:T(128)}, u32[]{:S(2)}) copy-start(f32[128]{0:T(128)} %param.35) | copy-start | bytes 1540
  18.7 311.4 %all-gather.11.cloned.1.call-start = ((), (), s32[]{:S(2)}) async-start(), calls=%async_computation.12 | async-start | bytes 2359296 | tf_op jit(solution)/shard_map/all_gather | solution.py:179
  19.3 310.9 %all-gather.13.cloned.1.call-start = ((), (), s32[]{:S(2)}) async-start(), calls=%async_computation.13 | async-start | bytes 2506752 | tf_op jit(solution)/shard_map/all_gather | solution.py:116
  19.8 318.4 %all-gather.19.cloned.1.call-start = ((), (), s32[]{:S(2)}) async-start(), calls=%async_computation.17 | async-start | bytes 2359296 | tf_op jit(solution)/shard_map/all_gather | solution.py:179
  20.6 325.2 %all-gather.15.cloned.1.call-start = ((), (), s32[]{:S(2)}) async-start(), calls=%async_computation.14 | async-start | bytes 2506752 | tf_op jit(solution)/shard_map/all_gather | solution.py:117
  21.3 556.0 %reduce-scatter.20.cloned.1.call-start = ((), (), s32[]{:S(2)}) async-start(), calls=%async_computation.23 | async-start | bytes 4718592 | tf_op jit(solution)/shard_map/reduce_scatter | solution.py:227
  21.4 67.0 %copy-start.58 = (f32[1024]{0:T(1024)}, f32[1024]{0:T(1024)S(1)}, u32[]{:S(2)}) copy-start(f32[1024]{0:T(1024)S(1)} %iota_convert_fusion) | copy-start | bytes 12292
  21.4 66.9 %copy-start.83 = (f32[8]{0:T(128)}, f32[8]{0:T(128)S(1)}, u32[]{:S(2)}) copy-start(f32[8]{0:T(128)S(1)} %multiply_power_fusion) | copy-start | bytes 100
  21.5 64.5 %copy-start.15 = (bf16[2,512,6,64]{1,3,2,0:T(8,128)(2,1)}, bf16[2,512,6,64]{1,3,2,0:T(8,128)(2,1)S(1)}, u32[]{:S(2)}) copy-start(bf16[2,512,6,64]{1,3,2,0:T(8,128)(2,1)S(1)} %fusion.208) | copy-start | bytes 2359300
  46.4 47.3 %copy-start.26 = (bf16[768,384]{1,0:T(8,128)(2,1)}, bf16[768,384]{1,0:T(8,128)(2,1)S(1)}, u32[]{:S(2)}) copy-start(bf16[768,384]{1,0:T(8,128)(2,1)S(1)} %all_gather.39) | copy-start | bytes 1769476
  64.4 27.0 %copy-start.38 = (bf16[768,128]{1,0:T(8,128)(2,1)}, bf16[768,128]{1,0:T(8,128)(2,1)S(1)}, u32[]{:S(2)}) copy-start(bf16[768,128]{1,0:T(8,128)(2,1)S(1)} %all_gather.40) | copy-start | bytes 589828
  85.8 42.2 %copy-start.28 = (bf16[384,768]{0,1:T(8,128)(2,1)}, bf16[384,768]{0,1:T(8,128)(2,1)S(1)}, u32[]{:S(2)}) copy-start(bf16[384,768]{0,1:T(8,128)(2,1)S(1)} %all_gather.41) | copy-start | bytes 1769476
  86.1 10.0 %copy-start.52 = (f32[1024,8]{0,1:T(8,128)}, f32[1024,8]{0,1:T(8,128)S(1)}, u32[]{:S(2)}) copy-start(f32[1024,8]{0,1:T(8,128)S(1)} %get-tuple-element.507) | copy-start | bytes 98308
  132.5 76.6 %copy-start.59 = (f32[1024]{0:T(1024)S(1)}, f32[1024]{0:T(1024)}, u32[]{:S(2)}) copy-start(f32[1024]{0:T(1024)} %copy-done.58) | copy-start | bytes 12292
  132.5 76.6 %copy-start.84 = (f32[8]{0:T(128)S(1)}, f32[8]{0:T(128)}, u32[]{:S(2)}) copy-start(f32[8]{0:T(128)} %copy-done.83) | copy-start | bytes 100
  132.5 79.9 %copy-start.16 = (bf16[2,512,6,64]{1,3,2,0:T(8,128)(2,1)S(1)}, bf16[2,512,6,64]{1,3,2,0:T(8,128)(2,1)}, u32[]{:S(2)}) copy-start(bf16[2,512,6,64]{1,3,2,0:T(8,128)(2,1)} %copy-done.15) | copy-start | bytes 2359300
  132.5 79.9 %copy-start.34 = (bf16[1024,64]{0,1:T(8,128)(2,1)S(1)}, bf16[1024,64]{0,1:T(8,128)(2,1)}, u32[]{:S(2)}) copy-start(bf16[1024,64]{0,1:T(8,128)(2,1)} %slice.233) | copy-start | bytes 393220
  137.2 10.1 %copy-start = (f32[512,6,1024]{2,0,1:T(8,128)}, f32[512,6,1024]{2,0,1:T(8,128)S(1)}, u32[]{:S(2)}) copy-start(f32[512,6,1024]{2,0,1:T(8,128)S(1)} %fusion.355) | copy-start | bytes 37748740 | tf_op jit(solution)/shard_map/while
  174.7 10.1 %copy-start = (f32[512,6,1024]{2,0,1:T(8,128)}, f32[512,6,1024]{2,0,1:T(8,128)S(1)}, u32[]{:S(2)}) copy-start(f32[512,6,1024]{2,0,1:T(8,128)S(1)} %fusion.355) | copy-start | bytes 37748740 | tf_op jit(solution)/shard_map/while
  212.4 28.0 %copy-start.29 = (bf16[384,768]{0,1:T(8,128)(2,1)S(1)}, bf16[384,768]{0,1:T(8,128)(2,1)}, u32[]{:S(2)}) copy-start(bf16[384,768]{0,1:T(8,128)(2,1)} %copy-done.28) | copy-start | bytes 1769476
  327.1 253.1 %reduce-scatter.16.cloned.1.call-start = ((), (), s32[]{:S(2)}) async-start(), calls=%async_computation.20 | async-start | bytes 4718592 | tf_op jit(solution)/shard_map/reduce_scatter | solution.py:227
  330.0 250.2 %reduce-scatter.18.cloned.1.call-start = ((), (), s32[]{:S(2)}) async-start(), calls=%async_computation.21 | async-start | bytes 4718592 | tf_op jit(solution)/shard_map/reduce_scatter | solution.py:228
  352.3 37.1 %copy-start.95 = (bf16[768,1536]{1,0:T(8,128)(2,1)S(1)}, bf16[768,1536]{1,0:T(8,128)(2,1)}, u32[]{:S(2)}) copy-start(bf16[768,1536]{1,0:T(8,128)(2,1)} %all-gather.13.cloned.1.call-done) | copy-start | bytes 7077892
  393.7 186.6 %reduce-scatter.22.cloned.1.call-start = ((), (), s32[]{:S(2)}) async-start(), calls=%async_computation.24 | async-start | bytes 4718592 | tf_op jit(solution)/shard_map/reduce_scatter | solution.py:228
  400.7 224.9 %reduce-scatter.14.cloned.1.call-start = ((), (), s32[]{:S(2)}) async-start(), calls=%async_computation.18 | async-start | bytes 4718592 | tf_op jit(solution)/shard_map/reduce_scatter | solution.py:194
  403.1 11.3 %copy-start.94 = (bf16[1536,768]{0,1:T(8,128)(2,1)S(1)}, bf16[1536,768]{0,1:T(8,128)(2,1)}, u32[]{:S(2)}) copy-start(bf16[1536,768]{0,1:T(8,128)(2,1)} %all-gather.15.cloned.1.call-done) | copy-start | bytes 7077892
  419.7 205.9 %reduce-scatter.12.cloned.1.call-start = ((), (), s32[]{:S(2)}) async-start(), calls=%async_computation.15 | async-start | bytes 4718592 | tf_op jit(solution)/shard_map/reduce_scatter | solution.py:194
  429.4 247.3 %reduce-scatter.26.cloned.1.call-start = ((), (), s32[]{:S(2)}) async-start(), calls=%async_computation.26 | async-start | bytes 417792 | tf_op jit(solution)/shard_map/reduce_scatter | solution.py:124
  430.4 52.8 %copy-start.7 = (bf16[1024,768]{1,0:T(8,128)(2,1)S(1)}, bf16[1024,768]{1,0:T(8,128)(2,1)}, u32[]{:S(2)}) copy-start(bf16[1024,768]{1,0:T(8,128)(2,1)} %all-gather.17.cloned.1.call-done) | copy-start | bytes 4718596
  484.6 253.7 %reduce-scatter.28.cloned.1.call-start = ((), (), s32[]{:S(2)}) async-start(), calls=%async_computation.27 | async-start | bytes 1253376 | tf_op jit(solution)/shard_map/reduce_scatter | solution.py:125
  489.4 310.5 %reduce-scatter.24.cloned.1.call-start = ((), (), s32[]{:S(2)}) async-start(), calls=%async_computation.25 | async-start | bytes 1253376 | tf_op jit(solution)/shard_map/reduce_scatter | solution.py:123
  494.4 384.9 %reduce-scatter.32.cloned.1.call-start = ((), (), s32[]{:S(2)}) async-start(), calls=%async_computation.29 | async-start | bytes 5013504 | tf_op jit(solution)/shard_map/reduce_scatter | solution.py:127
  504.0 454.3 %reduce-scatter.30.cloned.1.call-start = ((), (), s32[]{:S(2)}) async-start(), calls=%async_computation.28 | async-start | bytes 5013504 | tf_op jit(solution)/shard_map/reduce_scatter | solution.py:126
  514.7 62.6 %copy-start.39 = (bf16[768,128]{1,0:T(8,128)(2,1)S(1)}, bf16[768,128]{1,0:T(8,128)(2,1)}, u32[]{:S(2)}) copy-start(bf16[768,128]{1,0:T(8,128)(2,1)} %copy-done.38) | copy-start | bytes 589828
  514.7 65.6 %copy-start.5 = (bf16[2,1,512,768]{3,2,1,0:T(8,128)(2,1)S(1)}, bf16[2,1,512,768]{3,2,1,0:T(8,128)(2,1)}, u32[]{:S(2)}) copy-start(bf16[2,1,512,768]{3,2,1,0:T(8,128)(2,1)} %param.25) | copy-start | bytes 4718596
  514.7 65.6 %copy-start.62 = (f32[768]{0:T(1024)S(1)}, f32[768]{0:T(1024)}, u32[]{:S(2)}) copy-start(f32[768]{0:T(1024)} %param.30) | copy-start | bytes 9220
  514.7 65.6 %copy-start.64 = (f32[768]{0:T(1024)S(1)}, f32[768]{0:T(1024)}, u32[]{:S(2)}) copy-start(f32[768]{0:T(1024)} %param.28) | copy-start | bytes 9220
  514.8 65.6 %copy-start.68 = (f32[512]{0:T(512)S(1)}, f32[512]{0:T(512)}, u32[]{:S(2)}) copy-start(f32[512]{0:T(512)} %copy-done.67) | copy-start | bytes 6148
  514.8 65.6 %copy-start.70 = (f32[512]{0:T(512)S(1)}, f32[512]{0:T(512)}, u32[]{:S(2)}) copy-start(f32[512]{0:T(512)} %copy-done.69) | copy-start | bytes 6148
  514.8 65.6 %copy-start.74 = (f32[512]{0:T(512)S(1)}, f32[512]{0:T(512)}, u32[]{:S(2)}) copy-start(f32[512]{0:T(512)} %copy-done.73) | copy-start | bytes 6148
  514.8 65.6 %copy-start.78 = (f32[512]{0:T(512)S(1)}, f32[512]{0:T(512)}, u32[]{:S(2)}) copy-start(f32[512]{0:T(512)} %copy-done.77) | copy-start | bytes 6148
  625.6 332.7 %copy-start.90 = (f32[768]{0:T(1024)}, f32[768]{0:T(1024)S(1)}, u32[]{:S(2)}) copy-start(f32[768]{0:T(1024)S(1)} %get-tuple-element.945) | copy-start | bytes 9220
  (80 other events, 306.1 us)
Sparse Core Ops, SparseCore 0:
  13.8 29.9 all-gather.16
  46.0 27.2 all-gather.8
  74.8 27.1 all-gather.22
  103.4 27.2 all-gather.20
  132.1 27.1 all-gather.10
  161.4 42.3 all-gather.12
  205.3 25.9 all-gather.18
  233.6 42.3 all-gather.14
  327.2 40.6 reduce-scatter.19
  370.1 43.3 reduce-scatter.15
  415.7 58.2 reduce-scatter.17
  476.2 49.0 reduce-scatter.21
  527.5 43.3 reduce-scatter.13
  573.1 44.1 reduce-scatter.11
  621.2 55.5 reduce-scatter.25
  681.2 57.0 reduce-scatter.27
  742.8 57.0 reduce-scatter.23
  804.7 74.5 reduce-scatter.31
  883.7 74.5 reduce-scatter.29
where the time goes:
time: 970 us; the launch traced here: 966 us
  waiting for transfers between devices  330 us (34%)
  matrix products  257 us (26%)
  blocking collectives  209 us (22%)
  other arithmetic  96.7 us (10%)
  local copies, waits for them, and re-layouts  38.3 us (4%)
  loops' own time  16.8 us (2%)
  between operations  15.7 us (2%)
    reduce_scatter x1, waiting for transfers between devices, reduce_each(): lax.psum_scatter(step_grads[4], 'dp', scatter_dimension=1, tiled=True)  79.4 us
    reduce_scatter x1, waiting for transfers between devices, reduce_each(): lax.psum_scatter(step_grads[3], 'dp', scatter_dimension=0, tiled=True)  79 us
    reduce_scatter x1, waiting for transfers between devices, reduce_each(): lax.psum_scatter(step_grads[2], 'dp', scatter_dimension=1, tiled=True)  61.6 us
    reduce_scatter x1, waiting for transfers between devices, reduce_each(): lax.psum_scatter(step_grads[0], 'dp', scatter_dimension=0, tiled=True)  61.5 us
    psum x1, blocking collectives, per_device(): sum_bq, sum_bkv, sum_bup = lax.psum((sum_bq, sum_bkv, sum_bup), 'dp')  61.4 us
    psum x1, blocking collectives, per_device(): dshared = lax.psum(jnp.concatenate([dkey_lin, dvalues], axis=1), 'tensor')  46.7 us
    reduce_scatter x1, waiting for transfers between devices, reduce_each(): lax.psum_scatter(step_grads[1], 'dp', scatter_dimension=0, tiled=True)  44.9 us
    dot_general x2, matrix products, per_device(): jnp.einsum('ld,fd->lf', whole_up, wdown_all, preferred_element_type=jnp.f...  39.8 us
  transfers between devices with their start and end apart: 19, of which 5 were waited for; matrix products, arithmetic and copies ran while one was open for 38% of the time, Pallas kernels for 0%

commit v1 on v0

--- a/solution.py
+++ b/solution.py
@@ -2,7 +2,10 @@
 
 import jax
 import jax.numpy as jnp
+import numpy as np
 from jax import lax
+from jax.experimental import pallas as pl
+from jax.experimental.pallas import tpu as pltpu
 from jax.sharding import PartitionSpec as P
 
 HEAD_DIM = 64
@@ -274,6 +277,964 @@
     )
 
 
+MESH = pl.DeviceIdType.MESH
+BF = jnp.bfloat16
+F32 = jnp.float32
+LOG2E = 1.4426950408889634
+LN2 = 0.6931471805599453
+NEG = -1e30
+ZC, XC, CC = 4, 2, 2
+DMA = pltpu.SemaphoreType.DMA
+VMEM = pltpu.VMEM
+MIB = 1 << 20
+
+
+def nn(a, b):
+    return lax.dot_general(a, b, (((1,), (0,)), ((), ())), preferred_element_type=F32)
+
+
+def nt(a, b):
+    return lax.dot_general(a, b, (((1,), (1,)), ((), ())), preferred_element_type=F32)
+
+
+def eye(n):
+    return (
+        lax.broadcasted_iota(jnp.int32, (n, n), 0) == lax.broadcasted_iota(jnp.int32, (n, n), 1)
+    ).astype(BF)
+
+
+def flat(block):
+    return block.reshape(-1, block.shape[-1])
+
+
+class Place:
+    def __init__(self):
+        self.dp = lax.axis_index("dp")
+        self.t = lax.axis_index("tensor")
+        self.core = lax.rem(self.dp, CC)
+        self.x = lax.rem(lax.div(self.dp, CC), XC)
+        self.z = lax.div(self.dp, CC * XC)
+
+    def at(self, z, x, core):
+        return (z * XC + x) * CC + core
+
+    def z_peer(self, d):
+        return {"dp": self.at(lax.rem(self.z + d, ZC), self.x, self.core)}
+
+    def x_peer(self):
+        return {"dp": self.at(self.z, 1 - self.x, self.core)}
+
+    def core_peer(self):
+        return {"dp": self.at(self.z, self.x, 1 - self.core)}
+
+    def y_peer(self):
+        return {"tensor": 1 - self.t}
+
+    def greet(self):
+        bar = pltpu.get_barrier_semaphore()
+        peers = [self.z_peer(d) for d in (1, 2, 3)]
+        peers += [self.x_peer(), self.core_peer(), self.y_peer()]
+        for p in peers:
+            pl.semaphore_signal(bar, inc=1, device_id=p, device_id_type=MESH)
+        return bar, len(peers)
+
+
+def remote(src, dst, ss, rs, peer):
+    return pltpu.make_async_remote_copy(
+        src_ref=src, dst_ref=dst, send_sem=ss, recv_sem=rs, device_id=peer, device_id_type=MESH
+    )
+
+
+def split_cols(width):
+    a = (width // 128 + 1) // 2 * 128
+    return ((0, a), (a, width - a))
+
+
+class Gather:
+    N_SEMS = 12
+
+    def __init__(self, place, pieces, sems):
+        self.p = place
+        self.pieces = pieces
+        self.sems = sems
+
+    def z(self, c, h, d):
+        p = self.p
+        src, out, width = self.pieces[c]
+        o, w = split_cols(width)[h]
+        cols = pl.ds(o, w)
+        return remote(
+            src.at[:, cols],
+            out.at[p.t, p.z, p.x, p.core, :, cols],
+            self.sems.at[c, h, d - 1],
+            self.sems.at[c, h, 3 + d - 1],
+            p.z_peer(d),
+        )
+
+    def second(self, c, h):
+        p = self.p
+        _, out, width = self.pieces[c]
+        o, w = split_cols(width)[h]
+        view = out.at[p.t, :, p.x, p.core, :, pl.ds(o, w)]
+        peer = p.x_peer() if h == 0 else p.y_peer()
+        return remote(view, view, self.sems.at[c, h, 6], self.sems.at[c, h, 7], peer)
+
+    def third(self, c, h):
+        p = self.p
+        _, out, width = self.pieces[c]
+        o, w = split_cols(width)[h]
+        cols = pl.ds(o, w)
+        if h == 0:
+            view, peer = out.at[p.t, :, :, p.core, :, cols], p.y_peer()
+        else:
+            view, peer = out.at[:, :, p.x, p.core, :, cols], p.x_peer()
+        return remote(view, view, self.sems.at[c, h, 8], self.sems.at[c, h, 9], peer)
+
+    def cores(self, c, h):
+        p = self.p
+        _, out, width = self.pieces[c]
+        o, w = split_cols(width)[h]
+        view = out.at[:, :, :, p.core, :, pl.ds(o, w)]
+        return remote(view, view, self.sems.at[c, h, 10], self.sems.at[c, h, 11], p.core_peer())
+
+    def begin(self, c):
+        for h in (0, 1):
+            for d in (1, 2, 3):
+                self.z(c, h, d).start()
+
+    def step(self, i):
+        n = len(self.pieces)
+        for h in (0, 1):
+            if 0 <= i < n:
+                for d in (1, 2, 3):
+                    self.z(i, h, d).wait()
+                self.second(i, h).start()
+            if 0 <= i - 1 < n:
+                self.second(i - 1, h).wait()
+                self.third(i - 1, h).start()
+            if 0 <= i - 2 < n:
+                self.third(i - 2, h).wait()
+                self.cores(i - 2, h).start()
+            if 0 <= i - 3 < n:
+                self.cores(i - 3, h).wait()
+
+    def n_steps(self):
+        return len(self.pieces) + 3
+
+
+def normal_rows(rows):
+    mean = jnp.mean(rows, axis=-1, keepdims=True)
+    centre = rows - mean
+    var = jnp.mean(centre * centre, axis=-1, keepdims=True)
+    scale = lax.rsqrt(var + EPS)
+    return centre * scale, scale
+
+
+def rotate_t(v, cosine, sine):
+    a, b = v[0:8], v[8:16]
+    return jnp.concatenate([a * cosine - b * sine, b * cosine + a * sine, v[16:]], axis=0)
+
+
+def unrotate_t(v, cosine, sine):
+    a, b = v[0:8], v[8:16]
+    return jnp.concatenate([a * cosine + b * sine, b * cosine - a * sine, v[16:]], axis=0)
+
+
+def fill_bias(place, lens_ref, bias_ref, S):
+    t = place.t
+    for m in range(MB):
+        limit = lens_ref[m]
+        key = lax.broadcasted_iota(jnp.int32, (S, S), 0)
+        row = lax.broadcasted_iota(jnp.int32, (S, S), 1)
+        limit_other = jnp.where(t == 1, limit, 0)
+        bias_ref[m, 0:S] = jnp.where(key < limit_other, 0.0, NEG).astype(F32)
+        own = (key <= row) & (key + t * S < limit)
+        bias_ref[m, S : 2 * S] = jnp.where(own, 0.0, NEG).astype(F32)
+
+
+def front_kernel(
+    dims,
+    x_ref,
+    lens_ref,
+    tab_ref,
+    ln_ref,
+    bpack_ref,
+    bsh_ref,
+    wq_ref,
+    wsh_ref,
+    wout_ref,
+    wup_ref,
+    wdown_ref,
+    wa,
+    wb,
+    wf,
+    ball,
+    h1_ref,
+    h2_ref,
+    qt_ref,
+    att_ref,
+    lse_ref,
+    kc_ref,
+    vc_ref,
+    kt_ref,
+    sa,
+    sb,
+    sf,
+    kvt,
+    kvo,
+    vte,
+    bias,
+    bcol,
+    gsem,
+    lsem,
+    ysem,
+):
+    S, HT, NH, NF, T = dims["S"], dims["HT"], dims["NH"], dims["NF"], dims["T"]
+    D = x_ref.shape[1]
+    R = sa.shape[0]
+    p = Place()
+    bar, npeers = p.greet()
+
+    sa[:, 0:HT] = wq_ref[...]
+    sa[:, HT:] = wsh_ref[...]
+    ident = eye(R)
+    sb[...] = nt(ident, wout_ref[...]).astype(BF)
+    for f in range(NF):
+        sf[f, :, 0:256] = wup_ref[:, 256 * f : 256 * f + 256]
+        sf[f, :, 256:512] = nt(ident, wdown_ref[256 * f : 256 * f + 256, :]).astype(BF)
+    ball[p.t] = bpack_ref[...]
+
+    pieces = [(sa, wa, sa.shape[1]), (sb, wb, sb.shape[1])]
+    pieces += [(sf.at[f], wf.at[f], sf.shape[2]) for f in range(NF)]
+    g = Gather(p, pieces, gsem)
+
+    locals_ = [
+        pltpu.make_async_copy(pieces[c][0], pieces[c][1].at[p.t, p.z, p.x, p.core], lsem.at[c])
+        for c in range(len(pieces))
+    ]
+    for cp in locals_:
+        cp.start()
+    pl.semaphore_wait(bar, npeers)
+    bias_copy = remote(ball.at[p.t], ball.at[p.t], ysem.at[0], ysem.at[1], p.y_peer())
+    bias_copy.start()
+    for c in range(len(pieces)):
+        g.begin(c)
+
+    @pl.loop(0, T // 128)
+    def _(i):
+        rows = pl.ds(pl.multiple_of(i * 128, 128), 128)
+        z, _ = normal_rows(x_ref[rows, :].astype(F32))
+        h1_ref[rows, :] = (z * ln_ref[0:1, :] + ln_ref[1:2, :]).astype(BF)
+        h2_ref[rows, :] = (z * ln_ref[2:3, :] + ln_ref[3:4, :]).astype(BF)
+
+    for cp in locals_:
+        cp.wait()
+    g.step(0)
+    fill_bias(p, lens_ref, bias, S)
+    bias_copy.wait()
+    nq = HT // 128
+    for t in range(2):
+        for j in range(nq):
+            row = jnp.broadcast_to(ball[t, j : j + 1, :], (128, 128))
+            bcol[(t * nq + j) * 128 : (t * nq + j + 1) * 128, :] = row.T
+    bcol[2 * HT : 2 * HT + 128, :] = jnp.broadcast_to(bsh_ref[...], (128, 128)).T
+    for i in (1, 2, 3):
+        g.step(i)
+
+    cosine, sine = tab_ref[p.t, 0:8, :], tab_ref[p.t, 8:16, :]
+    wsh_t = nt(eye(128), flat(wa[0, :, :, :, :, HT:])).astype(BF)
+    for m in range(MB):
+        cols = slice(m * S, m * S + S)
+        kv = nt(wsh_t, h1_ref[cols, :]) + bcol[2 * HT : 2 * HT + 128, 0:1]
+        kvt[0:HEAD_DIM, cols] = rotate_t(kv[0:HEAD_DIM], cosine, sine).astype(BF)
+        kvt[HEAD_DIM:, cols] = kv[HEAD_DIM:].astype(BF)
+    kv_copy = remote(kvt, kvo, ysem.at[2], ysem.at[3], p.y_peer())
+    kv_copy.start()
+
+    for t in range(2):
+        wq_t = nt(eye(HT), flat(wa[t, :, :, :, :, 0:HT])).astype(BF)
+        for m in range(MB):
+            cols = slice(m * S, m * S + S)
+            q = nt(wq_t, h1_ref[cols, :])
+            for h in range(HT // HEAD_DIM):
+                base = t * HT + h * HEAD_DIM
+                qh = q[h * HEAD_DIM : (h + 1) * HEAD_DIM] + bcol[base : base + HEAD_DIM, 0:1]
+                qh = rotate_t(qh, cosine, sine) * (0.125 * LOG2E)
+                qt_ref[base : base + HEAD_DIM, cols] = qh.astype(BF)
+
+    id256 = eye(256)
+    kv_copy.wait()
+    for m in range(MB):
+        for half, src in ((0, kvo), (1, kvt)):
+            cols = slice(m * S, m * S + S)
+            keys = slice(half * S, half * S + S)
+            kt_ref[m, :, keys] = src[0:HEAD_DIM, cols]
+            vte[m, 0:HEAD_DIM, keys] = src[HEAD_DIM:, cols]
+        ones = (lax.broadcasted_iota(jnp.int32, (16, 2 * S), 0) == 0).astype(BF)
+        vte[m, HEAD_DIM:, :] = ones
+        for b in range(2 * S // 256):
+            blk = slice(b * 256, b * 256 + 256)
+            kc_ref[m, blk, :] = nt(id256, kt_ref[m, :, blk]).astype(BF)
+            vc_ref[m, blk, :] = nt(id256, vte[m, 0:HEAD_DIM, blk]).astype(BF)
+
+    first = 4
+
+    @pl.loop(0, MB * NH)
+    def _(i):
+        m = lax.div(i, NH)
+        h = lax.rem(i, NH)
+        head = pl.ds(pl.multiple_of(h * HEAD_DIM, HEAD_DIM), HEAD_DIM)
+        for r in range(S // 256):
+            nk = S + 256 * (r + 1)
+            cols = pl.ds(pl.multiple_of(m * S + r * 256, 256), 256)
+            q = qt_ref[head, cols]
+            s = nn(kc_ref[m, 0:nk, :], q) + bias[m, 0:nk, r * 256 : r * 256 + 256]
+            top = jnp.max(s, axis=0, keepdims=True)
+            e = jnp.exp2(s - top).astype(BF)
+            o = nn(vte[m, :, 0:nk], e)
+            total = o[HEAD_DIM : HEAD_DIM + 1]
+            att_ref[head, cols] = (o[0:HEAD_DIM] * (1.0 / total)).astype(BF)
+            lse_ref[i, :, r * 256 : r * 256 + 256] = top + jnp.log2(total)
+        for k in range(first, g.n_steps()):
+            pl.when(i == 3 * (k - first) + 1)(partial(g.step, k))
+
+    for k in range(g.n_steps()):
+        if k >= first and 3 * (k - first) + 1 >= MB * NH:
+            g.step(k)
+
+
+def masked_rows(place_t, lens_ref, dy_ref, rows, start, S):
+    m, off = divmod(start, S)
+    n = rows.stop - rows.start
+    pos = place_t * S + off + lax.broadcasted_iota(jnp.int32, (n, 1), 0)
+    return jnp.where(pos < lens_ref[m], dy_ref[rows, :].astype(F32), 0.0)
+
+
+def gelu_parts(u):
+    dens = jnp.exp(-0.5 * u * u)
+    v = jnp.abs(u) * 0.7071067811865476
+    k = 1.0 / (1.0 + 0.3275911 * v)
+    poly = k * (
+        0.254829592
+        + k * (-0.284496736 + k * (1.421413741 + k * (-1.453152027 + k * 1.061405429)))
+    )
+    tail = 0.5 * poly * dens
+    return jnp.where(u < 0, tail, 1.0 - tail), dens * 0.3989422804014327
+
+
+def ffn_kernel(
+    dims,
+    x_ref,
+    dy_ref,
+    lens_ref,
+    h2_ref,
+    att_ref,
+    wb_ref,
+    wf_ref,
+    ball_ref,
+    bo_ref,
+    out_ref,
+    gb_ref,
+    gf_ref,
+    dh2_ref,
+    bup_ref,
+    acc,
+    dh2,
+    dym,
+    h2t,
+    dyt,
+):
+    S, HT, NF, T = dims["S"], dims["HT"], dims["NF"], dims["T"]
+    D = x_ref.shape[1]
+    f = pl.program_id(0)
+    t_ = lax.axis_index("tensor")
+
+    @pl.when(f == 0)
+    def _():
+        id256 = eye(256)
+        for b in range(T // 256):
+            rows = slice(b * 256, b * 256 + 256)
+            dym[rows, :] = masked_rows(t_, lens_ref, dy_ref, rows, b * 256, S).astype(BF)
+            a = nt(id256, att_ref[:, rows]).astype(BF)
+            acc[rows, :] = (
+                x_ref[rows, :].astype(F32)
+                + bo_ref[...]
+                + nt(a[:, 0:HT], wb_ref[0])
+                + nt(a[:, HT:], wb_ref[1])
+            )
+            for c in range(D // 256):
+                cols = slice(c * 256, c * 256 + 256)
+                dyt[cols, rows] = nt(id256, dym[rows, cols]).astype(BF)
+                h2t[cols, rows] = nt(id256, h2_ref[rows, cols]).astype(BF)
+        for t in range(2):
+            gb_ref[t] = nt(dyt[...], att_ref[t * HT : (t + 1) * HT, :]).astype(BF)
+        dh2[...] = jnp.zeros_like(dh2)
+
+    first = ball_ref.shape[1] - 1 - 2 * NF
+    for t in range(2):
+        wu = wf_ref[0, t, :, 0:256]
+        wd = wf_ref[0, t, :, 256:512]
+        bias = jnp.concatenate(
+            [ball_ref[t, pl.ds(first + 2 * f, 1), :], ball_ref[t, pl.ds(first + 2 * f + 1, 1), :]],
+            axis=1,
+        )
+        u = nn(h2_ref[...], wu) + bias
+        cdf, dens = gelu_parts(u)
+        act = (u * cdf).astype(BF)
+        slope = cdf + u * dens
+        acc[...] += nt(act, wd)
+        gf_ref[0, t, :, 256:512] = nn(dyt[...], act).astype(BF)
+        du = (nn(dym[...], wd) * slope).astype(BF)
+        sums = jnp.sum(du.astype(F32), axis=0, keepdims=True)
+        bup_ref[0, 2 * t : 2 * t + 1, :] = sums[:, 0:128]
+        bup_ref[0, 2 * t + 1 : 2 * t + 2, :] = sums[:, 128:256]
+        gf_ref[0, t, :, 0:256] = nn(h2t[...], du).astype(BF)
+        dh2[...] += nt(du, wu)
+
+    @pl.when(f == NF - 1)
+    def _():
+        out_ref[...] = acc[...].astype(BF)
+        dh2_ref[...] = dh2[...]
+
+
+class Reduce:
+    def __init__(self, place, pieces, own, rc, r2a, r2b, r3, r4, sems):
+        self.p = place
+        self.pieces = pieces
+        self.own, self.rc, self.r2a, self.r2b, self.r3, self.r4 = own, rc, r2a, r2b, r3, r4
+        self.sems = sems
+
+    def cores(self, c):
+        g, _, w, _ = self.pieces[c]
+        return remote(
+            g.at[:, :, :, 1 - self.p.core],
+            self.rc.at[c, :, :, :, :, pl.ds(0, w)],
+            self.sems.at[c, 0],
+            self.sems.at[c, 1],
+            self.p.core_peer(),
+        )
+
+    def local(self, c):
+        g, _, w, _ = self.pieces[c]
+        return pltpu.make_async_copy(
+            g.at[:, :, :, self.p.core], self.own.at[c, :, :, :, :, pl.ds(0, w)], self.sems.at[c, 2]
+        )
+
+    def second(self, c, h):
+        p = self.p
+        o, w = split_cols(self.pieces[c][2])[h]
+        if h == 0:
+            src, dst, peer = self.rc.at[c, 1 - p.t, :, :, :, pl.ds(o, w)], self.r2a, p.y_peer()
+        else:
+            src, dst, peer = self.rc.at[c, :, :, 1 - p.x, :, pl.ds(o, w)], self.r2b, p.x_peer()
+        dst = dst.at[c, :, :, :, pl.ds(0, w)]
+        return remote(src, dst, self.sems.at[c, 3 + 2 * h], self.sems.at[c, 4 + 2 * h], peer)
+
+    def third(self, c, h):
+        p = self.p
+        o, w = split_cols(self.pieces[c][2])[h]
+        if h == 0:
+            src, peer = self.r2a.at[c, :, 1 - p.x, :, pl.ds(0, w)], p.x_peer()
+        else:
+            src, peer = self.r2b.at[c, 1 - p.t, :, :, pl.ds(0, w)], p.y_peer()
+        dst = self.r3.at[c, h, :, :, pl.ds(0, w)]
+        return remote(src, dst, self.sems.at[c, 7 + 2 * h], self.sems.at[c, 8 + 2 * h], peer)
+
+    def last(self, c, h, d):
+        p = self.p
+        o, w = split_cols(self.pieces[c][2])[h]
+        src = self.r3.at[c, h, lax.rem(p.z + d, ZC), :, pl.ds(0, w)]
+        dst = self.r4.at[c, h, d - 1, :, pl.ds(0, w)]
+        k = 11 + (h * 3 + d - 1) * 2
+        return remote(src, dst, self.sems.at[c, k], self.sems.at[c, k + 1], p.z_peer(d))
+
+    N_SEMS = 23
+
+    def begin(self, c):
+        self.cores(c).start()
+        if self.pieces[c][1]:
+            self.local(c).start()
+
+    def step1(self, c):
+        p = self.p
+        g, copied, width, _ = self.pieces[c]
+        self.cores(c).wait()
+        if copied:
+            self.local(c).wait()
+            own = self.own[c, :, :, :, :, 0:width]
+        else:
+            own = g[:, :, :, p.core]
+        mine = self.rc[c, :, :, :, :, 0:width].astype(F32) + own.astype(F32)
+        self.rc[c, :, :, :, :, 0:width] = mine.astype(BF)
+        for h in (0, 1):
+            self.second(c, h).start()
+
+    def step2(self, c):
+        p = self.p
+        for h in (0, 1):
+            self.second(c, h).wait()
+            o, w = split_cols(self.pieces[c][2])[h]
+            if h == 0:
+                ref, mine = self.r2a, self.rc[c, p.t, :, :, :, o : o + w]
+            else:
+                ref, mine = self.r2b, self.rc[c, :, :, p.x, :, o : o + w]
+            mine = mine.astype(F32) + ref[c, :, :, :, 0:w].astype(F32)
+            ref[c, :, :, :, 0:w] = mine.astype(BF)
+            self.third(c, h).start()
+
+    def step3(self, c):
+        p = self.p
+        for h in (0, 1):
+            self.third(c, h).wait()
+            o, w = split_cols(self.pieces[c][2])[h]
+            mine = self.r2a[c, :, p.x, :, 0:w] if h == 0 else self.r2b[c, p.t, :, :, 0:w]
+            mine = mine.astype(F32) + self.r3[c, h, :, :, 0:w].astype(F32)
+            self.r3[c, h, :, :, 0:w] = mine.astype(BF)
+            for d in (1, 2, 3):
+                self.last(c, h, d).start()
+
+    def step4(self, c):
+        p = self.p
+        parts = []
+        for h in (0, 1):
+            o, w = split_cols(self.pieces[c][2])[h]
+            for d in (1, 2, 3):
+                self.last(c, h, d).wait()
+            total = self.r3[c, h, p.z, :, 0:w].astype(F32)
+            for d in range(3):
+                total = total + self.r4[c, h, d, :, 0:w].astype(F32)
+            parts.append(total)
+        self.pieces[c][3](parts)
+
+    def step(self, i, lo, hi):
+        for k, act in enumerate((self.step4, self.step3, self.step2, self.step1)):
+            c = lo + i - (3 - k)
+            if lo <= c < hi:
+                act(c)
+
+
+def back_kernel(
+    dims,
+    x_ref,
+    dy_ref,
+    lens_ref,
+    tab_ref,
+    ln_ref,
+    h1_ref,
+    qt_ref,
+    att_ref,
+    lse_ref,
+    kc_ref,
+    vc_ref,
+    kt_ref,
+    wa_ref,
+    wb_ref,
+    dh2_ref,
+    bup_ref,
+    gb_in,
+    gf_in,
+    gx_ref,
+    gq_ref,
+    gkv_ref,
+    go_ref,
+    gup_ref,
+    gdn_ref,
+    sm,
+    bias,
+    da_ref,
+    dq_ref,
+    dkv,
+    dkvr,
+    dkvt,
+    h1t,
+    ga,
+    sums,
+    smr,
+    own,
+    rc,
+    r2a,
+    r2b,
+    r3,
+    r4,
+    rsem,
+    ysem,
+):
+    S, HT, NH, NF, T = dims["S"], dims["HT"], dims["NH"], dims["NF"], dims["T"]
+    D = x_ref.shape[1]
+    p = Place()
+    bar, npeers = p.greet()
+
+    def put_ffn(f):
+        def put(parts):
+            gup_ref[:, f * 256 : f * 256 + 256] = parts[0]
+            gdn_ref[:, f * 256 : f * 256 + 256] = parts[1]
+
+        return put
+
+    def put_out(parts):
+        a = parts[0].shape[1]
+        go_ref[:, 0:a] = parts[0]
+        go_ref[:, a:] = parts[1]
+
+    def put_a(parts):
+        a = parts[0].shape[1]
+        gq_ref[:, 0:a] = parts[0]
+        gq_ref[:, a:HT] = parts[1][:, 0 : HT - a]
+        gkv_ref[...] = parts[1][:, HT - a :]
+
+    pieces = [(gf_in.at[f], True, 512, put_ffn(f)) for f in range(NF)]
+    pieces += [(gb_in, True, HT, put_out), (ga, False, HT + 128, put_a)]
+    red = Reduce(p, pieces, own, rc, r2a, r2b, r3, r4, rsem)
+
+    id256 = eye(256)
+    fill_bias(p, lens_ref, bias, S)
+    pl.semaphore_wait(bar, npeers)
+    for c in range(NF + 1):
+        red.begin(c)
+
+    for t in range(2):
+        wo = nt(eye(HT), wb_ref[t]).astype(BF)
+        for b in range(T // 256):
+            rows = slice(b * 256, b * 256 + 256)
+            dyb = masked_rows(p.t, lens_ref, dy_ref, rows, b * 256, S).astype(BF)
+            da_ref[t * HT : (t + 1) * HT, rows] = nt(wo, dyb).astype(BF)
+    for b in range(T // 256):
+        rows = slice(b * 256, b * 256 + 256)
+        for c in range(D // 256):
+            cols = slice(c * 256, c * 256 + 256)
+            h1t[cols, rows] = nt(id256, h1_ref[rows, cols]).astype(BF)
+    dkv[...] = jnp.zeros_like(dkv)
+
+    n_first = NF + 1
+
+    @pl.loop(0, MB * NH)
+    def _(i):
+        m = lax.div(i, NH)
+        h = lax.rem(i, NH)
+        head = pl.ds(pl.multiple_of(h * HEAD_DIM, HEAD_DIM), HEAD_DIM)
+        for r in range(S // 256):
+            nk = S + 256 * (r + 1)
+            cols = pl.ds(pl.multiple_of(m * S + r * 256, 256), 256)
+            cosine = tab_ref[p.t, 0:8, r * 256 : r * 256 + 256]
+            sine = tab_ref[p.t, 8:16, r * 256 : r * 256 + 256]
+            q = qt_ref[head, cols]
+            da = da_ref[head, cols]
+            delta = jnp.sum(
+                da.astype(F32) * att_ref[head, cols].astype(F32), axis=0, keepdims=True
+            )
+            lse = lse_ref[i, :, r * 256 : r * 256 + 256]
+            zero = jnp.zeros_like(q)
+            both = jnp.concatenate(
+                [jnp.concatenate([q, zero], axis=1), jnp.concatenate([zero, da], axis=1)], axis=0
+            )
+            dq = jnp.zeros((HEAD_DIM, 256), F32)
+            for b in range(nk // 256):
+                keys = slice(b * 256, b * 256 + 256)
+                s = nn(kc_ref[m, keys, :], q) + bias[m, keys, r * 256 : r * 256 + 256]
+                pr = jnp.exp2(s - lse)
+                dp = nn(vc_ref[m, keys, :], da)
+                ds = (pr * (dp - delta)).astype(BF)
+                dq = dq + nn(kt_ref[m, :, keys], ds)
+                dkv[m, keys, :] += nt(jnp.concatenate([ds, pr.astype(BF)], axis=1), both)
+            dq_ref[head, cols] = (unrotate_t(dq, cosine, sine) * 0.125).astype(BF)
+        for k in range(n_first + 3):
+            pl.when(i == 2 * k + 1)(partial(red.step, k, 0, n_first))
+
+    kv_copy = remote(dkv.at[:, 0:S, :], dkvr, ysem.at[0], ysem.at[1], p.y_peer())
+    kv_copy.start()
+    for t in range(2):
+        gq = nt(h1t[...], dq_ref[t * HT : (t + 1) * HT, :]).astype(BF)
+        ga[t, :, :, :, :, 0:HT] = gq.reshape(ZC, XC, CC, -1, HT)
+    kv_copy.wait()
+    cosine, sine = tab_ref[p.t, 0:8, :], tab_ref[p.t, 8:16, :]
+    for m in range(MB):
+        mine = (dkv[m, S : 2 * S, :] + dkvr[m]).T
+        cols = slice(m * S, m * S + S)
+        dkvt[0:HEAD_DIM, cols] = (unrotate_t(mine[0:HEAD_DIM], cosine, sine) * LN2).astype(BF)
+        dkvt[HEAD_DIM:, cols] = mine[HEAD_DIM:].astype(BF)
+    gkv = nt(h1t[...], dkvt[...]).astype(BF).reshape(ZC, XC, CC, -1, 128)
+    for t in range(2):
+        ga[t, :, :, :, :, HT:] = gkv
+    red.begin(n_first)
+
+    sums[...] = jnp.zeros_like(sums)
+    wq = [flat(wa_ref[t, :, :, :, :, 0:HT]) for t in range(2)]
+    wsh = flat(wa_ref[0, :, :, :, :, HT:])
+    for b in range(T // 256):
+        rows = slice(b * 256, b * 256 + 256)
+        dq = nt(id256, dq_ref[:, rows])
+        dkvn = nt(id256, dkvt[:, rows])
+        dql = dq.astype(BF)
+        dh1 = nt(dql[:, 0:HT], wq[0]) + nt(dql[:, HT:], wq[1]) + nt(dkvn.astype(BF), wsh)
+        dh2 = dh2_ref[rows, :]
+        z, scale = normal_rows(x_ref[rows, :].astype(F32))
+        dy = masked_rows(p.t, lens_ref, dy_ref, rows, b * 256, S)
+        e = dh1 * ln_ref[0:1, :] + dh2 * ln_ref[2:3, :]
+        back = scale * (
+            e - jnp.mean(e, axis=-1, keepdims=True) - z * jnp.mean(e * z, axis=-1, keepdims=True)
+        )
+        gx_ref[rows, :] = (dy + back).astype(BF)
+        for k, v in enumerate((dh1 * z, dh1, dh2 * z, dh2, dy, dq)):
+            sums[k : k + 1, :] += jnp.sum(v, axis=0, keepdims=True)
+        sums[6:7, 0:128] += jnp.sum(dkvn, axis=0, keepdims=True)
+        if b < 2:
+            red.step(b, n_first, n_first + 1)
+    n = D // 128
+    for k in range(6):
+        for j in range(n):
+            sm[k * n + j : k * n + j + 1, :] = sums[k : k + 1, j * 128 : j * 128 + 128]
+    sm[6 * n : 6 * n + 4, :] = jnp.zeros((4, 128), F32)
+    sm[6 * n : 6 * n + 1, :] = sums[6:7, 0:128]
+    for f in range(NF):
+        sm[6 * n + 4 + 4 * f : 6 * n + 8 + 4 * f, :] = bup_ref[f]
+
+    for k, peer in enumerate((p.core_peer(), p.y_peer(), p.x_peer())):
+        cp = remote(sm, smr.at[k], ysem.at[2 + 2 * k], ysem.at[3 + 2 * k], peer)
+        cp.start()
+        if k < 2:
+            red.step(k + 2, n_first, n_first + 1)
+        cp.wait()
+        sm[...] += smr[k]
+    cps = [remote(sm, smr.at[2 + d], ysem.at[6 + 2 * d], ysem.at[7 + 2 * d], p.z_peer(d)) for d in (1, 2, 3)]
+    for cp in cps:
+        cp.start()
+    for cp in cps:
+        cp.wait()
+    sm[...] += smr[3] + smr[4] + smr[5]
+
+
+def angle_table(S):
+    places = np.arange(2 * S, dtype=np.float64)
+    freqs = 10000.0 ** (-np.arange(ROT // 2) * 2.0 / ROT)
+    angles = (places[:, None] * freqs[None, :]).astype(np.float32).astype(np.float64)
+    tab = np.concatenate([np.cos(angles).T, np.sin(angles).T], axis=0).astype(np.float32)
+    return tab.reshape(ROT, 2, S).transpose(1, 0, 2)
+
+
+def params(limit, collective_id=None):
+    if collective_id is None:
+        return pltpu.CompilerParams(vmem_limit_bytes=limit * MIB)
+    return pltpu.CompilerParams(
+        vmem_limit_bytes=limit * MIB, collective_id=collective_id, has_side_effects=True
+    )
+
+
+def token_plan(
+    block_input,
+    cotangent,
+    lengths,
+    ln1_gain,
+    ln1_bias,
+    ln2_gain,
+    ln2_bias,
+    w_query,
+    b_query,
+    w_shared,
+    b_shared,
+    w_out,
+    b_out,
+    w_up,
+    b_up,
+    w_down,
+    b_down,
+):
+    S, D = block_input.shape[2:]
+    R, HT = w_query.shape
+    FT = w_up.shape[1]
+    NF, T, NH = FT // 256, MB * S, 2 * HT // HEAD_DIM
+    dims = dict(S=S, HT=HT, NF=NF, T=T, NH=NH)
+    full = (2, ZC, XC, CC, R)
+    t = lax.axis_index("tensor")
+
+    def s(shape, dtype):
+        return jax.ShapeDtypeStruct(shape, dtype)
+
+    vm = pl.BlockSpec(memory_space=VMEM)
+    hbm = pl.BlockSpec(memory_space=pl.ANY)
+    smem = pl.BlockSpec(memory_space=pltpu.SMEM)
+
+    x = block_input.reshape(T, D)
+    dy = cotangent.reshape(T, D)
+    lens = lengths.reshape(MB)
+    tab = jnp.asarray(angle_table(S))
+    ln = jnp.stack([ln1_gain, ln1_bias, ln2_gain, ln2_bias])
+    bpack = jnp.concatenate([b_query, b_up, jnp.zeros((128,), F32)]).reshape(-1, 128)
+    nb = bpack.shape[0]
+    np_ = NF + 2
+
+    outs = pl.pallas_call(
+        partial(front_kernel, dims),
+        out_shape=[
+            s(full + (HT + 128,), BF),
+            s(full + (HT,), BF),
+            s((NF,) + full + (512,), BF),
+            s((2, nb, 128), F32),
+            s((T, D), BF),
+            s((T, D), BF),
+            s((D, T), BF),
+            s((D, T), BF),
+            s((MB * NH, 1, S), F32),
+            s((MB, 2 * S, HEAD_DIM), BF),
+            s((MB, 2 * S, HEAD_DIM), BF),
+            s((MB, HEAD_DIM, 2 * S), BF),
+        ],
+        in_specs=[vm, smem] + [vm] * 9,
+        out_specs=[vm, hbm, hbm] + [vm] * 9,
+        scratch_shapes=[
+            VMEM((R, HT + 128), BF),
+            VMEM((R, HT), BF),
+            VMEM((NF, R, 512), BF),
+            VMEM((128, T), BF),
+            VMEM((128, T), BF),
+            VMEM((MB, HEAD_DIM + 16, 2 * S), BF),
+            VMEM((MB, 2 * S, S), F32),
+            VMEM((2 * HT + 128, 128), F32),
+            DMA((np_, 2, Gather.N_SEMS)),
+            DMA((np_,)),
+            DMA((4,)),
+        ],
+        compiler_params=params(56, 0),
+        name="front",
+    )(x, lens, tab, ln, bpack, b_shared.reshape(1, 128), w_query, w_shared, w_out, w_up, w_down)
+    wa, wb, wf, ball, h1, h2, qt, att, lse, kc, vc, kt = outs
+
+    def whole(shape):
+        return pl.BlockSpec(shape, lambda f: (0,) * len(shape))
+
+    out, gb, gf, dh2, bup = pl.pallas_call(
+        partial(ffn_kernel, dims),
+        grid=(NF,),
+        out_shape=[
+            s((T, D), BF),
+            s((2, D, HT), BF),
+            s((NF, 2, D, 512), BF),
+            s((T, D), F32),
+            s((NF, 4, 128), F32),
+        ],
+        in_specs=[
+            whole((T, D)),
+            whole((T, D)),
+            smem,
+            whole((T, D)),
+            whole((D, T)),
+            whole((2, D, HT)),
+            pl.BlockSpec((1, 2, D, 512), lambda f: (f, 0, 0, 0)),
+            whole((2, nb, 128)),
+            whole((1, D)),
+        ],
+        out_specs=[
+            whole((T, D)),
+            whole((2, D, HT)),
+            pl.BlockSpec((1, 2, D, 512), lambda f: (f, 0, 0, 0)),
+            whole((T, D)),
+            pl.BlockSpec((1, 4, 128), lambda f: (f, 0, 0)),
+        ],
+        scratch_shapes=[
+            VMEM((T, D), F32),
+            VMEM((T, D), F32),
+            VMEM((T, D), BF),
+            VMEM((D, T), BF),
+            VMEM((D, T), BF),
+        ],
+        compiler_params=params(60),
+        name="ffn",
+    )(
+        x,
+        dy,
+        lens,
+        h2,
+        att,
+        wb.reshape(2, D, HT),
+        wf.reshape(NF, 2, D, 512),
+        ball,
+        (b_out + b_down).reshape(1, D),
+    )
+
+    outs = pl.pallas_call(
+        partial(back_kernel, dims),
+        out_shape=[
+            s((T, D), BF),
+            s((R, HT), F32),
+            s((R, 128), F32),
+            s((R, HT), F32),
+            s((R, FT), F32),
+            s((R, FT), F32),
+            s((6 * (D // 128) + 4 + 4 * NF, 128), F32),
+        ],
+        in_specs=[vm, vm, smem] + [vm] * 13 + [hbm, hbm],
+        out_specs=[vm] * 7,
+        scratch_shapes=[
+            VMEM((MB, 2 * S, S), F32),
+            VMEM((D, T), BF),
+            VMEM((D, T), BF),
+            VMEM((MB, 2 * S, 128), F32),
+            VMEM((MB, S, 128), F32),
+            VMEM((128, T), BF),
+            VMEM((D, T), BF),
+            VMEM(full + (HT + 128,), BF),
+            VMEM((8, D), F32),
+            VMEM((6, 6 * (D // 128) + 4 + 4 * NF, 128), F32),
+            VMEM((NF + 1, 2, ZC, XC, R, 512), BF),
+            VMEM((np_, 2, ZC, XC, R, 512), BF),
+            VMEM((np_, ZC, XC, R, 256), BF),
+            VMEM((np_, 2, ZC, R, 256), BF),
+            VMEM((np_, 2, ZC, R, 256), BF),
+            VMEM((np_, 2, 3, R, 256), BF),
+            DMA((np_, Reduce.N_SEMS)),
+            DMA((14,)),
+        ],
+        compiler_params=params(62, 1),
+        name="back",
+    )(
+        x,
+        dy,
+        lens,
+        tab,
+        ln,
+        h1,
+        qt,
+        att,
+        lse,
+        kc,
+        vc,
+        kt,
+        wa,
+        wb.reshape(2, D, HT),
+        dh2,
+        bup,
+        gb.reshape(full + (HT,)),
+        gf.reshape((NF,) + full + (512,)),
+    )
+    gx, gq, gkv, go, gup, gdn, sm = outs
+    n = D // 128
+    five = sm[0 : 5 * n].reshape(5, D)
+    bq = lax.dynamic_index_in_dim(sm[5 * n : 6 * n].reshape(2, HT), t, 0, False)
+    bkv = sm[6 * n]
+    bup = lax.dynamic_index_in_dim(sm[6 * n + 4 :].reshape(NF, 2, 256), t, 1, False).reshape(FT)
+    return (
+        out.reshape(block_input.shape),
+        gx.reshape(block_input.shape),
+        five[0],
+        five[1],
+        five[2],
+        five[3],
+        gq,
+        bq,
+        gkv,
+        bkv,
+        go.T,
+        five[4],
+        gup,
+        bup,
+        gdn.T,
+        five[4],
+    )
+
+
+def fits_token_plan(mesh):
+    return dict(mesh.shape) == {"dp": ZC * XC * CC, "tensor": 2}
+
+
 def solution(mesh):
     in_specs = (
         P(None, "dp", "tensor", None),
@@ -312,6 +1273,7 @@
         P("tensor", "dp"),
         P(),
     )
+    step = token_plan if fits_token_plan(mesh) else per_device
     return jax.shard_map(
-        per_device, mesh=mesh, in_specs=in_specs, out_specs=out_specs, check_vma=False
-    )
+        step, mesh=mesh, in_specs=in_specs, out_specs=out_specs, check_vma=False
+    )

time: 970 us -> 291 us (0.30)
  waiting for transfers between devices: 330 us -> 0 us
  Pallas kernels: 0 us -> 270 us
  matrix products: 257 us -> 0 us
  blocking collectives: 209 us -> 0 us
  other arithmetic: 96.7 us -> 1.92 us
  local copies, waits for them, and re-layouts: 38.3 us -> 17.9 us
  loops' own time: 16.8 us -> 0 us
  between operations: 15.7 us -> 0.74 us
    reduce_scatter x11 -> x0, waiting for transfers between devices: 326 us -> none  [the longest x1 79.4 us: reduce_each(): lax.psum_scatter(step_grads[4], 'dp', scatter_dimension=1, tiled=True)]
    pallas_call x0 -> x3, Pallas kernels: none -> 270 us  [the longest x1 120 us: token_plan(): pl.pallas_call(partial(back_kernel, dims), out_shape=[s((T, D), BF), s((R...]
    dot_general x58 -> x0, matrix products: 257 us -> none  [the longest x2 39.8 us: per_device(): jnp.einsum('ld,fd->lf', whole_up, wdown_all, preferred_element_type=jnp.f...]
    psum x3 -> x0, blocking collectives: 145 us -> none  [the longest x1 61.4 us: per_device(): sum_bq, sum_bkv, sum_bup = lax.psum((sum_bq, sum_bkv, sum_bup), 'dp')]
    all_gather x3 -> x0, blocking collectives: 63.4 us -> none  [the longest x1 24.8 us: fetch_each(): lax.all_gather(w_query, 'dp', axis=0, tiled=True)]
    convert_element_type x14 -> x0, other arithmetic: 45.5 us -> none  [the longest x4 27.2 us: block(): dscores = (probs * (dprobs - delta)).astype(jnp.bfloat16)]
    reduce_sum x9 -> x0, other arithmetic: 20.4 us -> none  [the longest x4 13.5 us: block(): total = jnp.sum(expo, axis=-1, keepdims=True)]
    another operation x4 -> x0, loops' own time: 16.8 us -> none  [the longest x2 8.79 us: attend_back(): (dkeys, dvalues), drows = lax.scan(block, (empty, empty), (starts, logsum))]
  transfers between devices with their start and end apart: 19 -> 0, of which waited for: 5 -> 0; matrix products, arithmetic and copies ran while one was open for 38% -> 0% of each run, Pallas kernels for 0% -> 0%
where the time goes in v1:
time: 291 us; the launch traced here: 290 us
  Pallas kernels  270 us (93%)
  local copies, waits for them, and re-layouts  17.9 us (6%)
    pallas_call x1, Pallas kernels, token_plan(): pl.pallas_call(partial(back_kernel, dims), out_shape=[s((T, D), BF), s((R...  120 us
    pallas_call x1, Pallas kernels, token_plan(): pl.pallas_call(partial(front_kernel, dims), out_shape=[s(full + (HT + 128...  92 us
    pallas_call x1, Pallas kernels, token_plan(): pl.pallas_call(partial(ffn_kernel, dims), grid=(NF,), out_shape=[s((T, D)...  57.7 us
    unnamed x25, local copies, waits for them, and re-layouts  9.99 us

profile of v1, /device:TPU:0, one launch (start us, length us, event | category | flops | bytes accessed | tf_op | source)
XLA Modules:
  0.0 290.4 jit_solution(17139525883591466216)
XLA Ops:
  0.6 0.0 copy-start.6
  0.7 0.0 copy-start.7
  0.7 0.7 stack.15
  1.4 0.7 stack.16
  2.1 0.7 stack.17
  2.7 0.7 stack.18
  3.4 0.6 pad_maximum_fusion.ln_ref
  4.1 1.8 copy.35.wdown_ref
  5.9 1.5 copy.34.wout_ref
  7.4 1.3 maximum_bitcast_fusion.bpack_ref
  8.7 92.0 %front.1 = (bf16[2,4,2,2,48,512]{5,4,3,2,1,0:T(8,128)(2,1)}, bf16[2,4,2,2,48,384]{5,4,3,2,1,0:T(8,128)(2,1)}, bf16[6,2,4,2,2,48,512]{6,5,4,3,2,1,0:T(8,128)(2,1)...) custom-call(bf16[1024,768]{1,0:T(8,128)(2,1)} %bitcast.30, ...), custom_call_target="tpu_custom_call" | custom-call | tf_op jit(solution)/shard_map/front/pallas_call | solution.py:1065
  100.7 0.0 copy-done.6
  100.7 0.0 copy-done.7
  100.7 0.6 reshape.97.bo_ref
  101.3 57.7 %ffn.1 = (bf16[1024,768]{1,0:T(8,128)(2,1)}, bf16[2,768,384]{2,1,0:T(8,128)(2,1)}, bf16[6,2,768,512]{3,2,1,0:T(8,128)(2,1)}, f32[1024,768]{1,0:T(8,128)}, f32[6,4,128]{2,1,0:T(4,128)}) custom-call(bf16[1024,768]{1,0:T(8,128)(2,1)} %bitcast.31, bf16[1024,768]{1,0:T(8,128)(2,1)} %bitcast.35, s32[2]{0:T(128)} %bitcast.44, ...), custom_call_target="tpu_custom_call" | custom-call | tf_op jit(solution)/shard_map/ffn/pallas_call | solution.py:1104
  159.0 120.2 %back.1 = (bf16[1024,768]{1,0:T(8,128)(2,1)}, f32[48,384]{1,0:T(8,128)}, f32[48,128]{1,0:T(8,128)}, f32[48,384]{1,0:T(8,128)}, f32[48,1536]{1,0:T(8,128)}, /*index=5*/f32[48,1536]{1,0:T(8,128)}, f32[64,128]{1,0:T(8,128)}) custom-call(bf16[1024,768]{1,0:T(8,128)(2,1)} %bitcast.32, bf16[1024,768]{1,0:T(8,128)(2,1)} %bitcast.36, s32[2]{0:T(128)} %bitcast.45, ...), custom_call_target="tpu_custom_call" | custom-call | tf_op jit(solution)/shard_map/back/pallas_call | solution.py:1153
  279.2 0.7 slice.43
  280.0 0.6 reshape.104
  280.6 1.4 slice_bitcast_fusion
  281.9 0.0 copy-start.5
  282.0 0.6 dynamic-slice_reduce_fusion.1
  282.6 1.2 slice_bitcast_fusion.5
  283.7 0.6 copy.45
  284.3 0.0 copy-start.3
  284.3 0.0 copy-start.4
  284.3 0.0 copy-start.2
  284.3 0.0 copy-start.1
  284.4 0.0 copy-start
  284.4 2.7 copy.46
  287.1 0.0 copy-done.5
  287.1 0.0 copy-done.3
  287.1 0.6 copy.47
  287.7 0.0 copy-done.4
  287.7 0.6 copy.48
  288.3 0.0 copy-done.2
  288.3 0.6 copy.49
  289.0 0.0 copy-done.1
  289.0 0.7 copy.50
  289.7 0.0 copy-done
  289.7 0.7 copy.51
  (5 shorter events, 0.1 us)
Async XLA Ops:
  0.6 100.1 %copy-start.6 = (f32[768]{0:T(1024)S(1)}, f32[768]{0:T(1024)}, u32[]{:S(2)}) copy-start(f32[768]{0:T(1024)} %param.30) | copy-start | bytes 9220
  0.7 100.1 %copy-start.7 = (f32[768]{0:T(1024)S(1)}, f32[768]{0:T(1024)}, u32[]{:S(2)}) copy-start(f32[768]{0:T(1024)} %param.34) | copy-start | bytes 9220
  281.9 5.1 %copy-start.5 = (f32[768]{0:T(1024)}, f32[768]{0:T(1024)S(1)}, u32[]{:S(2)}) copy-start(f32[768]{0:T(1024)S(1)} %get-tuple-element.145) | copy-start | bytes 9220
  284.3 2.7 copy-start.3
  284.3 3.4 %copy-start.4 = (f32[48,128]{1,0:T(8,128)S(1)}, f32[48,128]{1,0:T(8,128)}, u32[]{:S(2)}) copy-start(f32[48,128]{1,0:T(8,128)} %get-tuple-element.142) | copy-start | bytes 73732
  284.3 4.0 %copy-start.2 = (f32[48,384]{1,0:T(8,128)S(1)}, f32[48,384]{1,0:T(8,128)}, u32[]{:S(2)}) copy-start(f32[48,384]{1,0:T(8,128)} %get-tuple-element.61) | copy-start | bytes 221188
  284.3 4.6 %copy-start.1 = (f32[48,1536]{1,0:T(8,128)S(1)}, f32[48,1536]{1,0:T(8,128)}, u32[]{:S(2)}) copy-start(f32[48,1536]{1,0:T(8,128)} %get-tuple-element.146) | copy-start | bytes 884740
  284.4 5.3 %copy-start = (f32[48,1536]{1,0:T(8,128)S(1)}, f32[48,1536]{1,0:T(8,128)}, u32[]{:S(2)}) copy-start(f32[48,1536]{1,0:T(8,128)} %get-tuple-element.63) | copy-start | bytes 884740

commit v2 on v0

--- a/solution.py
+++ b/solution.py
@@ -2,7 +2,10 @@
 
 import jax
 import jax.numpy as jnp
+import numpy as np
 from jax import lax
+from jax.experimental import pallas as pl
+from jax.experimental.pallas import tpu as pltpu
 from jax.sharding import PartitionSpec as P
 
 HEAD_DIM = 64
@@ -274,6 +277,857 @@
     )
 
 
+MESH = pl.DeviceIdType.MESH
+BF = jnp.bfloat16
+F32 = jnp.float32
+LOG2E = 1.4426950408889634
+LN2 = 0.6931471805599453
+NEG = -1e30
+ZC, XC, CC = 4, 2, 2
+DMA = pltpu.SemaphoreType.DMA
+VMEM = pltpu.VMEM
+MIB = 1 << 20
+
+
+def nn(a, b):
+    return lax.dot_general(a, b, (((1,), (0,)), ((), ())), preferred_element_type=F32)
+
+
+def nt(a, b):
+    return lax.dot_general(a, b, (((1,), (1,)), ((), ())), preferred_element_type=F32)
+
+
+def tn(a, b):
+    return lax.dot_general(a, b, (((0,), (0,)), ((), ())), preferred_element_type=F32)
+
+
+def eye(n):
+    return (
+        lax.broadcasted_iota(jnp.int32, (n, n), 0) == lax.broadcasted_iota(jnp.int32, (n, n), 1)
+    ).astype(BF)
+
+
+def flat(block):
+    return block.reshape(-1, block.shape[-1])
+
+
+class Place:
+    def __init__(self):
+        self.dp = lax.axis_index("dp")
+        self.t = lax.axis_index("tensor")
+        self.core = lax.rem(self.dp, CC)
+        self.x = lax.rem(lax.div(self.dp, CC), XC)
+        self.z = lax.div(self.dp, CC * XC)
+
+    def at(self, z, x, core):
+        return (z * XC + x) * CC + core
+
+    def z_peer(self, d):
+        return {"dp": self.at(lax.rem(self.z + d, ZC), self.x, self.core)}
+
+    def x_peer(self):
+        return {"dp": self.at(self.z, 1 - self.x, self.core)}
+
+    def core_peer(self):
+        return {"dp": self.at(self.z, self.x, 1 - self.core)}
+
+    def y_peer(self):
+        return {"tensor": 1 - self.t}
+
+    def greet(self):
+        bar = pltpu.get_barrier_semaphore()
+        peers = [self.z_peer(d) for d in (1, 2, 3)]
+        peers += [self.x_peer(), self.core_peer(), self.y_peer()]
+        for p in peers:
+            pl.semaphore_signal(bar, inc=1, device_id=p, device_id_type=MESH)
+        return bar, len(peers)
+
+
+def remote(src, dst, ss, rs, peer):
+    return pltpu.make_async_remote_copy(
+        src_ref=src, dst_ref=dst, send_sem=ss, recv_sem=rs, device_id=peer, device_id_type=MESH
+    )
+
+
+def split_cols(width):
+    a = (width // 128 + 1) // 2 * 128
+    return ((0, a), (a, width - a))
+
+
+class Gather:
+    N_SEMS = 12
+    LAG = 2
+
+    def __init__(self, place, pieces, sems):
+        self.p = place
+        self.pieces = pieces
+        self.sems = sems
+
+    def halves(self, c):
+        if c == 0:
+            return ((0, self.pieces[c][2], "zx"),)
+        (o0, w0), (o1, w1) = split_cols(self.pieces[c][2])
+        return ((o0, w0, "zxy"), (o1, w1, "zyx"))
+
+    def copies(self, c, h, k):
+        p = self.p
+        src, out, _ = self.pieces[c]
+        o, w, order = self.halves(c)[h]
+        cols = pl.ds(o, w)
+        sem = self.sems.at[c, h]
+        if k == 0:
+            dst = out.at[(p.z, p.x, p.core) + (slice(None), cols)] if c == 0 else out.at[
+                p.t, p.z, p.x, p.core, :, cols
+            ]
+            return [
+                remote(src.at[:, cols], dst, sem.at[d - 1], sem.at[2 + d], p.z_peer(d))
+                for d in (1, 2, 3)
+            ]
+        done = order[:k]
+        every = slice(None)
+        index = (every, every if "x" in done else p.x, p.core, every, cols)
+        if c:
+            index = (every if "y" in done else p.t,) + index
+        view = out.at[index]
+        if k == len(order):
+            peer = p.core_peer()
+        else:
+            peer = p.x_peer() if order[k] == "x" else p.y_peer()
+        return [remote(view, view, sem.at[4 + 2 * k], sem.at[5 + 2 * k], peer)]
+
+    def start(self, c, k):
+        for h, (_, _, order) in enumerate(self.halves(c)):
+            if k <= len(order):
+                for cp in self.copies(c, h, k):
+                    cp.start()
+
+    def wait(self, c, k):
+        for h, (_, _, order) in enumerate(self.halves(c)):
+            if k <= len(order):
+                for cp in self.copies(c, h, k):
+                    cp.wait()
+
+    def begin(self):
+        for c in range(self.LAG):
+            self.start(c, 0)
+
+    def step(self, i):
+        n = len(self.pieces)
+        for k in (3, 2, 1, 0):
+            c = i - k
+            if 0 <= c < n:
+                self.wait(c, k)
+                if k < 3:
+                    self.start(c, k + 1)
+        if i + self.LAG < n:
+            self.start(i + self.LAG, 0)
+
+
+def normal_rows(rows):
+    mean = jnp.mean(rows, axis=-1, keepdims=True)
+    centre = rows - mean
+    var = jnp.mean(centre * centre, axis=-1, keepdims=True)
+    scale = lax.rsqrt(var + EPS)
+    return centre * scale, scale
+
+
+def rotate_t(v, cosine, sine):
+    a, b = v[0:8], v[8:16]
+    return jnp.concatenate([a * cosine - b * sine, b * cosine + a * sine, v[16:]], axis=0)
+
+
+def unrotate_t(v, cosine, sine):
+    a, b = v[0:8], v[8:16]
+    return jnp.concatenate([a * cosine + b * sine, b * cosine - a * sine, v[16:]], axis=0)
+
+
+def fill_bias(place, lens_ref, other_ref, own_ref, S):
+    t = place.t
+    for m in range(MB):
+        limit = lens_ref[m]
+        key = lax.broadcasted_iota(jnp.int32, (S, 128), 0)
+        limit_other = jnp.where(t == 1, limit, 0)
+        other_ref[m] = jnp.where(key < limit_other, 0.0, NEG).astype(F32)
+        key = lax.broadcasted_iota(jnp.int32, (S, S), 0)
+        row = lax.broadcasted_iota(jnp.int32, (S, S), 1)
+        own = (key <= row) & (key + t * S < limit)
+        own_ref[m] = jnp.where(own, 0.0, NEG).astype(F32)
+
+
+def masked_rows(place_t, lens_ref, dy, start, S):
+    m, off = divmod(start, S)
+    pos = place_t * S + off + lax.broadcasted_iota(jnp.int32, (dy.shape[0], 1), 0)
+    return jnp.where(pos < lens_ref[m], dy.astype(F32), 0.0)
+
+
+class Reduce:
+    def __init__(self, place, pieces, rc, r2a, r2b, r3, r4, sems):
+        self.p = place
+        self.pieces = pieces
+        self.rc, self.r2a, self.r2b, self.r3, self.r4 = rc, r2a, r2b, r3, r4
+        self.sems = sems
+
+    def cores(self, c):
+        g, w, _ = self.pieces[c]
+        return remote(
+            g.at[:, :, :, 1 - self.p.core],
+            self.rc.at[c, :, :, :, :, pl.ds(0, w)],
+            self.sems.at[c, 0],
+            self.sems.at[c, 1],
+            self.p.core_peer(),
+        )
+
+    def second(self, c, h):
+        p = self.p
+        o, w = split_cols(self.pieces[c][1])[h]
+        if h == 0:
+            src, dst, peer = self.rc.at[c, 1 - p.t, :, :, :, pl.ds(o, w)], self.r2a, p.y_peer()
+        else:
+            src, dst, peer = self.rc.at[c, :, :, 1 - p.x, :, pl.ds(o, w)], self.r2b, p.x_peer()
+        dst = dst.at[c, :, :, :, pl.ds(0, w)]
+        return remote(src, dst, self.sems.at[c, 2 + 2 * h], self.sems.at[c, 3 + 2 * h], peer)
+
+    def third(self, c, h):
+        p = self.p
+        o, w = split_cols(self.pieces[c][1])[h]
+        if h == 0:
+            src, peer = self.r2a.at[c, :, 1 - p.x, :, pl.ds(0, w)], p.x_peer()
+        else:
+            src, peer = self.r2b.at[c, 1 - p.t, :, :, pl.ds(0, w)], p.y_peer()
+        dst = self.r3.at[c, h, :, :, pl.ds(0, w)]
+        return remote(src, dst, self.sems.at[c, 6 + 2 * h], self.sems.at[c, 7 + 2 * h], peer)
+
+    def last(self, c, h, d):
+        p = self.p
+        o, w = split_cols(self.pieces[c][1])[h]
+        src = self.r3.at[c, h, lax.rem(p.z + d, ZC), :, pl.ds(0, w)]
+        dst = self.r4.at[c, h, d - 1, :, pl.ds(0, w)]
+        k = 10 + (h * 3 + d - 1) * 2
+        return remote(src, dst, self.sems.at[c, k], self.sems.at[c, k + 1], p.z_peer(d))
+
+    N_SEMS = 22
+
+    def begin(self, c):
+        self.cores(c).start()
+
+    def step1(self, c):
+        p = self.p
+        g, width, _ = self.pieces[c]
+        self.cores(c).wait()
+        own = g[:, :, :, p.core]
+        mine = self.rc[c, :, :, :, :, 0:width].astype(F32) + own.astype(F32)
+        self.rc[c, :, :, :, :, 0:width] = mine.astype(BF)
+        for h in (0, 1):
+            self.second(c, h).start()
+
+    def step2(self, c):
+        p = self.p
+        for h in (0, 1):
+            self.second(c, h).wait()
+            o, w = split_cols(self.pieces[c][1])[h]
+            if h == 0:
+                ref, mine = self.r2a, self.rc[c, p.t, :, :, :, o : o + w]
+            else:
+                ref, mine = self.r2b, self.rc[c, :, :, p.x, :, o : o + w]
+            mine = mine.astype(F32) + ref[c, :, :, :, 0:w].astype(F32)
+            ref[c, :, :, :, 0:w] = mine.astype(BF)
+            self.third(c, h).start()
+
+    def step3(self, c):
+        p = self.p
+        for h in (0, 1):
+            self.third(c, h).wait()
+            o, w = split_cols(self.pieces[c][1])[h]
+            mine = self.r2a[c, :, p.x, :, 0:w] if h == 0 else self.r2b[c, p.t, :, :, 0:w]
+            mine = mine.astype(F32) + self.r3[c, h, :, :, 0:w].astype(F32)
+            self.r3[c, h, :, :, 0:w] = mine.astype(BF)
+            for d in (1, 2, 3):
+                self.last(c, h, d).start()
+
+    def step4(self, c):
+        p = self.p
+        parts = []
+        for h in (0, 1):
+            o, w = split_cols(self.pieces[c][1])[h]
+            for d in (1, 2, 3):
+                self.last(c, h, d).wait()
+            total = self.r3[c, h, p.z, :, 0:w].astype(F32)
+            for d in range(3):
+                total = total + self.r4[c, h, d, :, 0:w].astype(F32)
+            parts.append(total)
+        self.pieces[c][2](parts)
+
+    def step(self, i, lo, hi):
+        for k, act in enumerate((self.step4, self.step3, self.step2, self.step1)):
+            c = lo + i - (3 - k)
+            if lo <= c < hi:
+                act(c)
+
+
+def block_kernel(
+    dims,
+    x_ref,
+    dy_hbm,
+    lens_ref,
+    tab_ref,
+    ln_ref,
+    bpack_ref,
+    bsh_ref,
+    bo_ref,
+    wq_in,
+    wsh_in,
+    wout_in,
+    wup_in,
+    wdown_in,
+    out_hbm,
+    gx_hbm,
+    wf,
+    gq_ref,
+    gkv_ref,
+    go_ref,
+    gup_ref,
+    gdn_ref,
+    sm,
+    sb,
+    sf,
+    wsh,
+    wq,
+    wb,
+    won,
+    wv,
+    ball,
+    bcol,
+    dym,
+    h1,
+    h2,
+    qt,
+    att,
+    da,
+    tmp,
+    acc,
+    dh2,
+    lse_ref,
+    kvt,
+    kvo,
+    kc,
+    vc,
+    kt,
+    vte,
+    bias_o,
+    bias_s,
+    dkv,
+    dkvr,
+    dkvn,
+    gring,
+    gb,
+    ga,
+    bup,
+    sums,
+    smr,
+    rc,
+    r2a,
+    r2b,
+    r3,
+    r4,
+    gsem,
+    rsem,
+    lsem,
+    wsem,
+    ysem,
+):
+    S, HT, NH, NF, T = dims["S"], dims["HT"], dims["NH"], dims["NF"], dims["T"]
+    D = x_ref.shape[1]
+    R = sb.shape[0]
+    NB = S // 256
+    p = Place()
+    bar, npeers = p.greet()
+
+    dy_copy = pltpu.make_async_copy(dy_hbm, dym, lsem.at[0])
+    dy_copy.start()
+    ident = eye(R)
+    sb[...] = nt(ident, wout_in[...]).astype(BF)
+    for f in range(NF):
+        sf[f, :, 0:256] = wup_in[:, 256 * f : 256 * f + 256]
+        sf[f, :, 256:512] = nt(ident, wdown_in[256 * f : 256 * f + 256, :]).astype(BF)
+    ball[p.t] = bpack_ref[...]
+
+    pieces = [(wsh_in, wsh, 128), (wq_in, wq, HT), (sb, wb, HT)]
+    pieces += [(sf.at[f], wf.at[f], 512) for f in range(NF)]
+    g = Gather(p, pieces, gsem)
+    mine = (p.z, p.x, p.core)
+    locals_ = [
+        pltpu.make_async_copy(src, out.at[mine if c == 0 else (p.t,) + mine], lsem.at[1 + c])
+        for c, (src, out, _) in enumerate(pieces)
+    ]
+    for cp in locals_:
+        cp.start()
+    pl.semaphore_wait(bar, npeers)
+    g.begin()
+    bias_copy = remote(ball.at[p.t], ball.at[p.t], ysem.at[0], ysem.at[1], p.y_peer())
+    bias_copy.start()
+
+    def norm_block(i):
+        rows = pl.ds(pl.multiple_of(i * 128, 128), 128)
+        z, _ = normal_rows(x_ref[rows, :].astype(F32))
+        h1[rows, :] = (z * ln_ref[0:1, :] + ln_ref[1:2, :]).astype(BF)
+        h2[rows, :] = (z * ln_ref[2:3, :] + ln_ref[3:4, :]).astype(BF)
+
+    half = T // 256
+    pl.loop(0, half)(norm_block)
+    for cp in locals_:
+        cp.wait()
+    g.step(0)
+    pl.loop(half, 2 * half)(norm_block)
+    g.step(1)
+    fill_bias(p, lens_ref, bias_o, bias_s, S)
+    bias_copy.wait()
+    nq = HT // 128
+    for t in range(2):
+        for j in range(nq):
+            row = jnp.broadcast_to(ball[t, j : j + 1, :], (128, 128))
+            bcol[(t * nq + j) * 128 : (t * nq + j + 1) * 128, :] = row.T
+    bcol[2 * HT : 2 * HT + 128, :] = jnp.broadcast_to(bsh_ref[...], (128, 128)).T
+    g.step(2)
+
+    id256 = eye(256)
+    cosine, sine = tab_ref[p.t, 0:8, :], tab_ref[p.t, 8:16, :]
+    wsh_t = nt(eye(128), flat(wsh[...])).astype(BF)
+    for m in range(MB):
+        cols = slice(m * S, m * S + S)
+        kv = nt(wsh_t, h1[cols, :]) + bcol[2 * HT : 2 * HT + 128, 0:1]
+        kvt[0:HEAD_DIM, cols] = rotate_t(kv[0:HEAD_DIM], cosine, sine).astype(BF)
+        kvt[HEAD_DIM:, cols] = kv[HEAD_DIM:].astype(BF)
+    kv_copy = remote(kvt, kvo, ysem.at[2], ysem.at[3], p.y_peer())
+    kv_copy.start()
+    g.step(3)
+    dy_copy.wait()
+    for b in range(T // 256):
+        rows = slice(b * 256, b * 256 + 256)
+        dym[rows, :] = masked_rows(p.t, lens_ref, dym[rows, :], b * 256, S).astype(BF)
+    g.step(4)
+
+    for t in range(2):
+        wq_t = nt(eye(HT), flat(wq[t])).astype(BF)
+        for m in range(MB):
+            cols = slice(m * S, m * S + S)
+            q = nt(wq_t, h1[cols, :])
+            for h in range(HT // HEAD_DIM):
+                base = t * HT + h * HEAD_DIM
+                qh = q[h * HEAD_DIM : (h + 1) * HEAD_DIM] + bcol[base : base + HEAD_DIM, 0:1]
+                qh = rotate_t(qh, cosine, sine) * (0.125 * LOG2E)
+                qt[base : base + HEAD_DIM, cols] = qh.astype(BF)
+
+    kv_copy.wait()
+    for m in range(MB):
+        cols = slice(m * S, m * S + S)
+        for part, src in ((0, kvo), (1, kvt)):
+            keys = slice(part * S, part * S + S)
+            kt[m, :, keys] = src[0:HEAD_DIM, cols]
+            vte[m, 0:HEAD_DIM, keys] = src[HEAD_DIM:, cols]
+        ones = (lax.broadcasted_iota(jnp.int32, (16, 2 * S), 0) == 0).astype(BF)
+        vte[m, HEAD_DIM:, :] = ones
+        for b in range(2 * NB):
+            blk = slice(b * 256, b * 256 + 256)
+            kc[m, blk, :] = nt(id256, kt[m, :, blk]).astype(BF)
+            vc[m, blk, :] = nt(id256, vte[m, 0:HEAD_DIM, blk]).astype(BF)
+
+    def spots(i, group):
+        res = []
+        for u in range(group):
+            j = i * group + u
+            m, h = lax.div(j, NH), lax.rem(j, NH)
+            head = pl.ds(pl.multiple_of(h * HEAD_DIM, HEAD_DIM), HEAD_DIM)
+            for r in range(NB):
+                cols = pl.ds(pl.multiple_of(m * S + r * 256, 256), 256)
+                res.append((j, m, head, cols, S + 256 * (r + 1), r))
+        return res
+
+    def scores(m, q, nk, r):
+        s = nn(kc[m, 0:nk, :], q)
+        wide = slice(r * 256, r * 256 + 256)
+        other = bias_o[m]
+        other = jnp.concatenate([other, other], axis=1)
+        return jnp.concatenate([s[0:S] + other, s[S:nk] + bias_s[m, 0 : nk - S, wide]], axis=0)
+
+    group = 3
+
+    @pl.loop(0, MB * NH // group)
+    def _(i):
+        todo = spots(i, group)
+        sc = [scores(m, qt[head, cols], nk, r) for _, m, head, cols, nk, r in todo]
+        tops = [jnp.max(s, axis=0, keepdims=True) for s in sc]
+        ex = [jnp.exp2(s - top).astype(BF) for s, top in zip(sc, tops)]
+        for (j, m, head, cols, nk, r), e, top in zip(todo, ex, tops):
+            o = nn(vte[m, :, 0:nk], e)
+            total = o[HEAD_DIM : HEAD_DIM + 1]
+            att[head, cols] = (o[0:HEAD_DIM] * (1.0 / total)).astype(BF)
+            lse_ref[j, :, r * 256 : r * 256 + 256] = top + jnp.log2(total)
+        for at, k in ((0, 5), (3, 6), (6, 7)):
+            pl.when(i == at)(partial(g.step, k))
+
+    for t in range(2):
+        won[t * HT : (t + 1) * HT, :] = nt(eye(HT), flat(wb[t])).astype(BF)
+
+    def load(f, slot):
+        return pltpu.make_async_copy(wf.at[f], wv.at[slot], wsem.at[slot])
+
+    load(0, 0).start()
+    for b in range(T // 256):
+        rows = slice(b * 256, b * 256 + 256)
+        tmp[rows, :] = nt(id256, att[:, rows]).astype(BF)
+    acc[...] = x_ref[...].astype(F32) + bo_ref[...] + nn(tmp[...], won[...])
+    for t in range(2):
+        cols = slice(t * HT, (t + 1) * HT)
+        gb[t] = tn(dym[...], tmp[:, cols]).astype(BF).reshape(ZC, XC, CC, R, HT)
+
+    def put_out(parts):
+        a = parts[0].shape[1]
+        go_ref[:, 0:a] = parts[0]
+        go_ref[:, a:] = parts[1]
+
+    def put_ffn(f):
+        def put(parts):
+            gup_ref[:, f * 256 : f * 256 + 256] = parts[0]
+            gdn_ref[:, f * 256 : f * 256 + 256] = parts[1]
+
+        return put
+
+    def put_a(parts):
+        a = parts[0].shape[1]
+        gq_ref[:, 0:a] = parts[0]
+        gq_ref[:, a:HT] = parts[1][:, 0 : HT - a]
+        gkv_ref[...] = parts[1][:, HT - a :]
+
+    sums_of = [(gb, HT, put_out)]
+    sums_of += [(gring.at[f % 3], 512, put_ffn(f)) for f in range(NF)]
+    sums_of += [(ga, HT + 128, put_a)]
+    red = Reduce(p, sums_of, rc, r2a, r2b, r3, r4, rsem)
+    last = NF + 1
+    red.begin(0)
+    dh2[...] = jnp.zeros_like(dh2)
+    first = ball.shape[1] - 1 - 2 * NF
+
+    @pl.loop(0, NF)
+    def _(f):
+        slot = lax.rem(f, 2)
+        load(f, slot).wait()
+        for k in range(NF - 1):
+
+            @pl.when(f == k)
+            def _():
+                g.step(8 + k)
+                load(k + 1, (k + 1) % 2).start()
+
+        for k in range(2, NF):
+            pl.when(f == k)(partial(red.step, k - 2, 0, last))
+        wu = [flat(wv[slot, t, :, :, :, :, 0:256]) for t in range(2)]
+        wd = [flat(wv[slot, t, :, :, :, :, 256:512]) for t in range(2)]
+        gslot = lax.rem(f, 3)
+        hid = [nn(h2[...], wu[t]) for t in range(2)]
+        dact = [nn(dym[...], wd[t]) for t in range(2)]
+        act, dhid = [], []
+        for t in range(2):
+            row = jnp.concatenate(
+                [ball[t, pl.ds(first + 2 * f, 1), :], ball[t, pl.ds(first + 2 * f + 1, 1), :]],
+                axis=1,
+            )
+            u = hid[t] + row
+            cdf = 0.5 + 0.5 * lax.erf(u * 0.7071067811865476)
+            dens = jnp.exp(-0.5 * u * u) * 0.3989422804014327
+            act.append((u * cdf).astype(BF))
+            d = (dact[t] * (cdf + u * dens)).astype(BF)
+            dhid.append(d)
+            total = jnp.sum(d.astype(F32), axis=0, keepdims=True)
+            bup[f, 2 * t : 2 * t + 1, :] = total[:, 0:128]
+            bup[f, 2 * t + 1 : 2 * t + 2, :] = total[:, 128:256]
+        acc[...] += nt(act[0], wd[0]) + nt(act[1], wd[1])
+        dh2[...] += nt(dhid[0], wu[0]) + nt(dhid[1], wu[1])
+        for t in range(2):
+            gd = tn(dym[...], act[t]).astype(BF)
+            gring[gslot, t, :, :, :, :, 256:512] = gd.reshape(ZC, XC, CC, R, 256)
+            gu = tn(h2[...], dhid[t]).astype(BF)
+            gring[gslot, t, :, :, :, :, 0:256] = gu.reshape(ZC, XC, CC, R, 256)
+        for k in range(NF):
+            pl.when(f == k)(partial(red.begin, 1 + k))
+
+    h2[...] = acc[...].astype(BF)
+    out_copy = pltpu.make_async_copy(h2, out_hbm, lsem.at[0])
+    out_copy.start()
+
+    da[...] = nt(won[...], dym[...]).astype(BF)
+    dkv[...] = jnp.zeros_like(dkv)
+    back = 2
+
+    @pl.loop(0, MB * NH // back)
+    def _(i):
+        todo = spots(i, back)
+        qs = [qt[head, cols] for _, m, head, cols, nk, r in todo]
+        das = [da[head, cols] for _, m, head, cols, nk, r in todo]
+        sc = [scores(m, q, nk, r) for (_, m, head, cols, nk, r), q in zip(todo, qs)]
+        dp = [nn(vc[m, 0:nk, :], d) for (_, m, head, cols, nk, r), d in zip(todo, das)]
+        pr, ds = [], []
+        for (j, m, head, cols, nk, r), d, s, dpj in zip(todo, das, sc, dp):
+            delta = jnp.sum(d.astype(F32) * att[head, cols].astype(F32), axis=0, keepdims=True)
+            w = jnp.exp2(s - lse_ref[j, :, r * 256 : r * 256 + 256])
+            pr.append(w.astype(BF))
+            ds.append((w * (dpj - delta)).astype(BF))
+        for (j, m, head, cols, nk, r), d in zip(todo, ds):
+            wide = slice(r * 256, r * 256 + 256)
+            dq = nn(kt[m, :, 0:nk], d)
+            dq = unrotate_t(dq, tab_ref[p.t, 0:8, wide], tab_ref[p.t, 8:16, wide])
+            qt[head, cols] = (dq * 0.125).astype(BF)
+        m = todo[0][1]
+        for blk in range(NB):
+            lo = 0 if blk == 0 else S + 256 * blk
+            hi = S + 256 * (blk + 1)
+            left, right = [], []
+            for u, (_, _, _, _, nk, r) in enumerate(todo):
+                if nk >= hi:
+                    zero = jnp.zeros_like(qs[u])
+                    left += [ds[u][lo:hi], pr[u][lo:hi]]
+                    right += [
+                        jnp.concatenate([qs[u], zero], axis=0),
+                        jnp.concatenate([zero, das[u]], axis=0),
+                    ]
+            dkv[m, lo:hi, :] += nt(
+                jnp.concatenate(left, axis=1), jnp.concatenate(right, axis=1)
+            )
+        for k in range(NF - 2, last + 3):
+            pl.when(i == 2 * (k - (NF - 2)) + 1)(partial(red.step, k, 0, last))
+
+    kv_back = remote(dkv.at[:, 0:S, :], dkvr, ysem.at[4], ysem.at[5], p.y_peer())
+    kv_back.start()
+    for b in range(T // 256):
+        rows = slice(b * 256, b * 256 + 256)
+        tmp[rows, :] = nt(id256, qt[:, rows]).astype(BF)
+    for t in range(2):
+        gq = tn(h1[...], tmp[:, t * HT : (t + 1) * HT]).astype(BF)
+        ga[t, :, :, :, :, 0:HT] = gq.reshape(ZC, XC, CC, R, HT)
+    kv_back.wait()
+    for m in range(MB):
+        both = (dkv[m, S : 2 * S, :] + dkvr[m]).T
+        dk = unrotate_t(both[0:HEAD_DIM], cosine, sine) * LN2
+        both = jnp.concatenate([dk, both[HEAD_DIM:]], axis=0).astype(BF)
+        for b in range(NB):
+            rows = slice(m * S + b * 256, m * S + b * 256 + 256)
+            dkvn[rows, :] = nt(id256, both[:, b * 256 : b * 256 + 256]).astype(BF)
+    gkv = tn(h1[...], dkvn[...]).astype(BF).reshape(ZC, XC, CC, R, 128)
+    for t in range(2):
+        ga[t, :, :, :, :, HT:] = gkv
+    red.begin(last)
+
+    sums[...] = jnp.zeros_like(sums)
+    wqf = [flat(wq[t]) for t in range(2)]
+    wshf = flat(wsh[...])
+    for b in range(T // 256):
+        rows = slice(b * 256, b * 256 + 256)
+        dq, dkvb = tmp[rows, :], dkvn[rows, :]
+        dh1 = nt(dq[:, 0:HT], wqf[0]) + nt(dq[:, HT:], wqf[1]) + nt(dkvb, wshf)
+        dh2b = dh2[rows, :]
+        z, scale = normal_rows(x_ref[rows, :].astype(F32))
+        dy = dym[rows, :].astype(F32)
+        e = dh1 * ln_ref[0:1, :] + dh2b * ln_ref[2:3, :]
+        back_in = scale * (
+            e - jnp.mean(e, axis=-1, keepdims=True) - z * jnp.mean(e * z, axis=-1, keepdims=True)
+        )
+        h1[rows, :] = (dy + back_in).astype(BF)
+        for k, v in enumerate((dh1 * z, dh1, dh2b * z, dh2b, dy, dq.astype(F32))):
+            sums[k : k + 1, :] += jnp.sum(v, axis=0, keepdims=True)
+        sums[6:7, 0:128] += jnp.sum(dkvb.astype(F32), axis=0, keepdims=True)
+        if b < 2:
+            red.step(b, last, last + 1)
+    gx_copy = pltpu.make_async_copy(h1, gx_hbm, lsem.at[1])
+    gx_copy.start()
+    n = D // 128
+    for k in range(6):
+        for j in range(n):
+            sm[k * n + j : k * n + j + 1, :] = sums[k : k + 1, j * 128 : j * 128 + 128]
+    sm[6 * n : 6 * n + 4, :] = jnp.zeros((4, 128), F32)
+    sm[6 * n : 6 * n + 1, :] = sums[6:7, 0:128]
+    for f in range(NF):
+        sm[6 * n + 4 + 4 * f : 6 * n + 8 + 4 * f, :] = bup[f]
+
+    for k, peer in enumerate((p.core_peer(), p.y_peer(), p.x_peer())):
+        cp = remote(sm, smr.at[k], ysem.at[6 + 2 * k], ysem.at[7 + 2 * k], peer)
+        cp.start()
+        if k < 2:
+            red.step(k + 2, last, last + 1)
+        cp.wait()
+        sm[...] += smr[k]
+    cps = [
+        remote(sm, smr.at[2 + d], ysem.at[10 + 2 * d], ysem.at[11 + 2 * d], p.z_peer(d))
+        for d in (1, 2, 3)
+    ]
+    for cp in cps:
+        cp.start()
+    for cp in cps:
+        cp.wait()
+    sm[...] += smr[3] + smr[4] + smr[5]
+    out_copy.wait()
+    gx_copy.wait()
+
+
+def angle_table(S):
+    places = np.arange(2 * S, dtype=np.float64)
+    freqs = 10000.0 ** (-np.arange(ROT // 2) * 2.0 / ROT)
+    angles = (places[:, None] * freqs[None, :]).astype(np.float32).astype(np.float64)
+    tab = np.concatenate([np.cos(angles).T, np.sin(angles).T], axis=0).astype(np.float32)
+    return tab.reshape(ROT, 2, S).transpose(1, 0, 2)
+
+
+def token_plan(
+    block_input,
+    cotangent,
+    lengths,
+    ln1_gain,
+    ln1_bias,
+    ln2_gain,
+    ln2_bias,
+    w_query,
+    b_query,
+    w_shared,
+    b_shared,
+    w_out,
+    b_out,
+    w_up,
+    b_up,
+    w_down,
+    b_down,
+):
+    S, D = block_input.shape[2:]
+    R, HT = w_query.shape
+    FT = w_up.shape[1]
+    NF, T, NH = FT // 256, MB * S, 2 * HT // HEAD_DIM
+    dims = dict(S=S, HT=HT, NF=NF, T=T, NH=NH)
+    plane = (ZC, XC, CC, R)
+    full = (2,) + plane
+    t = lax.axis_index("tensor")
+
+    def s(shape, dtype):
+        return jax.ShapeDtypeStruct(shape, dtype)
+
+    vm = pl.BlockSpec(memory_space=VMEM)
+    hbm = pl.BlockSpec(memory_space=pl.ANY)
+    smem = pl.BlockSpec(memory_space=pltpu.SMEM)
+
+    ln = jnp.stack([ln1_gain, ln1_bias, ln2_gain, ln2_bias])
+    bpack = jnp.concatenate([b_query, b_up, jnp.zeros((128,), F32)]).reshape(-1, 128)
+    nb = bpack.shape[0]
+    np_ = NF + 2
+    n_small = 6 * (D // 128) + 4 + 4 * NF
+
+    outs = pl.pallas_call(
+        partial(block_kernel, dims),
+        out_shape=[
+            s((T, D), BF),
+            s((T, D), BF),
+            s((NF,) + full + (512,), BF),
+            s((R, HT), F32),
+            s((R, 128), F32),
+            s((R, HT), F32),
+            s((R, FT), F32),
+            s((R, FT), F32),
+            s((n_small, 128), F32),
+        ],
+        in_specs=[vm, hbm, smem] + [vm] * 10,
+        out_specs=[hbm] * 3 + [vm] * 6,
+        scratch_shapes=[
+            VMEM((R, HT), BF),
+            VMEM((NF, R, 512), BF),
+            VMEM(plane + (128,), BF),
+            VMEM(full + (HT,), BF),
+            VMEM(full + (HT,), BF),
+            VMEM((2 * HT, D), BF),
+            VMEM((2,) + full + (512,), BF),
+            VMEM((2, nb, 128), F32),
+            VMEM((2 * HT + 128, 128), F32),
+            VMEM((T, D), BF),
+            VMEM((T, D), BF),
+            VMEM((T, D), BF),
+            VMEM((D, T), BF),
+            VMEM((D, T), BF),
+            VMEM((D, T), BF),
+            VMEM((T, D), BF),
+            VMEM((T, D), F32),
+            VMEM((T, D), F32),
+            VMEM((MB * NH, 1, S), F32),
+            VMEM((128, T), BF),
+            VMEM((128, T), BF),
+            VMEM((MB, 2 * S, HEAD_DIM), BF),
+            VMEM((MB, 2 * S, HEAD_DIM), BF),
+            VMEM((MB, HEAD_DIM, 2 * S), BF),
+            VMEM((MB, HEAD_DIM + 16, 2 * S), BF),
+            VMEM((MB, S, 128), F32),
+            VMEM((MB, S, S), F32),
+            VMEM((MB, 2 * S, 128), F32),
+            VMEM((MB, S, 128), F32),
+            VMEM((T, 128), BF),
+            VMEM((3,) + full + (512,), BF),
+            VMEM(full + (HT,), BF),
+            VMEM(full + (HT + 128,), BF),
+            VMEM((NF, 4, 128), F32),
+            VMEM((8, D), F32),
+            VMEM((6, n_small, 128), F32),
+            VMEM((np_, 2, ZC, XC, R, 512), BF),
+            VMEM((np_, ZC, XC, R, 256), BF),
+            VMEM((np_, 2, ZC, R, 256), BF),
+            VMEM((np_, 2, ZC, R, 256), BF),
+            VMEM((np_, 2, 3, R, 256), BF),
+            DMA((np_ + 1, 2, Gather.N_SEMS)),
+            DMA((np_, Reduce.N_SEMS)),
+            DMA((np_ + 2,)),
+            DMA((2,)),
+            DMA((18,)),
+        ],
+        compiler_params=pltpu.CompilerParams(
+            vmem_limit_bytes=64 * MIB - 65536, collective_id=0, has_side_effects=True
+        ),
+        name="block",
+    )(
+        block_input.reshape(T, D),
+        cotangent.reshape(T, D),
+        lengths.reshape(MB),
+        jnp.asarray(angle_table(S)),
+        ln,
+        bpack,
+        b_shared.reshape(1, 128),
+        (b_out + b_down).reshape(1, D),
+        w_query,
+        w_shared,
+        w_out,
+        w_up,
+        w_down,
+    )
+    out, gx, _, gq, gkv, go, gup, gdn, sm = outs
+    n = D // 128
+    five = sm[0 : 5 * n].reshape(5, D)
+    bq = lax.dynamic_index_in_dim(sm[5 * n : 6 * n].reshape(2, HT), t, 0, False)
+    bkv = sm[6 * n]
+    bup = lax.dynamic_index_in_dim(sm[6 * n + 4 :].reshape(NF, 2, 256), t, 1, False).reshape(FT)
+    return (
+        out.reshape(block_input.shape),
+        gx.reshape(block_input.shape),
+        five[0],
+        five[1],
+        five[2],
+        five[3],
+        gq,
+        bq,
+        gkv,
+        bkv,
+        go.T,
+        five[4],
+        gup,
+        bup,
+        gdn.T,
+        five[4],
+    )
+
+
+def fits_token_plan(mesh):
+    return dict(mesh.shape) == {"dp": ZC * XC * CC, "tensor": 2}
+
+
 def solution(mesh):
     in_specs = (
         P(None, "dp", "tensor", None),
@@ -312,6 +1166,7 @@
         P("tensor", "dp"),
         P(),
     )
+    step = token_plan if fits_token_plan(mesh) else per_device
     return jax.shard_map(
-        per_device, mesh=mesh, in_specs=in_specs, out_specs=out_specs, check_vma=False
-    )
+        step, mesh=mesh, in_specs=in_specs, out_specs=out_specs, check_vma=False
+    )

time: 970 us -> 217 us (0.22)
  waiting for transfers between devices: 330 us -> 0 us
  matrix products: 257 us -> 0 us
  blocking collectives: 209 us -> 0 us
  Pallas kernels: 0 us -> 193 us
  other arithmetic: 96.7 us -> 2.62 us
  local copies, waits for them, and re-layouts: 38.3 us -> 19 us
  loops' own time: 16.8 us -> 0 us
  between operations: 15.7 us -> 0.71 us
    reduce_scatter x11 -> x0, waiting for transfers between devices: 326 us -> none  [the longest x1 79.4 us: reduce_each(): lax.psum_scatter(step_grads[4], 'dp', scatter_dimension=1, tiled=True)]
    dot_general x58 -> x0, matrix products: 257 us -> none  [the longest x2 39.8 us: per_device(): jnp.einsum('ld,fd->lf', whole_up, wdown_all, preferred_element_type=jnp.f...]
    pallas_call x0 -> x1, Pallas kernels: none -> 193 us  [token_plan(): pl.pallas_call(partial(block_kernel, dims), out_shape=[s((T, D), BF), s((...]
    psum x3 -> x0, blocking collectives: 145 us -> none  [the longest x1 61.4 us: per_device(): sum_bq, sum_bkv, sum_bup = lax.psum((sum_bq, sum_bkv, sum_bup), 'dp')]
    all_gather x3 -> x0, blocking collectives: 63.4 us -> none  [the longest x1 24.8 us: fetch_each(): lax.all_gather(w_query, 'dp', axis=0, tiled=True)]
    convert_element_type x14 -> x0, other arithmetic: 45.5 us -> none  [the longest x4 27.2 us: block(): dscores = (probs * (dprobs - delta)).astype(jnp.bfloat16)]
    reduce_sum x9 -> x0, other arithmetic: 20.4 us -> none  [the longest x4 13.5 us: block(): total = jnp.sum(expo, axis=-1, keepdims=True)]
    another operation x4 -> x0, loops' own time: 16.8 us -> none  [the longest x2 8.79 us: attend_back(): (dkeys, dvalues), drows = lax.scan(block, (empty, empty), (starts, logsum))]
  transfers between devices with their start and end apart: 19 -> 0, of which waited for: 5 -> 0; matrix products, arithmetic and copies ran while one was open for 38% -> 0% of each run, Pallas kernels for 0% -> 0%
where the time goes in v2:
time: 217 us; the launch traced here: 216 us
  Pallas kernels  193 us (89%)
  local copies, waits for them, and re-layouts  19 us (9%)
  other arithmetic  2.62 us (1%)
    pallas_call x1, Pallas kernels, token_plan(): pl.pallas_call(partial(block_kernel, dims), out_shape=[s((T, D), BF), s((...  193 us
    unnamed x24, local copies, waits for them, and re-layouts  11.2 us

profile of v2, /device:TPU:0, one launch (start us, length us, event | category | flops | bytes accessed | tf_op | source)
XLA Modules:
  0.0 215.9 jit_solution(9654048471536969974)
XLA Ops:
  0.6 1.8 copy.35.wdown_in
  2.5 1.5 copy.34.wout_in
  4.0 0.7 stack.15
  4.7 0.7 stack.16
  5.4 0.7 stack.17
  6.1 0.7 stack.18
  6.7 0.6 pad_maximum_fusion.ln_ref
  7.4 1.3 maximum_bitcast_fusion.bpack_ref
  8.7 0.7 add.9
  9.4 0.6 reshape.82.bo_ref
  10.0 193.5 %block.1 = (bf16[1024,768]{1,0:T(8,128)(2,1)}, bf16[1024,768]{1,0:T(8,128)(2,1)}, bf16[6,2,4,2,2,48,512]{6,5,4,3,2,1,0:T(8,128)(2,1)}, f32[48,384]{1,0:T(8,128)}...) custom-call(bf16[1024,768]{1,0:T(8,128)(2,1)} %bitcast.28, ...), custom_call_target="tpu_custom_call" | custom-call | tf_op jit(solution)/shard_map/block/pallas_call | solution.py:1019
  203.5 1.4 slice_bitcast_fusion
  204.9 0.0 copy-start.6
  204.9 0.6 dynamic-slice_reduce_fusion.1
  205.5 0.7 slice.43
  206.2 0.6 reshape.87
  206.8 1.2 slice_bitcast_fusion.5
  208.0 0.6 copy.46
  208.6 0.0 copy-start
  208.6 2.8 %copy.47 = bf16[2,1,512,768]{3,2,1,0:T(8,128)(2,1)} copy(bf16[2,1,512,768]{3,2,1,0:T(8,128)(2,1)} %bitcast.27) | data formatting | bytes 3145728
  211.4 0.0 copy-done.6
  211.4 0.0 copy-done
  211.4 0.0 copy-start.4
  211.4 0.0 copy-start.5
  211.4 0.0 copy-start.3
  211.4 0.0 copy-start.2
  211.4 0.0 copy-start.1
  211.4 1.1 copy.48
  212.6 0.0 copy-done.4
  212.6 0.6 copy.49
  213.2 0.0 copy-done.5
  213.2 0.6 copy.50
  213.8 0.0 copy-done.3
  213.8 0.6 copy.51
  214.4 0.0 copy-done.2
  214.4 0.7 copy.52
  215.2 0.0 copy-done.1
  215.2 0.7 copy.53
  (4 shorter events, 0.0 us)
Async XLA Ops:
  204.9 6.5 %copy-start.6 = (f32[768]{0:T(1024)}, f32[768]{0:T(1024)S(1)}, u32[]{:S(2)}) copy-start(f32[768]{0:T(1024)S(1)} %get-tuple-element.113) | copy-start | bytes 9220
  208.6 2.8 %copy-start = (bf16[1024,768]{1,0:T(8,128)(2,1)S(1)}, bf16[1024,768]{1,0:T(8,128)(2,1)}, u32[]{:S(2)}) copy-start(bf16[1024,768]{1,0:T(8,128)(2,1)} %get-tuple-element.25) | copy-start | bytes 4718596
  211.4 1.2 copy-start.4
  211.4 1.8 copy-start.5
  211.4 2.4 %copy-start.3 = (f32[48,384]{1,0:T(8,128)S(1)}, f32[48,384]{1,0:T(8,128)}, u32[]{:S(2)}) copy-start(f32[48,384]{1,0:T(8,128)} %get-tuple-element.29) | copy-start | bytes 221188
  211.4 3.1 %copy-start.2 = (f32[48,1536]{1,0:T(8,128)S(1)}, f32[48,1536]{1,0:T(8,128)}, u32[]{:S(2)}) copy-start(f32[48,1536]{1,0:T(8,128)} %get-tuple-element.114) | copy-start | bytes 884740
  211.4 3.8 %copy-start.1 = (f32[48,1536]{1,0:T(8,128)S(1)}, f32[48,1536]{1,0:T(8,128)}, u32[]{:S(2)}) copy-start(f32[48,1536]{1,0:T(8,128)} %get-tuple-element.31) | copy-start | bytes 884740

commit v3 on v2

--- a/solution.py
+++ b/solution.py
@@ -334,10 +334,18 @@
     def y_peer(self):
         return {"tensor": 1 - self.t}
 
+    def layer_peers(self):
+        res = []
+        for k in range(1, 8):
+            x = 1 - self.x if k & 1 else self.x
+            t = 1 - self.t if k & 2 else self.t
+            core = 1 - self.core if k & 4 else self.core
+            res.append({"dp": self.at(self.z, x, core), "tensor": t})
+        return res
+
     def greet(self):
         bar = pltpu.get_barrier_semaphore()
-        peers = [self.z_peer(d) for d in (1, 2, 3)]
-        peers += [self.x_peer(), self.core_peer(), self.y_peer()]
+        peers = [self.z_peer(d) for d in (1, 2, 3)] + self.layer_peers()
         for p in peers:
             pl.semaphore_signal(bar, inc=1, device_id=p, device_id_type=MESH)
         return bar, len(peers)
@@ -356,71 +364,93 @@
 
 class Gather:
     N_SEMS = 12
-    LAG = 2
 
     def __init__(self, place, pieces, sems):
         self.p = place
         self.pieces = pieces
         self.sems = sems
 
-    def halves(self, c):
-        if c == 0:
-            return ((0, self.pieces[c][2], "zx"),)
-        (o0, w0), (o1, w1) = split_cols(self.pieces[c][2])
-        return ((o0, w0, "zxy"), (o1, w1, "zyx"))
+    def own(self, c, h):
+        p = self.p
+        _, o, w, order = self.pieces[c][0][h]
+        index = (p.z, p.x, p.core, slice(None), pl.ds(o, w))
+        return self.pieces[c][1].at[(p.t,) + index if "y" in order else index]
 
     def copies(self, c, h, k):
         p = self.p
-        src, out, _ = self.pieces[c]
-        o, w, order = self.halves(c)[h]
-        cols = pl.ds(o, w)
+        src, o, w, order = self.pieces[c][0][h]
         sem = self.sems.at[c, h]
         if k == 0:
-            dst = out.at[(p.z, p.x, p.core) + (slice(None), cols)] if c == 0 else out.at[
-                p.t, p.z, p.x, p.core, :, cols
-            ]
+            dst = self.own(c, h)
             return [
-                remote(src.at[:, cols], dst, sem.at[d - 1], sem.at[2 + d], p.z_peer(d))
-                for d in (1, 2, 3)
+                remote(src, dst, sem.at[d - 1], sem.at[2 + d], p.z_peer(d)) for d in (1, 2, 3)
             ]
         done = order[:k]
         every = slice(None)
-        index = (every, every if "x" in done else p.x, p.core, every, cols)
-        if c:
+        index = (every, every if "x" in done else p.x, p.core, every, pl.ds(o, w))
+        if "y" in order:
             index = (every if "y" in done else p.t,) + index
-        view = out.at[index]
+        view = self.pieces[c][1].at[index]
         if k == len(order):
             peer = p.core_peer()
         else:
             peer = p.x_peer() if order[k] == "x" else p.y_peer()
         return [remote(view, view, sem.at[4 + 2 * k], sem.at[5 + 2 * k], peer)]
 
+    def each(self, c, k):
+        res = []
+        for h, (_, _, _, order) in enumerate(self.pieces[c][0]):
+            if k <= len(order):
+                res += self.copies(c, h, k)
+        return res
+
     def start(self, c, k):
-        for h, (_, _, order) in enumerate(self.halves(c)):
-            if k <= len(order):
-                for cp in self.copies(c, h, k):
-                    cp.start()
-
-    def wait(self, c, k):
-        for h, (_, _, order) in enumerate(self.halves(c)):
-            if k <= len(order):
-                for cp in self.copies(c, h, k):
-                    cp.wait()
-
-    def begin(self):
-        for c in range(self.LAG):
-            self.start(c, 0)
-
-    def step(self, i):
-        n = len(self.pieces)
-        for k in (3, 2, 1, 0):
-            c = i - k
-            if 0 <= c < n:
-                self.wait(c, k)
-                if k < 3:
-                    self.start(c, k + 1)
-        if i + self.LAG < n:
-            self.start(i + self.LAG, 0)
+        for cp in self.each(c, k):
+            cp.start()
+
+    def run(self, ops):
+        for op in ops:
+            if isinstance(op, int):
+                self.start(op, 0)
+                continue
+            c, k = op
+            for cp in self.each(c, k):
+                cp.wait()
+            self.start(c, k + 1)
+
+
+class AllSum:
+    N_SEMS = 20
+
+    def __init__(self, place, buf, got, sems):
+        self.p = place
+        self.buf, self.got, self.sems = buf, got, sems
+
+    def copies(self, k):
+        peers = [self.p.z_peer(d) for d in (1, 2, 3)] if k else self.p.layer_peers()
+        base = 7 if k else 0
+        return [
+            remote(
+                self.buf,
+                self.got.at[base + i],
+                self.sems.at[2 * (base + i)],
+                self.sems.at[2 * (base + i) + 1],
+                peer,
+            )
+            for i, peer in enumerate(peers)
+        ]
+
+    def start(self, k):
+        for cp in self.copies(k):
+            cp.start()
+
+    def end(self, k):
+        for cp in self.copies(k):
+            cp.wait()
+        total = self.buf[...]
+        for i in range(7, 10) if k else range(7):
+            total = total + self.got[i]
+        self.buf[...] = total
 
 
 def normal_rows(rows):
@@ -467,8 +497,15 @@
         self.rc, self.r2a, self.r2b, self.r3, self.r4 = rc, r2a, r2b, r3, r4
         self.sems = sems
 
+    def cols(self, c, h):
+        widths = self.pieces[c][1]
+        return sum(widths[:h]), widths[h]
+
+    def halves(self, c):
+        return range(len(self.pieces[c][1]))
+
     def cores(self, c):
-        g, w, _ = self.pieces[c]
+        g, w = self.pieces[c][0], sum(self.pieces[c][1])
         return remote(
             g.at[:, :, :, 1 - self.p.core],
             self.rc.at[c, :, :, :, :, pl.ds(0, w)],
@@ -479,7 +516,7 @@
 
     def second(self, c, h):
         p = self.p
-        o, w = split_cols(self.pieces[c][1])[h]
+        o, w = self.cols(c, h)
         if h == 0:
             src, dst, peer = self.rc.at[c, 1 - p.t, :, :, :, pl.ds(o, w)], self.r2a, p.y_peer()
         else:
@@ -489,7 +526,7 @@
 
     def third(self, c, h):
         p = self.p
-        o, w = split_cols(self.pieces[c][1])[h]
+        o, w = self.cols(c, h)
         if h == 0:
             src, peer = self.r2a.at[c, :, 1 - p.x, :, pl.ds(0, w)], p.x_peer()
         else:
@@ -499,7 +536,7 @@
 
     def last(self, c, h, d):
         p = self.p
-        o, w = split_cols(self.pieces[c][1])[h]
+        o, w = self.cols(c, h)
         src = self.r3.at[c, h, lax.rem(p.z + d, ZC), :, pl.ds(0, w)]
         dst = self.r4.at[c, h, d - 1, :, pl.ds(0, w)]
         k = 10 + (h * 3 + d - 1) * 2
@@ -512,19 +549,19 @@
 
     def step1(self, c):
         p = self.p
-        g, width, _ = self.pieces[c]
+        g, width = self.pieces[c][0], sum(self.pieces[c][1])
         self.cores(c).wait()
         own = g[:, :, :, p.core]
         mine = self.rc[c, :, :, :, :, 0:width].astype(F32) + own.astype(F32)
         self.rc[c, :, :, :, :, 0:width] = mine.astype(BF)
-        for h in (0, 1):
+        for h in self.halves(c):
             self.second(c, h).start()
 
     def step2(self, c):
         p = self.p
-        for h in (0, 1):
+        for h in self.halves(c):
             self.second(c, h).wait()
-            o, w = split_cols(self.pieces[c][1])[h]
+            o, w = self.cols(c, h)
             if h == 0:
                 ref, mine = self.r2a, self.rc[c, p.t, :, :, :, o : o + w]
             else:
@@ -535,9 +572,9 @@
 
     def step3(self, c):
         p = self.p
-        for h in (0, 1):
+        for h in self.halves(c):
             self.third(c, h).wait()
-            o, w = split_cols(self.pieces[c][1])[h]
+            o, w = self.cols(c, h)
             mine = self.r2a[c, :, p.x, :, 0:w] if h == 0 else self.r2b[c, p.t, :, :, 0:w]
             mine = mine.astype(F32) + self.r3[c, h, :, :, 0:w].astype(F32)
             self.r3[c, h, :, :, 0:w] = mine.astype(BF)
@@ -547,8 +584,8 @@
     def step4(self, c):
         p = self.p
         parts = []
-        for h in (0, 1):
-            o, w = split_cols(self.pieces[c][1])[h]
+        for h in self.halves(c):
+            o, w = self.cols(c, h)
             for d in (1, 2, 3):
                 self.last(c, h, d).wait()
             total = self.r3[c, h, p.z, :, 0:w].astype(F32)
@@ -558,10 +595,35 @@
         self.pieces[c][2](parts)
 
     def step(self, i, lo, hi):
-        for k, act in enumerate((self.step4, self.step3, self.step2, self.step1)):
-            c = lo + i - (3 - k)
+        for late, act in ((4, self.step4), (3, self.step3), (2, self.step2), (0, self.step1)):
+            c = lo + i - late
             if lo <= c < hi:
                 act(c)
+
+
+HEAD_OPS = (
+    (0, 1, 2),
+    ((0, 0), (1, 0), 3),
+    ((0, 1), (2, 0), 4),
+    ((1, 1), (0, 2), (3, 0), 5),
+    ((1, 2), (2, 1)),
+    ((1, 3), (4, 0), 6),
+)
+ATTENTION_OPS = {
+    0: ((2, 2), (3, 1), (5, 0), 7),
+    3: ((2, 3), (3, 2), (4, 1), (6, 0), 8),
+    6: ((3, 3), (4, 2), (5, 1), (7, 0)),
+}
+MIDDLE_OPS = ((4, 3), (5, 2), (6, 1), (8, 0))
+FFN_OPS = {
+    1: ((5, 3), (6, 2), (7, 1)),
+    2: ((6, 3), (7, 2), (8, 1)),
+    3: ((7, 3), (8, 2)),
+    4: ((8, 3),),
+}
+FFN_LAG = 2
+BACK_FIRST, BACK_EVERY = 0, 2
+LAST_STEP = 4
 
 
 def block_kernel(
@@ -570,26 +632,26 @@
     dy_hbm,
     lens_ref,
     tab_ref,
-    ln_ref,
-    bpack_ref,
+    g1_ref,
+    b1_ref,
+    g2_ref,
+    b2_ref,
+    wq_in,
+    bq_ref,
+    wsh_in,
     bsh_ref,
-    bo_ref,
-    wq_in,
-    wsh_in,
     wout_in,
+    bout_ref,
     wup_in,
+    bup_ref,
     wdown_in,
+    bdown_ref,
     out_hbm,
     gx_hbm,
     wf,
-    gq_ref,
-    gkv_ref,
-    go_ref,
-    gup_ref,
-    gdn_ref,
-    sm,
-    sb,
-    sf,
+    grads,
+    early,
+    late,
     wsh,
     wq,
     wb,
@@ -616,14 +678,16 @@
     bias_o,
     bias_s,
     dkv,
+    dkvs,
     dkvr,
     dkvn,
     gring,
     gb,
-    ga,
-    bup,
+    gq,
+    gkv,
     sums,
-    smr,
+    early_in,
+    late_in,
     rc,
     r2a,
     r2b,
@@ -634,51 +698,63 @@
     lsem,
     wsem,
     ysem,
+    esem,
+    asem,
 ):
     S, HT, NH, NF, T = dims["S"], dims["HT"], dims["NH"], dims["NF"], dims["T"]
     D = x_ref.shape[1]
-    R = sb.shape[0]
+    R = wq_in.shape[0]
     NB = S // 256
     p = Place()
     bar, npeers = p.greet()
-
     dy_copy = pltpu.make_async_copy(dy_hbm, dym, lsem.at[0])
     dy_copy.start()
-    ident = eye(R)
-    sb[...] = nt(ident, wout_in[...]).astype(BF)
+
+    def halves(ref):
+        return [
+            (ref.at[:, pl.ds(o, w)], o, w, order)
+            for (o, w), order in zip(split_cols(HT), ("zxy", "zyx"))
+        ]
+
+    pieces = [([(wsh_in, 0, 128, "zx")], wsh), (halves(wq_in), wq), (halves(wout_in), wb)]
     for f in range(NF):
-        sf[f, :, 0:256] = wup_in[:, 256 * f : 256 * f + 256]
-        sf[f, :, 256:512] = nt(ident, wdown_in[256 * f : 256 * f + 256, :]).astype(BF)
-    ball[p.t] = bpack_ref[...]
-
-    pieces = [(wsh_in, wsh, 128), (wq_in, wq, HT), (sb, wb, HT)]
-    pieces += [(sf.at[f], wf.at[f], 512) for f in range(NF)]
+        cols = pl.ds(256 * f, 256)
+        parts = [(wup_in.at[:, cols], 0, 256, "zxy"), (wdown_in.at[:, cols], 256, 256, "zyx")]
+        pieces.append((parts, wf.at[f]))
     g = Gather(p, pieces, gsem)
-    mine = (p.z, p.x, p.core)
-    locals_ = [
-        pltpu.make_async_copy(src, out.at[mine if c == 0 else (p.t,) + mine], lsem.at[1 + c])
-        for c, (src, out, _) in enumerate(pieces)
-    ]
-    for cp in locals_:
-        cp.start()
     pl.semaphore_wait(bar, npeers)
-    g.begin()
+    g.run(HEAD_OPS[0])
+    locals_ = []
+    for c in range(len(pieces)):
+        for h in range(len(pieces[c][0])):
+            own = pltpu.make_async_copy(pieces[c][0][h][0], g.own(c, h), lsem.at[1 + 2 * c + h])
+            own.start()
+            locals_.append(own)
+    first = HT // 128
+    rows_b = ball.shape[1]
+    ball[p.t, 0:first, :] = bq_ref[...].reshape(first, 128)
+    ball[p.t, first : first + 2 * NF, :] = bup_ref[...].reshape(2 * NF, 128)
+    ball[p.t, first + 2 * NF :, :] = jnp.zeros((rows_b - first - 2 * NF, 128), F32)
     bias_copy = remote(ball.at[p.t], ball.at[p.t], ysem.at[0], ysem.at[1], p.y_peer())
     bias_copy.start()
+
+    gain1, shift1, gain2, shift2 = (
+        ref[...].reshape(1, D) for ref in (g1_ref, b1_ref, g2_ref, b2_ref)
+    )
 
     def norm_block(i):
         rows = pl.ds(pl.multiple_of(i * 128, 128), 128)
         z, _ = normal_rows(x_ref[rows, :].astype(F32))
-        h1[rows, :] = (z * ln_ref[0:1, :] + ln_ref[1:2, :]).astype(BF)
-        h2[rows, :] = (z * ln_ref[2:3, :] + ln_ref[3:4, :]).astype(BF)
+        h1[rows, :] = (z * gain1 + shift1).astype(BF)
+        h2[rows, :] = (z * gain2 + shift2).astype(BF)
 
     half = T // 256
     pl.loop(0, half)(norm_block)
     for cp in locals_:
         cp.wait()
-    g.step(0)
+    g.run(HEAD_OPS[1])
     pl.loop(half, 2 * half)(norm_block)
-    g.step(1)
+    g.run(HEAD_OPS[2])
     fill_bias(p, lens_ref, bias_o, bias_s, S)
     bias_copy.wait()
     nq = HT // 128
@@ -686,25 +762,30 @@
         for j in range(nq):
             row = jnp.broadcast_to(ball[t, j : j + 1, :], (128, 128))
             bcol[(t * nq + j) * 128 : (t * nq + j + 1) * 128, :] = row.T
-    bcol[2 * HT : 2 * HT + 128, :] = jnp.broadcast_to(bsh_ref[...], (128, 128)).T
-    g.step(2)
+    bcol[2 * HT : 2 * HT + 128, :] = jnp.broadcast_to(bsh_ref[...].reshape(1, 128), (128, 128)).T
+    g.run(HEAD_OPS[3])
 
     id256 = eye(256)
     cosine, sine = tab_ref[p.t, 0:8, :], tab_ref[p.t, 8:16, :]
     wsh_t = nt(eye(128), flat(wsh[...])).astype(BF)
+    kv_copies = [
+        remote(kvt.at[m], kvo.at[m], ysem.at[2 + 2 * m], ysem.at[3 + 2 * m], p.y_peer())
+        for m in range(MB)
+    ]
     for m in range(MB):
-        cols = slice(m * S, m * S + S)
-        kv = nt(wsh_t, h1[cols, :]) + bcol[2 * HT : 2 * HT + 128, 0:1]
-        kvt[0:HEAD_DIM, cols] = rotate_t(kv[0:HEAD_DIM], cosine, sine).astype(BF)
-        kvt[HEAD_DIM:, cols] = kv[HEAD_DIM:].astype(BF)
-    kv_copy = remote(kvt, kvo, ysem.at[2], ysem.at[3], p.y_peer())
-    kv_copy.start()
-    g.step(3)
+        kv = nt(wsh_t, h1[m * S : m * S + S, :]) + bcol[2 * HT : 2 * HT + 128, 0:1]
+        kvt[m, 0:HEAD_DIM, :] = rotate_t(kv[0:HEAD_DIM], cosine, sine).astype(BF)
+        kvt[m, HEAD_DIM:, :] = kv[HEAD_DIM:].astype(BF)
+        kv_copies[m].start()
+    g.run(HEAD_OPS[4])
     dy_copy.wait()
+    sums[...] = jnp.zeros_like(sums)
     for b in range(T // 256):
         rows = slice(b * 256, b * 256 + 256)
-        dym[rows, :] = masked_rows(p.t, lens_ref, dym[rows, :], b * 256, S).astype(BF)
-    g.step(4)
+        dy = masked_rows(p.t, lens_ref, dym[rows, :], b * 256, S)
+        dym[rows, :] = dy.astype(BF)
+        sums[6:7, :] += jnp.sum(dy, axis=0, keepdims=True)
+    g.run(HEAD_OPS[5])
 
     for t in range(2):
         wq_t = nt(eye(HT), flat(wq[t])).astype(BF)
@@ -717,19 +798,21 @@
                 qh = rotate_t(qh, cosine, sine) * (0.125 * LOG2E)
                 qt[base : base + HEAD_DIM, cols] = qh.astype(BF)
 
-    kv_copy.wait()
-    for m in range(MB):
-        cols = slice(m * S, m * S + S)
+    def both_halves(m):
+        kv_copies[m].wait()
         for part, src in ((0, kvo), (1, kvt)):
             keys = slice(part * S, part * S + S)
-            kt[m, :, keys] = src[0:HEAD_DIM, cols]
-            vte[m, 0:HEAD_DIM, keys] = src[HEAD_DIM:, cols]
-        ones = (lax.broadcasted_iota(jnp.int32, (16, 2 * S), 0) == 0).astype(BF)
-        vte[m, HEAD_DIM:, :] = ones
+            kt[m, :, keys] = src[m, 0:HEAD_DIM, :]
+            vte[m, 0:HEAD_DIM, keys] = src[m, HEAD_DIM:, :]
+        vte[m, HEAD_DIM:, :] = (
+            lax.broadcasted_iota(jnp.int32, (16, 2 * S), 0) == 0
+        ).astype(BF)
         for b in range(2 * NB):
             blk = slice(b * 256, b * 256 + 256)
             kc[m, blk, :] = nt(id256, kt[m, :, blk]).astype(BF)
             vc[m, blk, :] = nt(id256, vte[m, 0:HEAD_DIM, blk]).astype(BF)
+
+    both_halves(0)
 
     def spots(i, group):
         res = []
@@ -753,6 +836,10 @@
 
     @pl.loop(0, MB * NH // group)
     def _(i):
+        for m in range(1, MB):
+            pl.when(i == m * NH // group)(partial(both_halves, m))
+        for at, ops in ATTENTION_OPS.items():
+            pl.when(i == at)(partial(g.run, ops))
         todo = spots(i, group)
         sc = [scores(m, qt[head, cols], nk, r) for _, m, head, cols, nk, r in todo]
         tops = [jnp.max(s, axis=0, keepdims=True) for s in sc]
@@ -762,9 +849,8 @@
             total = o[HEAD_DIM : HEAD_DIM + 1]
             att[head, cols] = (o[0:HEAD_DIM] * (1.0 / total)).astype(BF)
             lse_ref[j, :, r * 256 : r * 256 + 256] = top + jnp.log2(total)
-        for at, k in ((0, 5), (3, 6), (6, 7)):
-            pl.when(i == at)(partial(g.step, k))
-
+
+    g.run(MIDDLE_OPS)
     for t in range(2):
         won[t * HT : (t + 1) * HT, :] = nt(eye(HT), flat(wb[t])).astype(BF)
 
@@ -775,37 +861,29 @@
     for b in range(T // 256):
         rows = slice(b * 256, b * 256 + 256)
         tmp[rows, :] = nt(id256, att[:, rows]).astype(BF)
-    acc[...] = x_ref[...].astype(F32) + bo_ref[...] + nn(tmp[...], won[...])
+    tail_bias = (bout_ref[...] + bdown_ref[...]).reshape(1, D)
+    acc[...] = x_ref[...].astype(F32) + tail_bias + nn(tmp[...], won[...])
     for t in range(2):
         cols = slice(t * HT, (t + 1) * HT)
         gb[t] = tn(dym[...], tmp[:, cols]).astype(BF).reshape(ZC, XC, CC, R, HT)
 
-    def put_out(parts):
-        a = parts[0].shape[1]
-        go_ref[:, 0:a] = parts[0]
-        go_ref[:, a:] = parts[1]
-
-    def put_ffn(f):
-        def put(parts):
-            gup_ref[:, f * 256 : f * 256 + 256] = parts[0]
-            gdn_ref[:, f * 256 : f * 256 + 256] = parts[1]
-
-        return put
-
-    def put_a(parts):
-        a = parts[0].shape[1]
-        gq_ref[:, 0:a] = parts[0]
-        gq_ref[:, a:HT] = parts[1][:, 0 : HT - a]
-        gkv_ref[...] = parts[1][:, HT - a :]
-
-    sums_of = [(gb, HT, put_out)]
-    sums_of += [(gring.at[f % 3], 512, put_ffn(f)) for f in range(NF)]
-    sums_of += [(ga, HT + 128, put_a)]
+    def put(*firsts):
+        def store(parts):
+            for o, v in zip(firsts, parts):
+                grads[:, o : o + v.shape[1]] = v
+
+        return store
+
+    wide = [w for _, w in split_cols(HT)]
+    at_out, at_up, at_down = HT + 128, 2 * HT + 128, 2 * HT + 128 + 256 * NF
+    sums_of = [(gb, wide, put(at_out, at_out + wide[0]))]
+    for f in range(NF):
+        sums_of.append((gring.at[f % 3], [256, 256], put(at_up + 256 * f, at_down + 256 * f)))
+    sums_of += [(gq, wide, put(0, wide[0])), (gkv, [128], put(HT))]
     red = Reduce(p, sums_of, rc, r2a, r2b, r3, r4, rsem)
     last = NF + 1
     red.begin(0)
     dh2[...] = jnp.zeros_like(dh2)
-    first = ball.shape[1] - 1 - 2 * NF
 
     @pl.loop(0, NF)
     def _(f):
@@ -815,11 +893,11 @@
 
             @pl.when(f == k)
             def _():
-                g.step(8 + k)
+                g.run(FFN_OPS.get(k, ()))
                 load(k + 1, (k + 1) % 2).start()
 
-        for k in range(2, NF):
-            pl.when(f == k)(partial(red.step, k - 2, 0, last))
+        for k in range(FFN_LAG, NF):
+            pl.when(f == k)(partial(red.step, k - FFN_LAG, 0, last))
         wu = [flat(wv[slot, t, :, :, :, :, 0:256]) for t in range(2)]
         wd = [flat(wv[slot, t, :, :, :, :, 256:512]) for t in range(2)]
         gslot = lax.rem(f, 3)
@@ -838,8 +916,9 @@
             d = (dact[t] * (cdf + u * dens)).astype(BF)
             dhid.append(d)
             total = jnp.sum(d.astype(F32), axis=0, keepdims=True)
-            bup[f, 2 * t : 2 * t + 1, :] = total[:, 0:128]
-            bup[f, 2 * t + 1 : 2 * t + 2, :] = total[:, 128:256]
+            for j in (0, 1):
+                at = D // 128 + 4 * f + 2 * t + j
+                early[pl.ds(at, 1), :] = total[:, 128 * j : 128 * j + 128]
         acc[...] += nt(act[0], wd[0]) + nt(act[1], wd[1])
         dh2[...] += nt(dhid[0], wu[0]) + nt(dhid[1], wu[1])
         for t in range(2):
@@ -854,12 +933,36 @@
     out_copy = pltpu.make_async_copy(h2, out_hbm, lsem.at[0])
     out_copy.start()
 
+    n = D // 128
+    early[0:n, :] = sums[6:7, :].reshape(n, 128)
+    early[n + 4 * NF :, :] = jnp.zeros((early.shape[0] - n - 4 * NF, 128), F32)
+    early_sum = AllSum(p, early, early_in, esem)
+    early_sum.start(0)
+
     da[...] = nt(won[...], dym[...]).astype(BF)
     dkv[...] = jnp.zeros_like(dkv)
     back = 2
+    dkv_copies = [
+        remote(dkvs.at[m], dkvr.at[m], ysem.at[6 + 2 * m], ysem.at[7 + 2 * m], p.y_peer())
+        for m in range(MB)
+    ]
+
+    def send_dkv(m):
+        dkvs[m] = dkv[m, 0:S, :].astype(BF)
+        dkv_copies[m].start()
+
+    def early_next():
+        early_sum.end(0)
+        early_sum.start(1)
 
     @pl.loop(0, MB * NH // back)
     def _(i):
+        for m in range(1, MB):
+            pl.when(i == m * NH // back)(partial(send_dkv, m - 1))
+        pl.when(i == 2)(early_next)
+        for k in range(NF - FFN_LAG, last + LAST_STEP):
+            at = BACK_FIRST + BACK_EVERY * (k - (NF - FFN_LAG))
+            pl.when(i == at)(partial(red.step, k, 0, last))
         todo = spots(i, back)
         qs = [qt[head, cols] for _, m, head, cols, nk, r in todo]
         das = [da[head, cols] for _, m, head, cols, nk, r in todo]
@@ -892,79 +995,114 @@
             dkv[m, lo:hi, :] += nt(
                 jnp.concatenate(left, axis=1), jnp.concatenate(right, axis=1)
             )
-        for k in range(NF - 2, last + 3):
-            pl.when(i == 2 * (k - (NF - 2)) + 1)(partial(red.step, k, 0, last))
-
-    kv_back = remote(dkv.at[:, 0:S, :], dkvr, ysem.at[4], ysem.at[5], p.y_peer())
-    kv_back.start()
+
+    send_dkv(MB - 1)
+    for k in range(NF - FFN_LAG, last + LAST_STEP):
+        if BACK_FIRST + BACK_EVERY * (k - (NF - FFN_LAG)) >= MB * NH // back:
+            red.step(k, 0, last)
     for b in range(T // 256):
         rows = slice(b * 256, b * 256 + 256)
         tmp[rows, :] = nt(id256, qt[:, rows]).astype(BF)
     for t in range(2):
-        gq = tn(h1[...], tmp[:, t * HT : (t + 1) * HT]).astype(BF)
-        ga[t, :, :, :, :, 0:HT] = gq.reshape(ZC, XC, CC, R, HT)
-    kv_back.wait()
-    for m in range(MB):
-        both = (dkv[m, S : 2 * S, :] + dkvr[m]).T
+        v = tn(h1[...], tmp[:, t * HT : (t + 1) * HT]).astype(BF)
+        gq[t] = v.reshape(ZC, XC, CC, R, HT)
+    red.begin(last)
+
+    def own_dkv(m):
+        dkv_copies[m].wait()
+        both = (dkv[m, S : 2 * S, :] + dkvr[m].astype(F32)).T
         dk = unrotate_t(both[0:HEAD_DIM], cosine, sine) * LN2
         both = jnp.concatenate([dk, both[HEAD_DIM:]], axis=0).astype(BF)
         for b in range(NB):
             rows = slice(m * S + b * 256, m * S + b * 256 + 256)
             dkvn[rows, :] = nt(id256, both[:, b * 256 : b * 256 + 256]).astype(BF)
-    gkv = tn(h1[...], dkvn[...]).astype(BF).reshape(ZC, XC, CC, R, 128)
-    for t in range(2):
-        ga[t, :, :, :, :, HT:] = gkv
-    red.begin(last)
-
-    sums[...] = jnp.zeros_like(sums)
+
     wqf = [flat(wq[t]) for t in range(2)]
     wshf = flat(wsh[...])
-    for b in range(T // 256):
+
+    def input_grad(b):
         rows = slice(b * 256, b * 256 + 256)
         dq, dkvb = tmp[rows, :], dkvn[rows, :]
         dh1 = nt(dq[:, 0:HT], wqf[0]) + nt(dq[:, HT:], wqf[1]) + nt(dkvb, wshf)
         dh2b = dh2[rows, :]
         z, scale = normal_rows(x_ref[rows, :].astype(F32))
         dy = dym[rows, :].astype(F32)
-        e = dh1 * ln_ref[0:1, :] + dh2b * ln_ref[2:3, :]
+        e = dh1 * gain1 + dh2b * gain2
         back_in = scale * (
             e - jnp.mean(e, axis=-1, keepdims=True) - z * jnp.mean(e * z, axis=-1, keepdims=True)
         )
-        h1[rows, :] = (dy + back_in).astype(BF)
-        for k, v in enumerate((dh1 * z, dh1, dh2b * z, dh2b, dy, dq.astype(F32))):
+        tmp[rows, :] = (dy + back_in).astype(BF)
+        for k, v in enumerate((dh1 * z, dh1, dh2b * z, dh2b, dq.astype(F32))):
             sums[k : k + 1, :] += jnp.sum(v, axis=0, keepdims=True)
-        sums[6:7, 0:128] += jnp.sum(dkvb.astype(F32), axis=0, keepdims=True)
-        if b < 2:
-            red.step(b, last, last + 1)
-    gx_copy = pltpu.make_async_copy(h1, gx_hbm, lsem.at[1])
+        sums[5:6, 0:128] += jnp.sum(dkvb.astype(F32), axis=0, keepdims=True)
+
+    own_dkv(0)
+    input_grad(0)
+    red.step1(last)
+    input_grad(1)
+    own_dkv(1)
+    gkvs = tn(h1[...], dkvn[...]).astype(BF).reshape(ZC, XC, CC, R, 128)
+    for t in range(2):
+        gkv[t] = gkvs
+    red.begin(last + 1)
+    input_grad(2)
+    red.step2(last)
+    input_grad(3)
+    red.step1(last + 1)
+    gx_copy = pltpu.make_async_copy(tmp, gx_hbm, lsem.at[1])
     gx_copy.start()
-    n = D // 128
-    for k in range(6):
-        for j in range(n):
-            sm[k * n + j : k * n + j + 1, :] = sums[k : k + 1, j * 128 : j * 128 + 128]
-    sm[6 * n : 6 * n + 4, :] = jnp.zeros((4, 128), F32)
-    sm[6 * n : 6 * n + 1, :] = sums[6:7, 0:128]
-    for f in range(NF):
-        sm[6 * n + 4 + 4 * f : 6 * n + 8 + 4 * f, :] = bup[f]
-
-    for k, peer in enumerate((p.core_peer(), p.y_peer(), p.x_peer())):
-        cp = remote(sm, smr.at[k], ysem.at[6 + 2 * k], ysem.at[7 + 2 * k], peer)
-        cp.start()
-        if k < 2:
-            red.step(k + 2, last, last + 1)
-        cp.wait()
-        sm[...] += smr[k]
-    cps = [
-        remote(sm, smr.at[2 + d], ysem.at[10 + 2 * d], ysem.at[11 + 2 * d], p.z_peer(d))
-        for d in (1, 2, 3)
-    ]
-    for cp in cps:
-        cp.start()
-    for cp in cps:
-        cp.wait()
-    sm[...] += smr[3] + smr[4] + smr[5]
+    for k in range(5):
+        late[k * n : k * n + n, :] = sums[k : k + 1, :].reshape(n, 128)
+    late[5 * n : 5 * n + 1, :] = sums[5:6, 0:128]
+    late[5 * n + 1 :, :] = jnp.zeros((late.shape[0] - 5 * n - 1, 128), F32)
+    late_sum = AllSum(p, late, late_in, asem)
+    late_sum.start(0)
+    early_sum.end(1)
+    red.step3(last)
+    red.step2(last + 1)
+    late_sum.end(0)
+    late_sum.start(1)
+    red.step4(last)
+    red.step3(last + 1)
+    red.step4(last + 1)
+    late_sum.end(1)
     out_copy.wait()
     gx_copy.wait()
+
+
+def finish_kernel(dims, out_in, gx_in, grads, early, late, *refs):
+    (out, gx, g1, b1, g2, b2, gq, bq, gkv, bkv, go, bo, gup, bup, gdn, bd, held, sem) = refs
+    HT, NF = dims["HT"], dims["NF"]
+    there, back = [], []
+    for k, (src, dst) in enumerate(((out_in, out), (gx_in, gx))):
+        there.append(pltpu.make_async_copy(src, held.at[k], sem.at[2 * k]))
+        back.append(pltpu.make_async_copy(held.at[k], dst, sem.at[2 * k + 1]))
+    for cp in there:
+        cp.start()
+    t = lax.axis_index("tensor")
+    n = g1.shape[0] // 128
+    for cp, then in zip(there, back):
+        cp.wait()
+        then.start()
+    for k, ref in enumerate((g1, b1, g2, b2)):
+        ref[...] = late[k * n : k * n + n, :].reshape(n * 128)
+    half = HT // 128
+    bq[...] = late[pl.ds(4 * n + half * t, half), :].reshape(HT)
+    bkv[...] = late[5 * n : 5 * n + 1, :].reshape(128)
+    total = early[0:n, :].reshape(n * 128)
+    bo[...] = total
+    bd[...] = total
+    for f in range(NF):
+        for j in (0, 1):
+            at = 256 * f + 128 * j
+            bup[at : at + 128] = early[pl.ds(n + 4 * f + 2 * t + j, 1), :].reshape(128)
+    at = 0
+    for ref in (gq, gkv, go, gup, gdn):
+        width = ref.shape[1]
+        ref[...] = grads[:, at : at + width]
+        at += width
+    for cp in back:
+        cp.wait()
 
 
 def angle_table(S):
@@ -1010,11 +1148,10 @@
     hbm = pl.BlockSpec(memory_space=pl.ANY)
     smem = pl.BlockSpec(memory_space=pltpu.SMEM)
 
-    ln = jnp.stack([ln1_gain, ln1_bias, ln2_gain, ln2_bias])
-    bpack = jnp.concatenate([b_query, b_up, jnp.zeros((128,), F32)]).reshape(-1, 128)
-    nb = bpack.shape[0]
-    np_ = NF + 2
-    n_small = 6 * (D // 128) + 4 + 4 * NF
+    nb = HT // 128 + 2 * NF + 1
+    np_ = NF + 3
+    n_early, n_late = 8 * ((D // 128 + 4 * NF + 7) // 8), 8 * ((5 * (D // 128) + 8) // 8)
+    n_grads = 2 * HT + 128 + 2 * FT
 
     outs = pl.pallas_call(
         partial(block_kernel, dims),
@@ -1022,18 +1159,13 @@
             s((T, D), BF),
             s((T, D), BF),
             s((NF,) + full + (512,), BF),
-            s((R, HT), F32),
-            s((R, 128), F32),
-            s((R, HT), F32),
-            s((R, FT), F32),
-            s((R, FT), F32),
-            s((n_small, 128), F32),
+            s((R, n_grads), F32),
+            s((n_early, 128), F32),
+            s((n_late, 128), F32),
         ],
-        in_specs=[vm, hbm, smem] + [vm] * 10,
-        out_specs=[hbm] * 3 + [vm] * 6,
+        in_specs=[vm, hbm, smem] + [vm] * 15,
+        out_specs=[hbm] * 3 + [vm] * 3,
         scratch_shapes=[
-            VMEM((R, HT), BF),
-            VMEM((NF, R, 512), BF),
             VMEM(plane + (128,), BF),
             VMEM(full + (HT,), BF),
             VMEM(full + (HT,), BF),
@@ -1051,8 +1183,8 @@
             VMEM((T, D), F32),
             VMEM((T, D), F32),
             VMEM((MB * NH, 1, S), F32),
-            VMEM((128, T), BF),
-            VMEM((128, T), BF),
+            VMEM((MB, 128, S), BF),
+            VMEM((MB, 128, S), BF),
             VMEM((MB, 2 * S, HEAD_DIM), BF),
             VMEM((MB, 2 * S, HEAD_DIM), BF),
             VMEM((MB, HEAD_DIM, 2 * S), BF),
@@ -1060,24 +1192,28 @@
             VMEM((MB, S, 128), F32),
             VMEM((MB, S, S), F32),
             VMEM((MB, 2 * S, 128), F32),
-            VMEM((MB, S, 128), F32),
+            VMEM((MB, S, 128), BF),
+            VMEM((MB, S, 128), BF),
             VMEM((T, 128), BF),
             VMEM((3,) + full + (512,), BF),
             VMEM(full + (HT,), BF),
-            VMEM(full + (HT + 128,), BF),
-            VMEM((NF, 4, 128), F32),
+            VMEM(full + (HT,), BF),
+            VMEM(full + (128,), BF),
             VMEM((8, D), F32),
-            VMEM((6, n_small, 128), F32),
+            VMEM((10, n_early, 128), F32),
+            VMEM((10, n_late, 128), F32),
             VMEM((np_, 2, ZC, XC, R, 512), BF),
             VMEM((np_, ZC, XC, R, 256), BF),
             VMEM((np_, 2, ZC, R, 256), BF),
             VMEM((np_, 2, ZC, R, 256), BF),
             VMEM((np_, 2, 3, R, 256), BF),
-            DMA((np_ + 1, 2, Gather.N_SEMS)),
+            DMA((np_, 2, Gather.N_SEMS)),
             DMA((np_, Reduce.N_SEMS)),
-            DMA((np_ + 2,)),
+            DMA((1 + 2 * np_,)),
             DMA((2,)),
-            DMA((18,)),
+            DMA((6 + 2 * MB,)),
+            DMA((AllSum.N_SEMS,)),
+            DMA((AllSum.N_SEMS,)),
         ],
         compiler_params=pltpu.CompilerParams(
             vmem_limit_bytes=64 * MIB - 65536, collective_id=0, has_side_effects=True
@@ -1088,40 +1224,41 @@
         cotangent.reshape(T, D),
         lengths.reshape(MB),
         jnp.asarray(angle_table(S)),
-        ln,
-        bpack,
-        b_shared.reshape(1, 128),
-        (b_out + b_down).reshape(1, D),
+        ln1_gain,
+        ln1_bias,
+        ln2_gain,
+        ln2_bias,
         w_query,
+        b_query,
         w_shared,
-        w_out,
+        b_shared,
+        w_out.T,
+        b_out,
         w_up,
-        w_down,
+        b_up,
+        w_down.T,
+        b_down,
     )
-    out, gx, _, gq, gkv, go, gup, gdn, sm = outs
-    n = D // 128
-    five = sm[0 : 5 * n].reshape(5, D)
-    bq = lax.dynamic_index_in_dim(sm[5 * n : 6 * n].reshape(2, HT), t, 0, False)
-    bkv = sm[6 * n]
-    bup = lax.dynamic_index_in_dim(sm[6 * n + 4 :].reshape(NF, 2, 256), t, 1, False).reshape(FT)
-    return (
-        out.reshape(block_input.shape),
-        gx.reshape(block_input.shape),
-        five[0],
-        five[1],
-        five[2],
-        five[3],
-        gq,
-        bq,
-        gkv,
-        bkv,
-        go.T,
-        five[4],
-        gup,
-        bup,
-        gdn.T,
-        five[4],
-    )
+    out, gx, _, grads, early, late = outs
+    vec = s((D,), F32)
+    shapes = [s((T, D), BF), s((T, D), BF), vec, vec, vec, vec, s((R, HT), F32), s((HT,), F32)]
+    shapes += [s((R, 128), F32), s((128,), F32), s((R, HT), F32), vec, s((R, FT), F32)]
+    shapes += [s((FT,), F32), s((R, FT), F32), vec]
+    outs = pl.pallas_call(
+        partial(finish_kernel, dims),
+        out_shape=shapes,
+        in_specs=[hbm, hbm, vm, vm, vm],
+        out_specs=[hbm, hbm] + [vm] * 14,
+        scratch_shapes=[VMEM((2, T, D), BF), DMA((4,))],
+        compiler_params=pltpu.CompilerParams(vmem_limit_bytes=16 * MIB),
+        name="finish",
+    )(out, gx, grads, early, late)
+    res = list(outs)
+    res[0] = res[0].reshape(block_input.shape)
+    res[1] = res[1].reshape(block_input.shape)
+    res[10] = res[10].T
+    res[14] = res[14].T
+    return tuple(res)
 
 
 def fits_token_plan(mesh):

time: 217 us -> 173 us (0.80)
  Pallas kernels: 193 us -> 167 us
  local copies, waits for them, and re-layouts: 19 us -> 5.37 us
  other arithmetic: 2.62 us -> 0 us
    pallas_call x1, Pallas kernels: 193 us -> 164 us  [token_plan(): pl.pallas_call(partial(block_kernel, dims), out_shape=[s((T, D), BF), s((...]
    unnamed x24 -> x10, local copies, waits for them, and re-layouts: 11.2 us -> 5.37 us
    pallas_call x0 -> x1, Pallas kernels: none -> 2.81 us  [token_plan(): pl.pallas_call(partial(finish_kernel, dims), out_shape=shapes, in_specs=[...]
    another operation x4 -> x0, local copies, waits for them, and re-layouts: 2.76 us -> none  [token_plan(): ln = jnp.stack([ln1_gain, ln1_bias, ln2_gain, ln2_bias])]
    squeeze x2 -> x0, local copies, waits for them, and re-layouts: 2.57 us -> none  [the longest x1 1.39 us: token_plan(): five[4]]
where the time goes in v3:
time: 173 us
  Pallas kernels  167 us (97%)
  local copies, waits for them, and re-layouts  5.37 us (3%)
    pallas_call x1, Pallas kernels, token_plan(): pl.pallas_call(partial(block_kernel, dims), out_shape=[s((T, D), BF), s((...  164 us
    unnamed x10, local copies, waits for them, and re-layouts  5.37 us

profile of v3, /device:TPU:0, one launch (start us, length us, event | category | flops | bytes accessed | tf_op | source)
XLA Modules:
  0.0 172.8 jit_solution(9232154800099443754)
XLA Ops:
  0.7 163.8 %block.1 = (bf16[1024,768]{1,0:T(8,128)(2,1)}, bf16[1024,768]{1,0:T(8,128)(2,1)}, bf16[6,2,4,2,2,48,512]{6,5,4,3,2,1,0:T(8,128)(2,1)}, f32[48,3968]{1,0:T(8,128)}, f32[32,128]{1,0:T(8,128)}, /*index=5*/f32[32,128]{1,0:T(8,128)}) custom-call(bf16[1024,768]{1,0:T(8,128)(2,1)} %bitcast.13, bf16[1024,768]{1,0:T(8,128)(2,1)} %bitcast.14, s32[2]{0:T(128)} %bitcast.17, ...), custom_call_target="tpu_custom_call" | custom-call | tf_op jit(solution)/shard_map/block/pallas_call | solution.py:1156
  164.5 0.0 copy-start
  164.5 1.4 copy-done
  165.9 0.0 copy-start.1
  165.9 1.4 copy-done.1
  167.3 0.0 copy-start.2
  167.3 1.1 copy-done.2
  168.4 0.0 copy-start.3
  168.4 0.7 copy-done.3
  169.1 0.0 copy-start.4
  169.1 0.7 copy-done.4
  169.8 2.8 %finish.1 = (bf16[1024,768]{1,0:T(8,128)(2,1)}, bf16[1024,768]{1,0:T(8,128)(2,1)}, f32[768]{0:T(1024)}, f32[768]{0:T(1024)}, f32[768]{0:T(1024)}, /*index=5*/f32...) custom-call(bf16[1024,768]{1,0:T(8,128)(2,1)S(1)} %copy-done, ...), custom_call_target="tpu_custom_call" | custom-call | tf_op jit(solution)/shard_map/finish/pallas_call | solution.py:1247
Async XLA Ops:
  164.5 1.4 copy-start
  165.9 1.4 copy-start.1
  167.3 1.1 copy-start.2
  168.4 0.7 copy-start.3
  169.1 0.7 copy-start.4

commit v4 on v3

--- a/solution.py
+++ b/solution.py
@@ -286,7 +286,7 @@
 ZC, XC, CC = 4, 2, 2
 DMA = pltpu.SemaphoreType.DMA
 VMEM = pltpu.VMEM
-MIB = 1 << 20
+VMEM_LIMIT = (64 << 20) - 65536
 
 
 def nn(a, b):
@@ -363,12 +363,12 @@
 
 
 class Gather:
-    N_SEMS = 12
-
-    def __init__(self, place, pieces, sems):
+    SLOTS = 3
+
+    def __init__(self, place, pieces, sends, gots):
         self.p = place
         self.pieces = pieces
-        self.sems = sems
+        self.sends, self.gots = sends, gots
 
     def own(self, c, h):
         p = self.p
@@ -376,79 +376,73 @@
         index = (p.z, p.x, p.core, slice(None), pl.ds(o, w))
         return self.pieces[c][1].at[(p.t,) + index if "y" in order else index]
 
-    def copies(self, c, h, k):
+    def copies(self, c, k):
         p = self.p
-        src, o, w, order = self.pieces[c][0][h]
-        sem = self.sems.at[c, h]
-        if k == 0:
-            dst = self.own(c, h)
-            return [
-                remote(src, dst, sem.at[d - 1], sem.at[2 + d], p.z_peer(d)) for d in (1, 2, 3)
-            ]
-        done = order[:k]
         every = slice(None)
-        index = (every, every if "x" in done else p.x, p.core, every, pl.ds(o, w))
-        if "y" in order:
-            index = (every if "y" in done else p.t,) + index
-        view = self.pieces[c][1].at[index]
-        if k == len(order):
-            peer = p.core_peer()
-        else:
-            peer = p.x_peer() if order[k] == "x" else p.y_peer()
-        return [remote(view, view, sem.at[4 + 2 * k], sem.at[5 + 2 * k], peer)]
-
-    def each(self, c, k):
         res = []
-        for h, (_, _, _, order) in enumerate(self.pieces[c][0]):
-            if k <= len(order):
-                res += self.copies(c, h, k)
+        for h, (src, o, w, order) in enumerate(self.pieces[c][0]):
+            if k == 0:
+                pairs = [(src, self.own(c, h), p.z_peer(d)) for d in (1, 2, 3)]
+            elif k <= len(order):
+                done = order[:k]
+                index = (every, every if "x" in done else p.x, p.core, every, pl.ds(o, w))
+                if "y" in order:
+                    index = (every if "y" in done else p.t,) + index
+                view = self.pieces[c][1].at[index]
+                axis = order[k] if k < len(order) else "core"
+                peers = {"x": p.x_peer(), "y": p.y_peer(), "core": p.core_peer()}
+                pairs = [(view, view, peers[axis])]
+            else:
+                pairs = []
+            for a, b, peer in pairs:
+                res.append(remote(a, b, self.sends.at[c % self.SLOTS, k], self.gots.at[c, k], peer))
         return res
 
-    def start(self, c, k):
-        for cp in self.each(c, k):
-            cp.start()
+    def total(self, c, k):
+        parts, out = self.pieces[c]
+        z = pl.ds(0, 3) if k == 0 else slice(None)
+        x = slice(None) if k > 1 else 0
+        index = (z, x, 0)
+        if "y" in parts[0][3]:
+            index = (slice(None) if k > 2 else 0,) + index
+        view = out.at[index]
+        return remote(
+            view, view, self.sends.at[c % self.SLOTS, k], self.gots.at[c, k], self.p.core_peer()
+        )
 
     def run(self, ops):
         for op in ops:
-            if isinstance(op, int):
-                self.start(op, 0)
-                continue
-            c, k = op
-            for cp in self.each(c, k):
-                cp.wait()
-            self.start(c, k + 1)
+            c, k = (op, -1) if isinstance(op, int) else op
+            if k >= 0:
+                self.total(c, k).wait()
+            for cp in self.copies(c, k + 1):
+                cp.start()
 
 
 class AllSum:
-    N_SEMS = 20
-
     def __init__(self, place, buf, got, sems):
         self.p = place
         self.buf, self.got, self.sems = buf, got, sems
 
-    def copies(self, k):
+    def part(self, k):
+        return (7, 3) if k else (0, 7)
+
+    def start(self, k):
         peers = [self.p.z_peer(d) for d in (1, 2, 3)] if k else self.p.layer_peers()
-        base = 7 if k else 0
-        return [
-            remote(
-                self.buf,
-                self.got.at[base + i],
-                self.sems.at[2 * (base + i)],
-                self.sems.at[2 * (base + i) + 1],
-                peer,
-            )
-            for i, peer in enumerate(peers)
-        ]
-
-    def start(self, k):
-        for cp in self.copies(k):
-            cp.start()
+        at, _ = self.part(k)
+        for i, peer in enumerate(peers):
+            got = self.got.at[at + i]
+            remote(self.buf, got, self.sems.at[2 * k], self.sems.at[2 * k + 1], peer).start()
 
     def end(self, k):
-        for cp in self.copies(k):
-            cp.wait()
+        at, n = self.part(k)
+        view = self.got.at[pl.ds(at, n)]
+        whole = remote(
+            view, view, self.sems.at[2 * k], self.sems.at[2 * k + 1], self.p.core_peer()
+        )
+        whole.wait()
         total = self.buf[...]
-        for i in range(7, 10) if k else range(7):
+        for i in range(at, at + n):
             total = total + self.got[i]
         self.buf[...] = total
 
@@ -491,122 +485,127 @@
 
 
 class Reduce:
-    def __init__(self, place, pieces, rc, r2a, r2b, r3, r4, sems):
+    SLOTS = 3
+
+    def __init__(self, place, pieces, rc, r2a, r2b, r3, r4, sends, gots):
         self.p = place
         self.pieces = pieces
         self.rc, self.r2a, self.r2b, self.r3, self.r4 = rc, r2a, r2b, r3, r4
-        self.sems = sems
-
-    def cols(self, c, h):
-        widths = self.pieces[c][1]
-        return sum(widths[:h]), widths[h]
-
-    def halves(self, c):
-        return range(len(self.pieces[c][1]))
-
-    def cores(self, c):
-        g, w = self.pieces[c][0], sum(self.pieces[c][1])
-        return remote(
-            g.at[:, :, :, 1 - self.p.core],
-            self.rc.at[c, :, :, :, :, pl.ds(0, w)],
-            self.sems.at[c, 0],
-            self.sems.at[c, 1],
-            self.p.core_peer(),
-        )
-
-    def second(self, c, h):
+        self.sends, self.gots = sends, gots
+
+    def part(self, c, h):
+        r, n, o, w = self.pieces[c][1][h]
+        _, first, _, second = self.pieces[c][3]
+        o += first
+        return (slice(r, r + n), slice(o, o + w)), (slice(0, n), slice(second, second + w))
+
+    def wide(self, c):
+        first = self.pieces[c][3][1]
+        return slice(first, first + self.pieces[c][0].shape[-1])
+
+    def sems(self, c, k):
+        return self.sends.at[c % self.SLOTS, k], self.gots.at[c, k]
+
+    def copies(self, c, k):
         p = self.p
-        o, w = self.cols(c, h)
-        if h == 0:
-            src, dst, peer = self.rc.at[c, 1 - p.t, :, :, :, pl.ds(o, w)], self.r2a, p.y_peer()
-        else:
-            src, dst, peer = self.rc.at[c, :, :, 1 - p.x, :, pl.ds(o, w)], self.r2b, p.x_peer()
-        dst = dst.at[c, :, :, :, pl.ds(0, w)]
-        return remote(src, dst, self.sems.at[c, 2 + 2 * h], self.sems.at[c, 3 + 2 * h], peer)
-
-    def third(self, c, h):
+        if k == 0:
+            src = self.pieces[c][0].at[:, :, :, 1 - p.core]
+            dst = self.rc.at[self.pieces[c][3][0], :, :, :, :, self.wide(c)]
+            return [remote(src, dst, *self.sems(c, k), p.core_peer())]
+        res = []
+        a, _, b, _ = self.pieces[c][3]
+        for h in (0, 1):
+            here, there = self.part(c, h)
+            if k == 1 and h == 0:
+                src, dst = self.rc.at[(a, 1 - p.t, slice(None), slice(None)) + here], self.r2a
+                todo = [(src, dst.at[(b, slice(None), slice(None)) + there], p.y_peer())]
+            elif k == 1:
+                src, dst = self.rc.at[(a, slice(None), slice(None), 1 - p.x) + here], self.r2b
+                todo = [(src, dst.at[(b, slice(None), slice(None)) + there], p.x_peer())]
+            elif k == 2:
+                if h == 0:
+                    src, peer = self.r2a.at[(b, slice(None), 1 - p.x) + there], p.x_peer()
+                else:
+                    src, peer = self.r2b.at[(b, 1 - p.t, slice(None)) + there], p.y_peer()
+                todo = [(src, self.r3.at[(b, h, slice(None)) + there], peer)]
+            else:
+                todo = [
+                    (
+                        self.r3.at[(b, h, lax.rem(p.z + d, ZC)) + there],
+                        self.r4.at[(b, h, d - 1) + there],
+                        p.z_peer(d),
+                    )
+                    for d in (1, 2, 3)
+                ]
+            res += [remote(src, dst, *self.sems(c, k), peer) for src, dst, peer in todo]
+        return res
+
+    def total(self, c, k):
+        cols = self.wide(c)
+        every = slice(None)
+        index = {
+            0: (every, every, every, every, cols),
+            1: (0, every, every, every, cols),
+            2: (0, every, 0, every, cols),
+            3: (0, pl.ds(0, 3), 0, every, cols),
+        }[k]
+        view = self.rc.at[(self.pieces[c][3][0],) + index]
+        return remote(view, view, *self.sems(c, k), self.p.core_peer())
+
+    def start(self, c, k):
+        for cp in self.copies(c, k):
+            cp.start()
+
+    def add(self, c, k):
         p = self.p
-        o, w = self.cols(c, h)
-        if h == 0:
-            src, peer = self.r2a.at[c, :, 1 - p.x, :, pl.ds(0, w)], p.x_peer()
-        else:
-            src, peer = self.r2b.at[c, 1 - p.t, :, :, pl.ds(0, w)], p.y_peer()
-        dst = self.r3.at[c, h, :, :, pl.ds(0, w)]
-        return remote(src, dst, self.sems.at[c, 6 + 2 * h], self.sems.at[c, 7 + 2 * h], peer)
-
-    def last(self, c, h, d):
-        p = self.p
-        o, w = self.cols(c, h)
-        src = self.r3.at[c, h, lax.rem(p.z + d, ZC), :, pl.ds(0, w)]
-        dst = self.r4.at[c, h, d - 1, :, pl.ds(0, w)]
-        k = 10 + (h * 3 + d - 1) * 2
-        return remote(src, dst, self.sems.at[c, k], self.sems.at[c, k + 1], p.z_peer(d))
-
-    N_SEMS = 22
-
-    def begin(self, c):
-        self.cores(c).start()
-
-    def step1(self, c):
-        p = self.p
-        g, width = self.pieces[c][0], sum(self.pieces[c][1])
-        self.cores(c).wait()
-        own = g[:, :, :, p.core]
-        mine = self.rc[c, :, :, :, :, 0:width].astype(F32) + own.astype(F32)
-        self.rc[c, :, :, :, :, 0:width] = mine.astype(BF)
-        for h in self.halves(c):
-            self.second(c, h).start()
-
-    def step2(self, c):
-        p = self.p
-        for h in self.halves(c):
-            self.second(c, h).wait()
-            o, w = self.cols(c, h)
-            if h == 0:
-                ref, mine = self.r2a, self.rc[c, p.t, :, :, :, o : o + w]
+        a, _, b, _ = self.pieces[c][3]
+        if k == 1:
+            cols = self.wide(c)
+            mine = self.pieces[c][0][:, :, :, p.core].astype(F32)
+            mine = mine + self.rc[a, :, :, :, :, cols].astype(F32)
+            self.rc[a, :, :, :, :, cols] = mine.astype(BF)
+            return
+        sums = []
+        for h in (0, 1):
+            here, there = self.part(c, h)
+            every = slice(None)
+            if k == 2:
+                if h == 0:
+                    ref, mine = self.r2a, self.rc[(a, p.t, every, every) + here]
+                else:
+                    ref, mine = self.r2b, self.rc[(a, every, every, p.x) + here]
+                at = (b, every, every) + there
+                ref[at] = (mine.astype(F32) + ref[at].astype(F32)).astype(BF)
+            elif k == 3:
+                if h == 0:
+                    mine = self.r2a[(b, every, p.x) + there]
+                else:
+                    mine = self.r2b[(b, p.t, every) + there]
+                at = (b, h, every) + there
+                self.r3[at] = (mine.astype(F32) + self.r3[at].astype(F32)).astype(BF)
             else:
-                ref, mine = self.r2b, self.rc[c, :, :, p.x, :, o : o + w]
-            mine = mine.astype(F32) + ref[c, :, :, :, 0:w].astype(F32)
-            ref[c, :, :, :, 0:w] = mine.astype(BF)
-            self.third(c, h).start()
-
-    def step3(self, c):
-        p = self.p
-        for h in self.halves(c):
-            self.third(c, h).wait()
-            o, w = self.cols(c, h)
-            mine = self.r2a[c, :, p.x, :, 0:w] if h == 0 else self.r2b[c, p.t, :, :, 0:w]
-            mine = mine.astype(F32) + self.r3[c, h, :, :, 0:w].astype(F32)
-            self.r3[c, h, :, :, 0:w] = mine.astype(BF)
-            for d in (1, 2, 3):
-                self.last(c, h, d).start()
-
-    def step4(self, c):
-        p = self.p
-        parts = []
-        for h in self.halves(c):
-            o, w = self.cols(c, h)
-            for d in (1, 2, 3):
-                self.last(c, h, d).wait()
-            total = self.r3[c, h, p.z, :, 0:w].astype(F32)
-            for d in range(3):
-                total = total + self.r4[c, h, d, :, 0:w].astype(F32)
-            parts.append(total)
-        self.pieces[c][2](parts)
-
-    def step(self, i, lo, hi):
-        for late, act in ((4, self.step4), (3, self.step3), (2, self.step2), (0, self.step1)):
-            c = lo + i - late
-            if lo <= c < hi:
-                act(c)
+                total = self.r3[(b, h, p.z) + there].astype(F32)
+                for d in range(3):
+                    total = total + self.r4[(b, h, d) + there].astype(F32)
+                sums.append(total)
+        if k == 4:
+            self.pieces[c][2](sums)
+
+    def run(self, ops):
+        for c, k in ops:
+            if k:
+                self.total(c, k - 1).wait()
+                self.add(c, k)
+            if k < 4:
+                self.start(c, k)
 
 
 HEAD_OPS = (
-    (0, 1, 2),
-    ((0, 0), (1, 0), 3),
-    ((0, 1), (2, 0), 4),
-    ((1, 1), (0, 2), (3, 0), 5),
-    ((1, 2), (2, 1)),
+    (0, 1),
+    ((0, 0), (1, 0), 2),
+    ((0, 1), (1, 1), (2, 0), 3),
+    ((0, 2), (1, 2), (3, 0), 4, 5),
+    ((2, 1),),
     ((1, 3), (4, 0), 6),
 )
 ATTENTION_OPS = {
@@ -621,14 +620,35 @@
     3: ((7, 3), (8, 2)),
     4: ((8, 3),),
 }
-FFN_LAG = 2
-BACK_FIRST, BACK_EVERY = 0, 2
-LAST_STEP = 4
+FFN_SUMS = {
+    2: ((0, 1),),
+    3: ((1, 1),),
+    4: ((0, 2), (2, 1)),
+    5: ((0, 3), (1, 2), (3, 1)),
+}
+BACK_SUMS = {
+    0: ((0, 4), (1, 3), (2, 2), (4, 1)),
+    2: ((1, 4), (2, 3), (3, 2), (5, 1)),
+    4: ((2, 4), (3, 3), (4, 2), (6, 1)),
+    6: ((3, 4), (4, 3), (5, 2)),
+    8: ((4, 4), (5, 3), (6, 2)),
+    9: ((7, 1),),
+    10: ((5, 4), (6, 3)),
+    11: ((7, 2), (8, 1)),
+}
+LAST_SUMS = (
+    ((6, 4), (7, 3), (8, 2)),
+    ((9, 1), (7, 4), (8, 3)),
+    ((9, 2),),
+    ((10, 1), (9, 3)),
+    ((10, 2), (8, 4), (9, 4)),
+    ((10, 3), (10, 4)),
+)
 
 
 def block_kernel(
     dims,
-    x_ref,
+    x_hbm,
     dy_hbm,
     lens_ref,
     tab_ref,
@@ -659,6 +679,7 @@
     wv,
     ball,
     bcol,
+    x_ref,
     dym,
     h1,
     h2,
@@ -693,7 +714,9 @@
     r2b,
     r3,
     r4,
+    gsend,
     gsem,
+    rsend,
     rsem,
     lsem,
     wsem,
@@ -707,29 +730,40 @@
     NB = S // 256
     p = Place()
     bar, npeers = p.greet()
+    x_copy = pltpu.make_async_copy(x_hbm, x_ref, lsem.at[1])
+    x_copy.start()
     dy_copy = pltpu.make_async_copy(dy_hbm, dym, lsem.at[0])
     dy_copy.start()
 
-    def halves(ref):
-        return [
-            (ref.at[:, pl.ds(o, w)], o, w, order)
-            for (o, w), order in zip(split_cols(HT), ("zxy", "zyx"))
-        ]
-
-    pieces = [([(wsh_in, 0, 128, "zx")], wsh), (halves(wq_in), wq), (halves(wout_in), wb)]
+    def parts_of(ref, widths, orders):
+        at = [sum(widths[:i]) for i in range(len(widths))]
+        return [(ref.at[:, pl.ds(o, w)], o, w, order) for o, w, order in zip(at, widths, orders)]
+
+    wide = [w for _, w in split_cols(HT)]
+    pieces = [
+        ([(wsh_in, 0, 128, "zx")], wsh),
+        (parts_of(wq_in, wide, ("zxy", "zyx")), wq),
+        (parts_of(wout_in, wide, ("zxy", "zyx")), wb),
+    ]
     for f in range(NF):
         cols = pl.ds(256 * f, 256)
         parts = [(wup_in.at[:, cols], 0, 256, "zxy"), (wdown_in.at[:, cols], 256, 256, "zyx")]
         pieces.append((parts, wf.at[f]))
-    g = Gather(p, pieces, gsem)
+    g = Gather(p, pieces, gsend, gsem)
     pl.semaphore_wait(bar, npeers)
     g.run(HEAD_OPS[0])
-    locals_ = []
-    for c in range(len(pieces)):
-        for h in range(len(pieces[c][0])):
-            own = pltpu.make_async_copy(pieces[c][0][h][0], g.own(c, h), lsem.at[1 + 2 * c + h])
-            own.start()
-            locals_.append(own)
+    locals_ = [
+        pltpu.make_async_copy(wsh_in, wsh.at[p.z, p.x, p.core], lsem.at[2]),
+        pltpu.make_async_copy(wq_in, wq.at[p.t, p.z, p.x, p.core], lsem.at[3]),
+        pltpu.make_async_copy(wout_in, wb.at[p.t, p.z, p.x, p.core], lsem.at[4]),
+    ]
+    for cp in locals_:
+        cp.start()
+    for c in range(3, len(pieces)):
+        for h in (0, 1):
+            pltpu.make_async_copy(pieces[c][0][h][0], g.own(c, h), lsem.at[5]).start()
+    held = wf.at[:, 0, 0, 0, 0]
+    locals_.append(pltpu.make_async_copy(held, held, lsem.at[5]))
     first = HT // 128
     rows_b = ball.shape[1]
     ball[p.t, 0:first, :] = bq_ref[...].reshape(first, 128)
@@ -749,6 +783,7 @@
         h2[rows, :] = (z * gain2 + shift2).astype(BF)
 
     half = T // 256
+    x_copy.wait()
     pl.loop(0, half)(norm_block)
     for cp in locals_:
         cp.wait()
@@ -814,11 +849,15 @@
 
     both_halves(0)
 
-    def spots(i, group):
+    def spots(i, group, by_thirds=False):
         res = []
         for u in range(group):
             j = i * group + u
             m, h = lax.div(j, NH), lax.rem(j, NH)
+            if by_thirds:
+                k = lax.div(h, 2)
+                h = lax.rem(k, 2) * (NH // 2) + lax.div(k, 2) * 2 + u
+                j = m * NH + h
             head = pl.ds(pl.multiple_of(h * HEAD_DIM, HEAD_DIM), HEAD_DIM)
             for r in range(NB):
                 cols = pl.ds(pl.multiple_of(m * S + r * 256, 256), 256)
@@ -874,15 +913,34 @@
 
         return store
 
-    wide = [w for _, w in split_cols(HT)]
     at_out, at_up, at_down = HT + 128, 2 * HT + 128, 2 * HT + 128 + 256 * NF
-    sums_of = [(gb, wide, put(at_out, at_out + wide[0]))]
+    thirds = HT // 128
+
+    def by_cols(*widths):
+        at = [sum(widths[:i]) for i in range(len(widths))]
+        return [(0, R, o, w) for o, w in zip(at, widths)]
+
+    def put_rows(first):
+        def store(parts):
+            r = 0
+            for v in parts:
+                grads[r : r + v.shape[0], first : first + 128] = v
+                r += v.shape[0]
+
+        return store
+
+    by_rows = [(0, 32, 0, 128), (32, R - 32, 0, 128)]
+    sums_of = [(gb, by_cols(*wide), put(at_out, at_out + wide[0]), (0, 0, 0, 0))]
     for f in range(NF):
-        sums_of.append((gring.at[f % 3], [256, 256], put(at_up + 256 * f, at_down + 256 * f)))
-    sums_of += [(gq, wide, put(0, wide[0])), (gkv, [128], put(HT))]
-    red = Reduce(p, sums_of, rc, r2a, r2b, r3, r4, rsem)
+        store = put(at_up + 256 * f, at_down + 256 * f)
+        sums_of.append((gring.at[f % 3], by_cols(256, 256), store, (1 + f, 0, 1 + f, 0)))
+    for k in range(thirds + 1):
+        store = put_rows(128 * k)
+        slot = (NF + 1, 128 * k, NF + 1 + k // 2, 128 * (k % 2))
+        sums_of.append((gq.at[k] if k < thirds else gkv, by_rows, store, slot))
+    red = Reduce(p, sums_of, rc, r2a, r2b, r3, r4, rsend, rsem)
     last = NF + 1
-    red.begin(0)
+    red.run([(0, 0)])
     dh2[...] = jnp.zeros_like(dh2)
 
     @pl.loop(0, NF)
@@ -896,8 +954,8 @@
                 g.run(FFN_OPS.get(k, ()))
                 load(k + 1, (k + 1) % 2).start()
 
-        for k in range(FFN_LAG, NF):
-            pl.when(f == k)(partial(red.step, k - FFN_LAG, 0, last))
+        for k, ops in FFN_SUMS.items():
+            pl.when(f == k)(partial(red.run, ops))
         wu = [flat(wv[slot, t, :, :, :, :, 0:256]) for t in range(2)]
         wd = [flat(wv[slot, t, :, :, :, :, 256:512]) for t in range(2)]
         gslot = lax.rem(f, 3)
@@ -927,10 +985,10 @@
             gu = tn(h2[...], dhid[t]).astype(BF)
             gring[gslot, t, :, :, :, :, 0:256] = gu.reshape(ZC, XC, CC, R, 256)
         for k in range(NF):
-            pl.when(f == k)(partial(red.begin, 1 + k))
+            pl.when(f == k)(partial(red.run, [(1 + k, 0)]))
 
     h2[...] = acc[...].astype(BF)
-    out_copy = pltpu.make_async_copy(h2, out_hbm, lsem.at[0])
+    out_copy = pltpu.make_async_copy(h2, out_hbm, lsem.at[6])
     out_copy.start()
 
     n = D // 128
@@ -951,6 +1009,16 @@
         dkvs[m] = dkv[m, 0:S, :].astype(BF)
         dkv_copies[m].start()
 
+    def query_third(k):
+        for t in range(2):
+            at = t * HT + 128 * k
+            for b in range(T // 256):
+                rows = slice(b * 256, b * 256 + 256)
+                tmp[rows, at : at + 128] = nt(id256, qt[at : at + 128, rows]).astype(BF)
+            v = tn(h1[...], tmp[:, at : at + 128]).astype(BF)
+            gq[k, t] = v.reshape(ZC, XC, CC, R, 128)
+        red.run([(last + k, 0)])
+
     def early_next():
         early_sum.end(0)
         early_sum.start(1)
@@ -960,10 +1028,12 @@
         for m in range(1, MB):
             pl.when(i == m * NH // back)(partial(send_dkv, m - 1))
         pl.when(i == 2)(early_next)
-        for k in range(NF - FFN_LAG, last + LAST_STEP):
-            at = BACK_FIRST + BACK_EVERY * (k - (NF - FFN_LAG))
-            pl.when(i == at)(partial(red.step, k, 0, last))
-        todo = spots(i, back)
+        for at, ops in BACK_SUMS.items():
+            pl.when(i == at)(partial(red.run, ops))
+        for k in range(thirds - 1):
+            at = MB * NH // back - 2 * (thirds - 1 - k)
+            pl.when(i == at)(partial(query_third, k))
+        todo = spots(i, back, True)
         qs = [qt[head, cols] for _, m, head, cols, nk, r in todo]
         das = [da[head, cols] for _, m, head, cols, nk, r in todo]
         sc = [scores(m, q, nk, r) for (_, m, head, cols, nk, r), q in zip(todo, qs)]
@@ -997,16 +1067,8 @@
             )
 
     send_dkv(MB - 1)
-    for k in range(NF - FFN_LAG, last + LAST_STEP):
-        if BACK_FIRST + BACK_EVERY * (k - (NF - FFN_LAG)) >= MB * NH // back:
-            red.step(k, 0, last)
-    for b in range(T // 256):
-        rows = slice(b * 256, b * 256 + 256)
-        tmp[rows, :] = nt(id256, qt[:, rows]).astype(BF)
-    for t in range(2):
-        v = tn(h1[...], tmp[:, t * HT : (t + 1) * HT]).astype(BF)
-        gq[t] = v.reshape(ZC, XC, CC, R, HT)
-    red.begin(last)
+    query_third(thirds - 1)
+    red.run(LAST_SUMS[0])
 
     def own_dkv(m):
         dkv_copies[m].wait()
@@ -1038,18 +1100,18 @@
 
     own_dkv(0)
     input_grad(0)
-    red.step1(last)
+    red.run(LAST_SUMS[1])
     input_grad(1)
     own_dkv(1)
     gkvs = tn(h1[...], dkvn[...]).astype(BF).reshape(ZC, XC, CC, R, 128)
     for t in range(2):
         gkv[t] = gkvs
-    red.begin(last + 1)
+    red.run([(last + thirds, 0)])
+    red.run(LAST_SUMS[2])
     input_grad(2)
-    red.step2(last)
+    red.run(LAST_SUMS[3])
     input_grad(3)
-    red.step1(last + 1)
-    gx_copy = pltpu.make_async_copy(tmp, gx_hbm, lsem.at[1])
+    gx_copy = pltpu.make_async_copy(tmp, gx_hbm, lsem.at[7])
     gx_copy.start()
     for k in range(5):
         late[k * n : k * n + n, :] = sums[k : k + 1, :].reshape(n, 128)
@@ -1058,13 +1120,10 @@
     late_sum = AllSum(p, late, late_in, asem)
     late_sum.start(0)
     early_sum.end(1)
-    red.step3(last)
-    red.step2(last + 1)
+    red.run(LAST_SUMS[4])
     late_sum.end(0)
     late_sum.start(1)
-    red.step4(last)
-    red.step3(last + 1)
-    red.step4(last + 1)
+    red.run(LAST_SUMS[5])
     late_sum.end(1)
     out_copy.wait()
     gx_copy.wait()
@@ -1149,7 +1208,7 @@
     smem = pl.BlockSpec(memory_space=pltpu.SMEM)
 
     nb = HT // 128 + 2 * NF + 1
-    np_ = NF + 3
+    n_gather, n_reduce = NF + 3, NF + 2 + HT // 128
     n_early, n_late = 8 * ((D // 128 + 4 * NF + 7) // 8), 8 * ((5 * (D // 128) + 8) // 8)
     n_grads = 2 * HT + 128 + 2 * FT
 
@@ -1163,7 +1222,7 @@
             s((n_early, 128), F32),
             s((n_late, 128), F32),
         ],
-        in_specs=[vm, hbm, smem] + [vm] * 15,
+        in_specs=[hbm, hbm, smem] + [vm] * 15,
         out_specs=[hbm] * 3 + [vm] * 3,
         scratch_shapes=[
             VMEM(plane + (128,), BF),
@@ -1173,6 +1232,7 @@
             VMEM((2,) + full + (512,), BF),
             VMEM((2, nb, 128), F32),
             VMEM((2 * HT + 128, 128), F32),
+            VMEM((T, D), BF),
             VMEM((T, D), BF),
             VMEM((T, D), BF),
             VMEM((T, D), BF),
@@ -1197,26 +1257,28 @@
             VMEM((T, 128), BF),
             VMEM((3,) + full + (512,), BF),
             VMEM(full + (HT,), BF),
-            VMEM(full + (HT,), BF),
+            VMEM((HT // 128,) + full + (128,), BF),
             VMEM(full + (128,), BF),
             VMEM((8, D), F32),
             VMEM((10, n_early, 128), F32),
             VMEM((10, n_late, 128), F32),
-            VMEM((np_, 2, ZC, XC, R, 512), BF),
-            VMEM((np_, ZC, XC, R, 256), BF),
-            VMEM((np_, 2, ZC, R, 256), BF),
-            VMEM((np_, 2, ZC, R, 256), BF),
-            VMEM((np_, 2, 3, R, 256), BF),
-            DMA((np_, 2, Gather.N_SEMS)),
-            DMA((np_, Reduce.N_SEMS)),
-            DMA((1 + 2 * np_,)),
+            VMEM((NF + 2, 2, ZC, XC, R, 512), BF),
+            VMEM((NF + 3, ZC, XC, R, 256), BF),
+            VMEM((NF + 3, 2, ZC, R, 256), BF),
+            VMEM((NF + 3, 2, ZC, R, 256), BF),
+            VMEM((NF + 3, 2, 3, R, 256), BF),
+            DMA((Gather.SLOTS, 4)),
+            DMA((n_gather, 4)),
+            DMA((Reduce.SLOTS, 4)),
+            DMA((n_reduce, 4)),
+            DMA((8,)),
             DMA((2,)),
             DMA((6 + 2 * MB,)),
-            DMA((AllSum.N_SEMS,)),
-            DMA((AllSum.N_SEMS,)),
+            DMA((4,)),
+            DMA((4,)),
         ],
         compiler_params=pltpu.CompilerParams(
-            vmem_limit_bytes=64 * MIB - 65536, collective_id=0, has_side_effects=True
+            vmem_limit_bytes=VMEM_LIMIT, collective_id=0, has_side_effects=True
         ),
         name="block",
     )(
@@ -1250,7 +1312,7 @@
         in_specs=[hbm, hbm, vm, vm, vm],
         out_specs=[hbm, hbm] + [vm] * 14,
         scratch_shapes=[VMEM((2, T, D), BF), DMA((4,))],
-        compiler_params=pltpu.CompilerParams(vmem_limit_bytes=16 * MIB),
+        compiler_params=pltpu.CompilerParams(vmem_limit_bytes=VMEM_LIMIT),
         name="finish",
     )(out, gx, grads, early, late)
     res = list(outs)

time: 173 us -> 164 us (0.948)
  local copies, waits for them, and re-layouts: 5.37 us -> 0 us
  Pallas kernels: 167 us -> 163 us
    pallas_call x1, Pallas kernels: 164 us -> 158 us  [token_plan(): pl.pallas_call(partial(block_kernel, dims), out_shape=[s((T, D), BF), s((...]
    unnamed x10 -> x0, local copies, waits for them, and re-layouts: 5.37 us -> none
    pallas_call x1, Pallas kernels: 2.81 us -> 5.16 us  [token_plan(): pl.pallas_call(partial(finish_kernel, dims), out_shape=shapes, in_specs=[...]
where the time goes in v4:
time: 164 us
  Pallas kernels  163 us (99%)
    pallas_call x1, Pallas kernels, token_plan(): pl.pallas_call(partial(block_kernel, dims), out_shape=[s((T, D), BF), s((...  158 us
    pallas_call x1, Pallas kernels, token_plan(): pl.pallas_call(partial(finish_kernel, dims), out_shape=shapes, in_specs=[...  5.16 us

profile of v4, /device:TPU:0, one launch (start us, length us, event | category | flops | bytes accessed | tf_op | source)
XLA Modules:
  0.0 163.6 jit_solution(9474367013833455371)
XLA Ops:
  0.7 157.6 %block.1 = (bf16[1024,768]{1,0:T(8,128)(2,1)}, bf16[1024,768]{1,0:T(8,128)(2,1)}, bf16[6,2,4,2,2,48,512]{6,5,4,3,2,1,0:T(8,128)(2,1)}, f32[48,3968]{1,0:T(8,128)}, f32[32,128]{1,0:T(8,128)}, /*index=5*/f32[32,128]{1,0:T(8,128)}) custom-call(bf16[1024,768]{1,0:T(8,128)(2,1)} %bitcast.13, bf16[1024,768]{1,0:T(8,128)(2,1)} %bitcast.14, s32[2]{0:T(128)} %bitcast.17, ...), custom_call_target="tpu_custom_call" | custom-call | tf_op jit(solution)/shard_map/block/pallas_call | solution.py:1215
  158.3 5.2 %finish.1 = (bf16[1024,768]{1,0:T(8,128)(2,1)}, bf16[1024,768]{1,0:T(8,128)(2,1)}, f32[768]{0:T(1024)}, f32[768]{0:T(1024)}, f32[768]{0:T(1024)}, /*index=5*/f32...) custom-call(bf16[1024,768]{1,0:T(8,128)(2,1)} %get-tuple-element.37., ...), custom_call_target="tpu_custom_call" | custom-call | tf_op jit(solution)/shard_map/finish/pallas_call | solution.py:1309
